TPU v7x, 32 devices: a whole 2x2x4 slice. The times are simulated.
32 devices in a mesh: seq: 8 (over z, x), tp: 4 (over y, core).
Axes of the slice: x: 2, y: 2, z: 4, core: 2. Of those that a mesh axis runs over, the one named last changes fastest.
Arguments:
- tokens: bfloat16 [4096, 3072], P('seq', 'tp')
- norm_gain: float32 [3072], replicated, may hold values from 0.1 to 1.9
- w_query: bfloat16 [3072, 1536], P(None, 'tp'), as said below
- w_key: bfloat16 [3072, 1536], P(None, 'tp'), as said below
- w_value: bfloat16 [3072, 1536], P(None, 'tp'), may hold values from -0.109375 to 0.109375
- w_out: bfloat16 [1536, 3072], P('tp'), may hold values from -0.625 to 0.625
- final_gain: float32 [3072], P('tp'), may hold values from 0.1 to 1.9
- w_vocab: bfloat16 [3072, 32064], P('tp', 'seq'), may hold values from -0.3125 to 0.3125
- segment_ids: int32 [4096], P('seq'), may hold values from -1 to 7, as said below
- prompt_lengths: int32 [8], replicated, may hold values from 1 to 1024, as said below
- request_slots: int32 [128], replicated, may hold values from 0 to 3839, as said below
Outputs:
- kv_cache: bfloat16 [16, 4096, 192], P('tp', 'seq')
- hidden: bfloat16 [4096, 3072], P('seq', 'tp')
- hidden_norm: float32 [128], replicated
- top_logit: float32 [128], replicated
Inputs may be any that keep to these rules, and one draw needn't show every extreme that they name: `segment_ids`: prompts 0 to 7 fill the slots in order from slot 0, prompt p on prompt_lengths[p] consecutive slots; all later slots are -1. `prompt_lengths`: they sum to 3840; the last prompt has exactly 1024 slots, and no prompt has more. `request_slots`: request r names a slot of prompt r // 16; the last request of each prompt names that prompt's final slot. `w_query`: Real-valued weights. `w_key`: Real-valued weights.
All inputs are finite; a program needn't handle non-finite values.
Results may differ from a plain program's by a relative error of at most 0.0095.
Values may be sent and summed in bfloat16 or wider, within the bound.
No kernel may reach another device: no remote copies, remote signals or barrier semaphores. Data moves between devices by JAX's collectives and lax.ppermute only.
A program may use at most 128 MiB of HBM per device.

v0:
```python
from functools import partial

import jax
import jax.numpy as jnp
from jax import lax
from jax.sharding import PartitionSpec as P

D = 3072
HD = 96


NEG = -1e30


def from_behind(array, axis, by):
    devices = lax.axis_size(axis)
    pairs = [(i, i + by) for i in range(devices) if 0 <= i + by < devices]
    return lax.ppermute(array, axis, pairs)


def rotate(field, positions, head_dim):
    middle = head_dim // 2
    inverse = 10000.0 ** (-(jnp.arange(middle, dtype=jnp.float32) * 2.0 / head_dim))
    angles = positions.astype(jnp.float32)[:, None] * inverse[None, :]
    cosine = jnp.cos(angles)[:, None, :]
    sine = jnp.sin(angles)[:, None, :]
    first = field[..., :middle]
    second = field[..., middle:]
    return jnp.concatenate(
        [first * cosine - second * sine, second * cosine + first * sine], axis=-1
    )


def attend(state, block, key_marks, distance, queries, query_marks):
    largest, total, accum = state
    rows = queries.shape[0]
    heads = queries.shape[1]
    head_dim = queries.shape[2]
    paired = block.reshape(block.shape[0], heads, 2 * head_dim)
    keys = paired[..., :head_dim]
    values = paired[..., head_dim:]
    scores = jnp.einsum(
        "qhd,khd->hqk", queries, keys, preferred_element_type=jnp.float32
    ) * head_dim ** (-0.5)
    query_index = jnp.arange(rows, dtype=jnp.int32)[:, None]
    key_index = jnp.arange(block.shape[0], dtype=jnp.int32)[None, :]
    allowed = (
        (query_marks[:, None] == key_marks[None, :])
        & (query_marks[:, None] > 0)
        & (distance * rows + query_index - key_index >= 0)
    )
    masked = jnp.where(allowed[None], scores, NEG)
    newest = jnp.maximum(largest, jnp.max(masked, axis=-1))
    weights = jnp.where(allowed[None], jnp.exp(masked - newest[..., None]), 0.0)
    factor = jnp.exp(largest - newest)
    total = total * factor + jnp.sum(weights, axis=-1)
    accum = accum * factor[..., None] + jnp.einsum(
        "hqk,khd->hqd", weights.astype(jnp.bfloat16), values, preferred_element_type=jnp.float32
    )
    return (newest, total, accum)


def shards(
    tokens,
    norm_gain,
    w_query,
    w_key,
    w_value,
    w_out,
    final_gain,
    w_vocab,
    segment_ids,
    prompt_lengths,
    request_slots,
):
    rows = tokens.shape[0]
    heads = w_query.shape[1] // HD
    seq_index = lax.axis_index("seq")
    whole = lax.all_gather(tokens, "tp", axis=1, tiled=True)
    wide = whole.astype(jnp.float32)
    normed = (
        wide * lax.rsqrt(jnp.mean(wide * wide, axis=-1, keepdims=True) + 1e-05) * norm_gain
    ).astype(jnp.bfloat16)
    starts = jnp.cumsum(prompt_lengths) - prompt_lengths
    matches = segment_ids[:, None] == jnp.arange(prompt_lengths.shape[0], dtype=jnp.int32)[None, :]
    first_slot = jnp.sum(jnp.where(matches, starts[None, :], 0), axis=1)
    slots = seq_index * rows + jnp.arange(rows, dtype=jnp.int32)
    positions = jnp.where(segment_ids >= 0, slots - first_slot, 0)
    query = jnp.dot(normed, w_query, preferred_element_type=jnp.float32).reshape(rows, heads, HD)
    key = jnp.dot(normed, w_key, preferred_element_type=jnp.float32).reshape(rows, heads, HD)
    value = jnp.dot(normed, w_value, preferred_element_type=jnp.float32).reshape(rows, heads, HD)
    rot_query = rotate(query, positions, HD).astype(jnp.bfloat16)
    rot_key = rotate(key, positions, HD).astype(jnp.bfloat16)
    paired = jnp.concatenate([rot_key, value.astype(jnp.bfloat16)], axis=-1)
    kv_cache = jnp.transpose(paired, (1, 0, 2))
    own_block = paired.reshape(rows, heads * 2 * HD)
    marks = jnp.where(segment_ids >= 0, segment_ids + 1, 0)
    span = lax.axis_size("seq") // 4
    attend_here = partial(attend, queries=rot_query, query_marks=marks)

    def visit(state, block, key_marks, distance):
        return attend_here(state, block, key_marks, distance)

    start_state = (
        jnp.full((heads, rows), NEG, jnp.float32),
        jnp.zeros((heads, rows), jnp.float32),
        jnp.zeros((heads, rows, HD), jnp.float32),
    )
    state = attend_here(start_state, own_block, marks, 0)

    def hop(distance, carry):
        current, block, key_marks = carry
        block, key_marks = from_behind((block, key_marks), "seq", 1)
        return (visit(current, block, key_marks, distance), block, key_marks)

    state = lax.fori_loop(1, span + 1, hop, (state, own_block, marks))[0]
    largest, total, accum = state
    attended = (accum / jnp.where(total > 0, total, 1.0)[..., None]).astype(jnp.bfloat16)
    mixed = jnp.transpose(attended, (1, 0, 2)).reshape(rows, heads * HD)
    projected = jnp.dot(mixed, w_out, preferred_element_type=jnp.float32)
    summed = lax.psum_scatter(
        projected.astype(jnp.bfloat16), "tp", scatter_dimension=1, tiled=True
    ).astype(jnp.float32)
    hidden_full = tokens.astype(jnp.float32) + summed
    hidden = hidden_full.astype(jnp.bfloat16)
    picks = (request_slots[:, None] == slots[None, :]).astype(jnp.float32)
    local_rows = jnp.dot(picks, hidden_full, precision=lax.Precision.HIGHEST)
    request_rows = lax.psum(local_rows, "seq")
    squares = jnp.sum(request_rows * request_rows, axis=-1)
    weighted = request_rows * final_gain
    vocab_wide = w_vocab.astype(jnp.float32)
    total_squares = lax.psum(squares, "tp")
    hidden_norm = jnp.sqrt(total_squares / D + 1e-05)
    local_logits = jnp.dot(
        weighted / hidden_norm[:, None], vocab_wide, precision=lax.Precision.HIGHEST
    )
    logits = lax.psum(local_logits.astype(jnp.bfloat16), "tp").astype(jnp.float32)
    top_logit = lax.pmax(jnp.max(logits, axis=-1), "seq")
    return (kv_cache, hidden, hidden_norm, top_logit)


def solution(mesh):
    return jax.shard_map(
        shards,
        mesh=mesh,
        in_specs=(
            P("seq", "tp"),
            P(),
            P(None, "tp"),
            P(None, "tp"),
            P(None, "tp"),
            P("tp", None),
            P("tp"),
            P("tp", "seq"),
            P("seq"),
            P(),
            P(),
        ),
        out_specs=(P("tp", "seq", None), P("seq", "tp"), P(), P()),
        check_vma=False,
    )
```

profile of v0, /device:TPU:0, one launch (start us, length us, event | category | flops | bytes accessed | tf_op | source)
XLA Modules:
  0.0 312.2 jit_solution(10277999835860470456)
XLA Ops:
  12.9 28.0 %all-gather.2.cloned.1.call-done = bf16[512,3072]{1,0:T(8,128)(2,1)} async-done(((bf16[512,768]{1,0:T(8,128)(2,1)}), bf16[512,3072]{1,0:T(8,128)(2,1)}) %all-gather.2.cloned.1.call-update) | async-done | bytes 3145744 | tf_op jit(solution)/shard_map/all_gather | solution.py:79
  40.9 2.6 fusion.16
  43.5 4.3 %fusion.48 = f32[512,384]{0,1:T(8,128)S(1)} fusion(bf16[3072,384]{1,0:T(8,128)(2,1)} %param.15, bf16[512,3072]{1,0:T(8,128)(2,1)} %all-gather.2.cloned.1.call-done, f32[3072]{0:T(1024)S(1)} %copy-done.10, f32[512]{0:T(512)S(1)} %add_rsqrt_fusion), kind=kOutput, calls=%fused_computation.82 | convolution fusion | flops 1214251008 | bytes 6305792 | tf_op jit(solution)/shard_map/dot_general | solution.py:89
  47.9 1.6 fusion.51
  49.8 1.6 convolution_convert_fusion.2
  55.3 2.2 fusion.27
  57.5 53.3 %while.21 = (s32[]{:T(128)}, f32[4,512]{1,0:T(4,128)S(1)}, f32[4,512]{1,0:T(4,128)}, f32[4,512,96]{1,2,0:T(8,128)}, bf16[512,768]{0,1:T(8,128)(2,1)}, /*index=5*...) while((s32[]{:T(128)}, f32[4,512]{1,0:T(4,128)S(1)}, ...), condition=%wide.region_8.9_spmd, body=%wide.region_5.8_spmd.sunk | while | flops 417993728 | bytes 27614516 | solution.py:116
  57.5 3.4 %collective-permute-start.1 = (bf16[512,768]{0,1:T(8,128)(2,1)}, bf16[512,768]{0,1:T(8,128)(2,1)S(1)}, u32[]{:S(2)}, u32[]{:S(2)}) collective-permute-start(bf16[512,768]{0,1:T(8,128)(2,1)} %get-tuple-element.253), channel_id=1, source_target_pairs={{0,4},{4,8},{8,12},{12,16},{16,20},{20,24},{24,28},{1,5},{5,9},{9,... | collective-permute-start | bytes 2359304 | tf_op jit(solution)/shard_map/while/body/eval_jaxpr/ppermute | solution.py:18
  60.9 3.3 %collective-permute-start = (s32[512]{0:T(512)}, s32[512]{0:T(512)S(1)}, u32[]{:S(2)}, u32[]{:S(2)}) collective-permute-start(s32[512]{0:T(512)} %get-tuple-element.254), channel_id=1, source_target_pairs={{0,4},{4,8},{8,12},{12,16},{16,20},{20,24},{24,28},{1,5},{5,9},{9,... | collective-permute-start | bytes 6152 | tf_op jit(solution)/shard_map/while/body/eval_jaxpr/ppermute | solution.py:18
  64.3 14.1 %collective-permute-done = s32[512]{0:T(512)S(1)} collective-permute-done((s32[512]{0:T(512)}, s32[512]{0:T(512)S(1)}, u32[]{:S(2)}, u32[]{:S(2)}) %collective-permute-start) | collective-permute-done | bytes 2080 | tf_op jit(solution)/shard_map/while/body/eval_jaxpr/ppermute | solution.py:18
  84.1 4.3 %collective-permute-start.1 = (bf16[512,768]{0,1:T(8,128)(2,1)}, bf16[512,768]{0,1:T(8,128)(2,1)S(1)}, u32[]{:S(2)}, u32[]{:S(2)}) collective-permute-start(bf16[512,768]{0,1:T(8,128)(2,1)} %get-tuple-element.253), channel_id=1, source_target_pairs={{0,4},{4,8},{8,12},{12,16},{16,20},{20,24},{24,28},{1,5},{5,9},{9,... | collective-permute-start | bytes 2359304 | tf_op jit(solution)/shard_map/while/body/eval_jaxpr/ppermute | solution.py:18
  88.4 4.2 %collective-permute-start = (s32[512]{0:T(512)}, s32[512]{0:T(512)S(1)}, u32[]{:S(2)}, u32[]{:S(2)}) collective-permute-start(s32[512]{0:T(512)} %get-tuple-element.254), channel_id=1, source_target_pairs={{0,4},{4,8},{8,12},{12,16},{16,20},{20,24},{24,28},{1,5},{5,9},{9,... | collective-permute-start | bytes 6152 | tf_op jit(solution)/shard_map/while/body/eval_jaxpr/ppermute | solution.py:18
  92.7 12.4 %collective-permute-done = s32[512]{0:T(512)S(1)} collective-permute-done((s32[512]{0:T(512)}, s32[512]{0:T(512)S(1)}, u32[]{:S(2)}, u32[]{:S(2)}) %collective-permute-start) | collective-permute-done | bytes 2080 | tf_op jit(solution)/shard_map/while/body/eval_jaxpr/ppermute | solution.py:18
  108.1 1.5 fusion.74
  112.7 3.5 %convolution_convert_fusion.1 = bf16[512,3072]{1,0:T(8,128)(2,1)} fusion(bf16[512,384]{0,1:T(8,128)(2,1)S(1)} %bitcast.32, bf16[384,3072]{1,0:T(8,128)(2,1)S(1)} %copy-done), kind=kOutput, calls=%fused_computation.26 | convolution fusion | flops 1209532416 | bytes 5898240 | tf_op jit(solution)/shard_map/dot_general | solution.py:120
  116.3 39.9 %reduce-scatter.2.cloned.1.call-done = bf16[512,768]{1,0:T(8,128)(2,1)} async-done(((bf16[512,3072]{1,0:T(8,128)(2,1)}), bf16[512,768]{1,0:T(8,128)(2,1)}) %reduce-scatter.2.cloned.1.call-update) | async-done | bytes 786448 | tf_op jit(solution)/shard_map/reduce_scatter | solution.py:121
  156.2 2.7 fusion.25
  159.0 72.7 %all-reduce.3.cloned.1.call-done = f32[128,768]{1,0:T(8,128)} async-done(((f32[128,768]{1,0:T(8,128)}), f32[128,768]{1,0:T(8,128)}) %all-reduce.3.cloned.1.call-update) | async-done | bytes 393232 | tf_op jit(solution)/shard_map/psum | solution.py:128
  232.8 5.7 %psum.22 = f32[128]{0:T(128)S(1)} all-reduce(f32[128]{0:T(128)S(1)} %multiply_reduce_fusion), channel_id=1, replica_groups=mesh['seq'=8,'tp'=4] {'tp'}, use_global_device_ids=true, to_apply=%region_12.13 | all-reduce | flops 128 | bytes 1024 | tf_op jit(solution)/shard_map/psum | solution.py:132
  238.5 8.2 %convolution_convert_fusion = bf16[128,4008]{0,1:T(8,128)(2,1)} fusion(bf16[768,4008]{0,1:T(8,128)(2,1)} %param.20, f32[128,768]{1,0:T(8,128)} %all-reduce.3.cloned.1.call-done, f32[128]{0:T(128)S(1)} %add_sqrt_fusion, f32[768]{0:T(1024)S(1)} %copy-done.11), kind=kOutput, calls=%fused_computation.25 | convolution fusion | flops 4728738816 | bytes 7579136 | tf_op jit(solution)/shard_map/dot_general | solution.py:134
  246.7 2.2 fusion.26
  248.9 33.2 %all-reduce.5.cloned.1.call-done = bf16[128,4008]{0,1:T(8,128)(2,1)} async-done(((bf16[128,4008]{0,1:T(8,128)(2,1)}), bf16[128,4008]{0,1:T(8,128)(2,1)}) %all-reduce.5.cloned.1.call-update) | async-done | bytes 1026064 | tf_op jit(solution)/shard_map/psum | solution.py:137
  282.0 1.8 reduce_max.37
  283.8 21.9 %pmax.7 = f32[128]{0:T(128)} all-reduce(bf16[128]{0:T(256)(128)(2,1)S(1)} %reduce_max.37), channel_id=1, replica_groups=mesh['seq'=8,'tp'=4] {'seq'}, use_global_device_ids=true, to_apply=%region_15.16 | all-reduce | flops 128 | bytes 768 | tf_op jit(solution)/shard_map/pmax | solution.py:138
  (87 shorter events, 22.8 us)
Async XLA Ops:
  7.2 105.5 %copy-start = (bf16[384,3072]{1,0:T(8,128)(2,1)S(1)}, bf16[384,3072]{1,0:T(8,128)(2,1)}, u32[]{:S(2)}) copy-start(bf16[384,3072]{1,0:T(8,128)(2,1)} %param.18) | copy-start | bytes 7077892
  7.2 36.3 %copy-start.10 = (f32[3072]{0:T(1024)S(1)}, f32[3072]{0:T(1024)}, u32[]{:S(2)}) copy-start(f32[3072]{0:T(1024)} %param.14) | copy-start | bytes 36868
  7.2 33.7 %all-gather.2.cloned.1.call-start = ((), (), s32[]{:S(2)}) async-start(), calls=%async_computation.1 | async-start | bytes 3932160 | tf_op jit(solution)/shard_map/all_gather | solution.py:79
  7.9 148.3 %reduce-scatter.2.cloned.1.call-start = ((), (), s32[]{:S(2)}) async-start(), calls=%async_computation.2 | async-start | bytes 3932160 | tf_op jit(solution)/shard_map/reduce_scatter | solution.py:121
  43.5 4.4 %copy-start.2 = (bf16[512,3072]{1,0:T(8,128)(2,1)S(1)}, bf16[512,3072]{1,0:T(8,128)(2,1)}, u32[]{:S(2)}) copy-start(bf16[512,3072]{1,0:T(8,128)(2,1)} %all-gather.2.cloned.1.call-done) | copy-start | bytes 9437188
  43.5 4.4 %copy-start.8 = (bf16[3072,384]{1,0:T(8,128)(2,1)S(1)}, bf16[3072,384]{1,0:T(8,128)(2,1)}, u32[]{:S(2)}) copy-start(bf16[3072,384]{1,0:T(8,128)(2,1)} %param.16) | copy-start | bytes 7077892
  47.8 1.9 copy-start.9
  57.5 21.8 %collective-permute-start.1 = (bf16[512,768]{0,1:T(8,128)(2,1)}, bf16[512,768]{0,1:T(8,128)(2,1)S(1)}, u32[]{:S(2)}, u32[]{:S(2)}) collective-permute-start(bf16[512,768]{0,1:T(8,128)(2,1)} %get-tuple-element.253), channel_id=1, source_target_pairs={{0,4},{4,8},{8,12},{12,16},{16,20},{20,24},{24,28},{1,5},{5,9},{9,... | collective-permute-start | bytes 2359304 | tf_op jit(solution)/shard_map/while/body/eval_jaxpr/ppermute | solution.py:18
  60.9 17.5 %collective-permute-start = (s32[512]{0:T(512)}, s32[512]{0:T(512)S(1)}, u32[]{:S(2)}, u32[]{:S(2)}) collective-permute-start(s32[512]{0:T(512)} %get-tuple-element.254), channel_id=1, source_target_pairs={{0,4},{4,8},{8,12},{12,16},{16,20},{20,24},{24,28},{1,5},{5,9},{9,... | collective-permute-start | bytes 6152 | tf_op jit(solution)/shard_map/while/body/eval_jaxpr/ppermute | solution.py:18
  79.3 2.1 copy-start.5
  79.3 2.1 copy-start.3
  81.4 1.5 copy-start.6
  84.1 21.9 %collective-permute-start.1 = (bf16[512,768]{0,1:T(8,128)(2,1)}, bf16[512,768]{0,1:T(8,128)(2,1)S(1)}, u32[]{:S(2)}, u32[]{:S(2)}) collective-permute-start(bf16[512,768]{0,1:T(8,128)(2,1)} %get-tuple-element.253), channel_id=1, source_target_pairs={{0,4},{4,8},{8,12},{12,16},{16,20},{20,24},{24,28},{1,5},{5,9},{9,... | collective-permute-start | bytes 2359304 | tf_op jit(solution)/shard_map/while/body/eval_jaxpr/ppermute | solution.py:18
  88.4 16.7 %collective-permute-start = (s32[512]{0:T(512)}, s32[512]{0:T(512)S(1)}, u32[]{:S(2)}, u32[]{:S(2)}) collective-permute-start(s32[512]{0:T(512)} %get-tuple-element.254), channel_id=1, source_target_pairs={{0,4},{4,8},{8,12},{12,16},{16,20},{20,24},{24,28},{1,5},{5,9},{9,... | collective-permute-start | bytes 6152 | tf_op jit(solution)/shard_map/while/body/eval_jaxpr/ppermute | solution.py:18
  106.0 2.1 copy-start.5
  106.0 2.1 copy-start.3
  108.1 1.5 copy-start.6
  109.6 1.1 copy-start.4
  112.7 43.5 %copy-start.1 = (bf16[512,768]{1,0:T(8,128)(2,1)S(1)}, bf16[512,768]{1,0:T(8,128)(2,1)}, u32[]{:S(2)}) copy-start(bf16[512,768]{1,0:T(8,128)(2,1)} %param.13) | copy-start | bytes 2359300
  112.7 43.5 %copy-start.7 = (s32[128]{0:T(128)S(1)}, s32[128]{0:T(128)}, u32[]{:S(2)}) copy-start(s32[128]{0:T(128)} %param.23) | copy-start | bytes 1540
  116.2 122.2 %copy-start.11 = (f32[768]{0:T(1024)S(1)}, f32[768]{0:T(1024)}, u32[]{:S(2)}) copy-start(f32[768]{0:T(1024)} %param.19) | copy-start | bytes 9220
  116.3 115.4 %all-reduce.3.cloned.1.call-start = ((), (), s32[]{:S(2)}) async-start(), calls=%async_computation.3 | async-start | bytes 786432 | tf_op jit(solution)/shard_map/psum | solution.py:128
  159.0 123.1 %all-reduce.5.cloned.1.call-start = ((), (), s32[]{:S(2)}) async-start(), calls=%async_computation.4 | async-start | bytes 2052096 | tf_op jit(solution)/shard_map/psum | solution.py:137
  238.5 8.2 %copy-start.12 = (f32[128]{0:T(128)}, f32[128]{0:T(128)S(1)}, u32[]{:S(2)}) copy-start(f32[128]{0:T(128)S(1)} %add_sqrt_fusion) | copy-start | bytes 1540
  (1 other events, 1.1 us)
Sparse Core Ops, SparseCore 0:
  9.6 31.2 all-gather.1
  116.4 39.7 reduce-scatter.1
  160.5 71.1 all-reduce.2
  246.8 35.1 all-reduce.4
where the time goes:
time: 313 us; the launch traced here: 312 us
  waiting for transfers between devices  201 us (64%)
  matrix products  30.1 us (10%)
  blocking collectives  27.5 us (9%)
  other arithmetic  19.9 us (6%)
  starting transfers between devices  15.5 us (5%)
  between operations  14 us (4%)
  local copies, waits for them, and re-layouts  4.06 us (1%)
    psum x1, waiting for transfers between devices, shards(): request_rows = lax.psum(local_rows, 'seq')  72.7 us
    reduce_scatter x1, waiting for transfers between devices, shards(): lax.psum_scatter(projected.astype(jnp.bfloat16), 'tp', scatter_dimension=...  39.9 us
    psum x1, waiting for transfers between devices, shards(): lax.psum(local_logits.astype(jnp.bfloat16), 'tp').astype(jnp.float32)  33.2 us
    all_gather x1, waiting for transfers between devices, shards(): whole = lax.all_gather(tokens, 'tp', axis=1, tiled=True)  28 us
    ppermute x4, waiting for transfers between devices, from_behind(): return lax.ppermute(array, axis, pairs)  26.5 us
    pmax x1, blocking collectives, shards(): top_logit = lax.pmax(jnp.max(logits, axis=-1), 'seq')  21.9 us
    ppermute x4, starting transfers between devices, from_behind(): return lax.ppermute(array, axis, pairs)  15.3 us
    dot_general x1, matrix products, shards(): jnp.dot(weighted / hidden_norm[:, None], vocab_wide, precision=lax.Precis...  8.16 us
  transfers between devices with their start and end apart: 8, of which 6 were waited for; matrix products, arithmetic and copies ran while one was open for 3% of the time, Pallas kernels for 0%

commit v1 on v0

v1 whole, which is shorter than its diff:
```python
from functools import partial

import jax
import jax.numpy as jnp
from jax import lax
from jax.experimental import pallas as pl
from jax.experimental.pallas import tpu as pltpu
from jax.sharding import PartitionSpec as P

D = 3072
HD = 96
EPS = 1e-05
NEG = -1e30
FLOOR = -5e29
NEVER = 2**30
LEVEL_ROWS = 16
SHRINK = 2.0**-16
DAMP = 2.0**-24
F32 = jnp.float32
BF16 = jnp.bfloat16
VMEM_LIMIT = 12 * 1024 * 1024

SCALARS = pl.BlockSpec(memory_space=pltpu.SMEM)
ANYWHERE = pl.BlockSpec(memory_space=pl.ANY)
FAR_MEMORY = pl.BlockSpec(memory_space=pltpu.HBM)


WHOLE = pl.BlockSpec(memory_space=pltpu.VMEM)


def call(body, outs, scalars, arrays, after=(), scratch=(), length=0, far=()):
    return pl.pallas_call(
        body,
        out_shape=outs,
        in_specs=[SCALARS] * len(scalars)
        + [FAR_MEMORY] * len(far)
        + [WHOLE] * len(arrays)
        + [ANYWHERE] * len(after),
        out_specs=[WHOLE] * len(outs),
        scratch_shapes=list(scratch),
        compiler_params=pltpu.CompilerParams(vmem_limit_bytes=VMEM_LIMIT),
        cost_estimate=pl.CostEstimate(
            flops=length * 10**9, bytes_accessed=0, transcendentals=0
        ),
    )(*scalars, *far, *arrays, *after)


def struct(shape, dtype):
    return jax.ShapeDtypeStruct(shape, dtype)


def swap(array, axis, bit):
    count = lax.axis_size(axis)
    return lax.ppermute(array, axis, [(i, i ^ bit) for i in range(count)])


def shifted(array, axis, by):
    count = lax.axis_size(axis)
    pairs = [(i, i + by) for i in range(count) if 0 <= i + by < count]
    return lax.ppermute(array, axis, pairs)


def spread(array):
    far = swap(array, "tp", 2)
    near = swap(array, "tp", 1)
    return array, near, far, swap(far, "tp", 1)


def mm(a, b):
    return jnp.dot(a, b, preferred_element_type=F32)


def mm_first(a, b):
    return lax.dot_general(a, b, (((0,), (0,)), ((), ())), preferred_element_type=F32)


def project_body(blocks, first, last, *refs):
    refs = list(refs)
    take = lambda count: [refs.pop(0) for _ in range(count)]
    mine = refs.pop(0)
    base = refs.pop(0) if last else None
    weights = take(3)
    (gain,) = take(1)
    pieces = take(len(blocks))
    accum, squares = take(2) if not first else (None, None)
    cosine, sine, asked = take(3) if last else (None, None, None)
    held, sems = refs[-2:]
    del refs[-2:]
    rows, part = pieces[0].shape
    width = weights[0].shape[1]
    copies = []
    for i in range(3):
        for j, block in enumerate(blocks):
            at = pl.ds(pl.multiple_of((mine[0] ^ block) * part, part), part)
            copies.append(
                pltpu.make_async_copy(weights[i].at[at, :], held.at[i, j], sems.at[i, j])
            )
    for copy in copies:
        copy.start()
    wide = [piece[...].astype(F32) for piece in pieces]
    total = sum(jnp.sum(w * w, axis=1, keepdims=True) for w in wide)
    if not first:
        total = total + squares[...]
    scaled = [
        (w * (gain[pl.ds(mine[0] ^ block, 1), :] * DAMP)).astype(BF16)
        for block, w in zip(blocks, wide)
    ]
    factor = lax.rsqrt(total / D + EPS) * (1.0 / DAMP)
    middle = HD // 2
    for i in range(3):
        at = slice(i * width, (i + 1) * width)
        field = 0.0
        for j, x in enumerate(scaled):
            copies[i * len(blocks) + j].wait()
            field = field + mm(x, held[i, j])
        if not first:
            field = field + accum[:, at]
        if not last:
            refs[-2][:, at] = field
            continue
        field = (field * factor).T
        kv, query, own = refs[-3:]
        for h in range(width // HD):
            at = h * HD
            a = field[at : at + middle]
            b = field[at + middle : at + HD]
            if i == 1:
                kv[2 * at + HD : 2 * at + 2 * HD, :] = field[at : at + HD].astype(BF16)
            else:
                to, out = (2 * at, kv) if i == 0 else (at, query)
                out[to : to + middle, :] = (a * cosine[...] - b * sine[...]).astype(BF16)
                out[to + middle : to + HD, :] = (b * cosine[...] + a * sine[...]).astype(BF16)
    if last:
        row = base[0] + lax.broadcasted_iota(jnp.int32, (rows, asked.shape[1]), 0)
        own[...] = mm(query[...], (asked[...] == row).astype(BF16)).astype(BF16)
    else:
        refs[-1][...] = total


def project(blocks, mine, gain, pieces, weights, before=(), ending=None, after=(), length=0):
    rows = pieces[0].shape[0]
    width = weights[0].shape[1]
    scalars, arrays = [mine], [gain, *pieces, *before]
    if ending is None:
        outs = [struct((rows, 3 * width), F32), struct((rows, 1), F32)]
    else:
        base, cosine, sine, asked = ending
        scalars.append(base)
        arrays += [cosine, sine, asked]
        outs = [
            struct((2 * width, rows), BF16),
            struct((width, rows), BF16),
            struct((width, asked.shape[1]), BF16),
        ]
    body = partial(project_body, blocks, not before, ending is not None)
    scratch = [
        pltpu.VMEM((3, len(blocks), pieces[0].shape[1], width), BF16),
        pltpu.SemaphoreType.DMA((3, len(blocks))),
    ]
    return call(body, outs, scalars, arrays, after, scratch, length, weights)


def copy_body(source, *refs):
    refs[-1][...] = source[...]


def pick_body(base, slots, tokens, out):
    rows = tokens.shape[0]
    count = slots.shape[1]
    row = base[0] + lax.broadcasted_iota(jnp.int32, (rows, count), 0)
    out[...] = mm_first((slots[...] == row).astype(BF16), tokens[...]).astype(BF16)


def request_body(count, low, high, block, *refs):
    out = refs[-1]
    query = sum(part[...] for part in refs[:count])
    width, rows = query.shape
    half = block.shape[1] // 2
    allowed = []
    for i in range(2):
        key_slot = i * half + lax.broadcasted_iota(jnp.int32, (half, rows), 0)
        allowed.append((key_slot >= low[...]) & (key_slot <= high[...]))
    results = []
    levels = []
    for h in range(width // HD):
        at = slice(h * HD, (h + 1) * HD)
        k_at = slice(2 * h * HD, (2 * h + 1) * HD)
        v_at = slice((2 * h + 1) * HD, (2 * h + 2) * HD)
        scores = [
            jnp.where(
                allowed[i], mm_first(block[k_at, i * half : (i + 1) * half], query[at, :]) * HD**-0.5, NEG
            )
            for i in range(2)
        ]
        largest = jnp.maximum(*[jnp.max(part, axis=0, keepdims=True) for part in scores])
        largest = jnp.maximum(largest, FLOOR)
        weights = [jnp.exp(part - largest) for part in scores]
        total = sum(jnp.sum(part, axis=0, keepdims=True) for part in weights)
        mixed = sum(
            mm(block[v_at, i * half : (i + 1) * half], weights[i].astype(BF16)) for i in range(2)
        )
        filled = total > 0
        safe = jnp.where(filled, total, 1.0)
        results.append((mixed * (1.0 / safe)).astype(BF16))
        levels.append(jnp.where(filled, largest + jnp.log(safe), NEG))
    for h, result in enumerate(results):
        out[h * HD : (h + 1) * HD, :] = result
    out[width:, :] = pack_levels(levels)


def pack_levels(levels):
    row = lax.broadcasted_iota(jnp.int32, (LEVEL_ROWS, levels[0].shape[1]), 0)
    packed = jnp.zeros(row.shape, F32)
    for h, level in enumerate(levels):
        for part in range(3):
            rounded = level.astype(BF16).astype(F32)
            packed = jnp.where(row == 3 * h + part, rounded, packed)
            level = level - rounded
    return packed.astype(BF16)


def combine_body(flip, own, other, *refs):
    out = refs[-1]
    width = own.shape[0] - LEVEL_ROWS
    turned = flip[0] > 0
    a = own[...].astype(F32)
    b = other[...].astype(F32)
    lower = jnp.where(turned, b, a)
    upper = jnp.where(turned, a, b)
    levels = []
    results = []
    for h in range(width // HD):
        marks = []
        for side in (lower, upper):
            at = width + 3 * h
            marks.append(side[at : at + 1] + side[at + 1 : at + 2] + side[at + 2 : at + 3])
        top = jnp.maximum(*marks)
        one, two = (jnp.exp(mark - top) for mark in marks)
        both = one + two
        levels.append(top + jnp.log(both))
        at = slice(h * HD, (h + 1) * HD)
        results.append((lower[at] * (one / both) + upper[at] * (two / both)).astype(BF16))
    for h, result in enumerate(results):
        out[h * HD : (h + 1) * HD, :] = result
    out[width:, :] = pack_levels(levels)


def combine(flip, own, other, after=()):
    return call(
        combine_body, [struct(own.shape, BF16)], [flip], [own, other], after
    )[0]


def attend_body(distances, last, low, query, *refs):
    width, rows = query.shape
    half = rows // 2
    heads = width // HD
    blocks = refs[: len(distances)]
    state = refs[len(distances) :]
    accum, largest, total = refs[-3:]
    if distances[0] == 0:
        accum[...] = jnp.zeros(accum.shape, F32)
        largest[...] = jnp.full(largest.shape, FLOOR, F32)
        total[...] = jnp.zeros(total.shape, F32)
    else:
        accum[...] = state[0][...]
        largest[...] = state[1][...]
        total[...] = state[2][...]

    def visit(distance, block, i, j):
        q_at = slice(i * half, (i + 1) * half)
        k_half = slice(j * half, (j + 1) * half)
        offset = j * half - distance * rows
        key_slot = offset + lax.broadcasted_iota(jnp.int32, (half, half), 0)
        allowed = key_slot >= low[:, q_at]
        if distance == 0 and i == j:
            query_slot = i * half + lax.broadcasted_iota(jnp.int32, (half, half), 1)
            allowed = allowed & (key_slot <= query_slot)
        done = []
        for h in range(heads):
            at = slice(h * HD, (h + 1) * HD)
            k_at = slice(2 * h * HD, (2 * h + 1) * HD)
            v_at = slice((2 * h + 1) * HD, (2 * h + 2) * HD)
            scores = mm_first(block[k_at, k_half], query[at, q_at]) * HD**-0.5
            scores = jnp.where(allowed, scores, NEG)
            m_old = largest[h : h + 1, q_at]
            m_new = jnp.maximum(m_old, jnp.max(scores, axis=0, keepdims=True))
            weights = jnp.exp(scores - m_new)
            factor = jnp.exp(m_old - m_new)
            t_new = total[h : h + 1, q_at] * factor + jnp.sum(weights, axis=0, keepdims=True)
            mixed = accum[at, q_at] * factor + mm(block[v_at, k_half], weights.astype(BF16))
            done.append((m_new, t_new, mixed))
        for h, (m_new, t_new, mixed) in enumerate(done):
            accum[h * HD : (h + 1) * HD, q_at] = mixed
            largest[h : h + 1, q_at] = m_new
            total[h : h + 1, q_at] = t_new

    limits = [jnp.min(low[:, i * half : (i + 1) * half]) for i in range(2)]
    for distance, block in zip(distances, blocks):
        for i in range(2):
            for j in range(2):
                if distance == 0 and j > i:
                    continue
                end = (j + 1) * half - distance * rows
                pl.when(limits[i] < end)(partial(visit, distance, block, i, j))
    if last:
        out = refs[-4]
        for h in range(heads):
            at = slice(h * HD, (h + 1) * HD)
            t_h = total[h : h + 1, :]
            accum[at, :] = accum[at, :] * (1.0 / jnp.where(t_h > 0, t_h, 1.0))
        out[...] = accum[...].T.astype(BF16)


def attend(distances, last, low, query, blocks, state=(), length=0):
    width, rows = query.shape
    shapes = [struct((width, rows), F32), struct((8, rows), F32), struct((8, rows), F32)]
    scratch = []
    outs = shapes
    if last:
        scratch = [pltpu.VMEM(s.shape, s.dtype) for s in shapes]
        outs = [struct((rows, width), BF16)]
    return call(
        partial(attend_body, distances, last),
        outs,
        [],
        [low, query, *blocks, *state],
        (),
        scratch,
        length,
    )


def logits_body(limit, tile, start, *refs):
    parts, weights = refs[:4], refs[4:8]
    tokens, gain, vocab = refs[8:11]
    sent, kept, squares, scaled = refs[-4:]
    step = pl.program_id(0)

    @pl.when(step == 0)
    def _():
        summed = sum(
            mm_first(a[...], w[...]).astype(BF16).astype(F32) for a, w in zip(parts, weights)
        )
        rows = tokens[...].astype(F32) + summed
        turned = rows.T
        squares[...] = jnp.sum(turned * turned, axis=0, keepdims=True)
        scaled[...] = (rows * (gain[...] * SHRINK)).T.astype(BF16)

    first = lax.rem(start[0] + step, 4) * tile
    row = first + lax.broadcasted_iota(jnp.int32, sent.shape, 0)
    logits = jnp.where(row < limit, mm(vocab[...], scaled[...]), NEG).astype(BF16)

    @pl.when(step < 2)
    def _():
        sent[...] = logits

    @pl.when(step >= 2)
    def _():
        kept[...] = logits


def request_logits(start, parts, weights, tokens, gain, vocab, after):
    limit, width = vocab.shape
    count = tokens.shape[0]
    tile = pl.cdiv(limit, 4 * 32) * 32
    keep = lambda a: pl.BlockSpec(a.shape, lambda i, start: (0, 0))
    return pl.pallas_call(
        partial(logits_body, limit, tile),
        grid_spec=pltpu.PrefetchScalarGridSpec(
            num_scalar_prefetch=1,
            grid=(4,),
            in_specs=[keep(a) for a in (*parts, *weights, tokens, gain)]
            + [pl.BlockSpec((tile, width), lambda i, start: (lax.rem(start[0] + i, 4), 0))]
            + [ANYWHERE] * len(after),
            out_specs=[
                pl.BlockSpec((tile, count), lambda i, start: (jnp.minimum(i, 1), 0)),
                pl.BlockSpec((tile, count), lambda i, start: (jnp.maximum(i - 2, 0), 0)),
                pl.BlockSpec((1, count), lambda i, start: (0, 0)),
            ],
            scratch_shapes=[pltpu.VMEM((width, count), BF16)],
        ),
        out_shape=[
            struct((2 * tile, count), BF16),
            struct((2 * tile, count), BF16),
            struct((1, count), F32),
        ],
        compiler_params=pltpu.CompilerParams(vmem_limit_bytes=VMEM_LIMIT),
        cost_estimate=pl.CostEstimate(flops=0, bytes_accessed=0, transcendentals=0),
    )(start, *parts, *weights, tokens, gain, vocab, *after)


def fold_body(side, kept, came, send, keep):
    quarter = send.shape[0]
    for out, turn in ((send, 1 - side[0]), (keep, side[0])):
        at = pl.ds(pl.multiple_of(turn * quarter, 16), quarter)
        out[...] = (kept[at, :].astype(F32) + came[at, :].astype(F32)).astype(out.dtype)


def top_body(kept, came, *refs):
    out = refs[-1]
    out[...] = jnp.max(kept[...] + came[...].astype(F32), axis=0, keepdims=True)


def split_body(mine, whole, *refs):
    outs = refs[-4:]
    width = outs[0].shape[1]
    for b in range(4):
        at = pl.ds(pl.multiple_of((mine[0] ^ b) * width, width), width)
        outs[b][...] = whole[:, at]


def shards(
    tokens,
    norm_gain,
    w_query,
    w_key,
    w_value,
    w_out,
    final_gain,
    w_vocab,
    segment_ids,
    prompt_lengths,
    request_slots,
):
    rows, columns = tokens.shape
    half = rows // 2
    width = w_query.shape[1]
    heads = width // HD
    n_seq = lax.axis_size("seq")
    span = n_seq // 4
    seq_index = lax.axis_index("seq")
    tp_index = lax.axis_index("tp")
    mine = tp_index.reshape(1)
    base = seq_index * rows
    requests = request_slots.shape[0]

    far = swap(tokens, "tp", 2)
    pieces = [tokens, swap(tokens, "tp", 1), far]
    gain = norm_gain.reshape(4, columns)
    weights = [
        pltpu.with_memory_space_constraint(w, pltpu.HBM) for w in (w_key, w_value, w_query)
    ]
    sums = project((0, 1), mine, gain, pieces[:2], weights)
    (relayed,) = call(copy_body, [struct(far.shape, BF16)], [], [far], sums[1:])
    pieces.append(swap(relayed, "tp", 1))

    inside = request_slots - base
    asked = request_slots[None, :]
    (own_tokens,) = call(
        pick_body, [struct((requests, columns), BF16)], [base.reshape(1)], [asked, tokens]
    )
    all_tokens = [own_tokens]
    bit = 1
    while bit < n_seq:
        all_tokens.append(all_tokens[-1] + swap(all_tokens[-1], "seq", bit))
        bit *= 2

    starts = jnp.cumsum(prompt_lengths) - prompt_lengths
    prompts = prompt_lengths.shape[0]
    matches = segment_ids[:, None] == jnp.arange(prompts, dtype=jnp.int32)[None, :]
    first_slot = jnp.sum(jnp.where(matches, starts[None, :], 0), axis=1)
    slots = base + jnp.arange(rows, dtype=jnp.int32)
    valid = segment_ids >= 0
    positions = jnp.where(valid, slots - first_slot, 0)
    low = jnp.where(valid, first_slot - base, NEVER)
    request_low = jnp.repeat(starts, requests // prompts) - base

    inverse = 10000.0 ** (-(jnp.arange(HD // 2, dtype=F32) * 2.0 / HD))

    def tables(places):
        angles = inverse[:, None] * places.astype(F32)[None, :]
        return jnp.cos(angles), jnp.sin(angles)

    cosine, sine = tables(positions)
    sums = project(
        (2,), mine, gain, pieces[2:3], weights, sums, None, all_tokens[2:3], length=10
    )
    kv, query, own_query = project(
        (3,),
        mine,
        gain,
        pieces[3:],
        weights,
        sums,
        (base.reshape(1), cosine, sine, asked),
    )
    asking = [own_query] + [shifted(own_query, "seq", -by) for by in range(1, span + 1)]

    kv_cache = jnp.transpose(kv.reshape(heads, 2 * HD, rows), (0, 2, 1))
    behind = shifted(kv, "seq", 1)

    own_state = attend((0,), False, low[None, :], query, (kv,))

    (mixed,) = call(
        partial(request_body, len(asking)),
        [struct((width + LEVEL_ROWS, requests), BF16)],
        [],
        [request_low[None, :], inside[None, :], kv, *asking],
        (all_tokens[-1], own_state[1]),
    )
    w_parts = call(
        split_body,
        [struct((width, columns), BF16)] * 4,
        [mine],
        [w_out],
        (mixed,),
    )
    w_split = w_parts[0]
    w_parts = [w_split] + [swap(w_parts[b], "tp", b) for b in range(1, 4)]

    afters = [[], [w_split], w_parts[1:2]]
    stages = [mixed]
    bit = 1
    while bit < n_seq:
        flip = ((seq_index & bit) > 0).astype(jnp.int32).reshape(1)
        after = afters.pop(0) if afters else ()
        stages.append(combine(flip, stages[-1], swap(stages[-1], "seq", bit), after))
        bit *= 2
    mixed = stages[-1]
    (later_kv,) = call(copy_body, [struct(kv.shape, BF16)], [], [kv], (mixed,))
    request_mixed = spread(mixed[:width])

    core = tp_index & 1
    side = tp_index >> 1
    sent, kept, squares = request_logits(
        (2 * (1 - core)).reshape(1),
        request_mixed,
        w_parts,
        all_tokens[-1],
        final_gain[None, :],
        pltpu.with_memory_space_constraint(w_vocab.T, pltpu.HBM),
        (),
    )
    quarter = kept.shape[0] // 2
    sent, kept = call(
        fold_body,
        [struct((quarter, requests), BF16), struct((quarter, requests), F32)],
        [side.reshape(1)],
        [kept, swap(sent, "tp", 1)],
    )
    blocks = [behind] + [shifted(later_kv, "seq", by) for by in range(2, span + 1)]
    distances = list(range(1, span + 1))
    state = own_state
    while distances:
        last = len(distances) <= 3
        state = attend(distances[:3], last, low[None, :], query, blocks[:3], state, 30)
        distances, blocks = distances[3:], blocks[3:]
    (best,) = call(
        top_body, [struct((1, requests), F32)], [], [kept, swap(sent, "tp", 2)], state[:1]
    )
    bit = 1
    while bit < n_seq:
        best = jnp.maximum(best, swap(best, "seq", bit))
        bit *= 2
    pair = jnp.concatenate([best, squares])
    for bit in (2, 1):
        other = swap(pair, "tp", bit)
        pair = jnp.stack([jnp.maximum(pair[0], other[0]), pair[1] + other[1]])
    hidden_norm = jnp.sqrt(pair[1] / D + EPS)
    top_logit = pair[0] / hidden_norm * (1.0 / SHRINK)

    attended = spread(state[0])
    summed = sum(
        mm(part, w).astype(BF16).astype(F32) for part, w in zip(attended, w_parts)
    )
    hidden = (tokens.astype(F32) + summed).astype(BF16)
    return (kv_cache, hidden, hidden_norm, top_logit)


def solution(mesh):
    return jax.shard_map(
        shards,
        mesh=mesh,
        in_specs=(
            P("seq", "tp"),
            P(),
            P(None, "tp"),
            P(None, "tp"),
            P(None, "tp"),
            P("tp", None),
            P("tp"),
            P("tp", "seq"),
            P("seq"),
            P(),
            P(),
        ),
        out_specs=(P("tp", "seq", None), P("seq", "tp"), P(), P()),
        check_vma=False,
    )
```

time: 313 us -> 136 us (0.43)
  waiting for transfers between devices: 201 us -> 33.1 us
  Pallas kernels: 0 us -> 33.6 us
  starting transfers between devices: 15.5 us -> 46 us
  blocking collectives: 27.5 us -> 0 us
  matrix products: 30.1 us -> 4.35 us
  other arithmetic: 19.9 us -> 5.03 us
  between operations: 14 us -> 0.9 us
  local copies, waits for them, and re-layouts: 4.06 us -> 11.9 us
    psum x2 -> x0, waiting for transfers between devices: 106 us -> none  [the longest x1 72.7 us: shards(): request_rows = lax.psum(local_rows, 'seq')]
    reduce_scatter x1 -> x0, waiting for transfers between devices: 39.9 us -> none  [shards(): lax.psum_scatter(projected.astype(jnp.bfloat16), 'tp', scatter_dimension=...]
    pallas_call x0 -> x16, Pallas kernels: none -> 33.6 us  [the longest x15 27.1 us: call(): pl.pallas_call(body, out_shape=outs, in_specs=[SCALARS] * len(scalars) +...]
    ppermute x4 -> x29, starting transfers between devices: 15.3 us -> 46 us  [the longest x25 36.7 us: swap(): return lax.ppermute(array, axis, [(i, i ^ bit) for i in range(count)])]
    all_gather x1 -> x0, waiting for transfers between devices: 28 us -> none  [shards(): whole = lax.all_gather(tokens, 'tp', axis=1, tiled=True)]
    dot_general x12 -> x4, matrix products: 30.1 us -> 4.35 us  [mm(): return jnp.dot(a, b, preferred_element_type=F32)]
    pmax x1 -> x0, blocking collectives: 21.9 us -> none  [shards(): top_logit = lax.pmax(jnp.max(logits, axis=-1), 'seq')]
    unnamed x19 -> x38, local copies, waits for them, and re-layouts: 0.63 us -> 9.73 us
  transfers between devices with their start and end apart: 8 -> 29, of which waited for: 6 -> 15; matrix products, arithmetic and copies ran while one was open for 3% -> 7% of each run, Pallas kernels for 0% -> 22%
where the time goes in v1:
time: 136 us; the launch traced here: 135 us
  starting transfers between devices  46 us (34%)
  Pallas kernels  33.6 us (25%)
  waiting for transfers between devices  33.1 us (24%)
  local copies, waits for them, and re-layouts  11.9 us (9%)
  other arithmetic  5.03 us (4%)
  matrix products  4.35 us (3%)
    ppermute x25, starting transfers between devices, swap(): return lax.ppermute(array, axis, [(i, i ^ bit) for i in range(count)])  36.7 us
    ppermute x25, waiting for transfers between devices, swap(): return lax.ppermute(array, axis, [(i, i ^ bit) for i in range(count)])  32.9 us
    pallas_call x15, Pallas kernels, call(): pl.pallas_call(body, out_shape=outs, in_specs=[SCALARS] * len(scalars) +...  27.1 us
    unnamed x38, local copies, waits for them, and re-layouts  9.73 us
    ppermute x4, starting transfers between devices, shifted(): return lax.ppermute(array, axis, pairs)  9.34 us
    pallas_call x1, Pallas kernels, request_logits(): pl.pallas_call(partial(logits_body, limit, tile), grid_spec=pltpu.Prefetc...  6.54 us
    dot_general x4, matrix products, mm(): return jnp.dot(a, b, preferred_element_type=F32)  4.35 us
  transfers between devices with their start and end apart: 29, of which 15 were waited for; matrix products, arithmetic and copies ran while one was open for 7% of the time, Pallas kernels for 22%

profile of v1, /device:TPU:0, one launch (start us, length us, event | category | flops | bytes accessed | tf_op | source)
XLA Modules:
  0.0 135.0 jit_solution(3607353766255838585)
XLA Ops:
  1.1 2.6 %collective-permute-start = (bf16[512,768]{1,0:T(8,128)(2,1)}, bf16[512,768]{1,0:T(8,128)(2,1)S(1)}, u32[]{:S(2)}, u32[]{:S(2)}) collective-permute-start(bf16[512,768]{1,0:T(8,128)(2,1)} %tokens.1), channel_id=1, source_target_pairs={{0,2},{1,3},{2,0},{3,1},{4,6},{5,7},{6,4},{7,5},{8,10},{9,11},{10,... | collective-permute-start | bytes 2359304 | tf_op jit(solution)/shard_map/ppermute | solution.py:54
  15.1 4.1 %collective-permute-done.4 = bf16[128,768]{1,0:T(8,128)(2,1)S(1)} collective-permute-done((bf16[128,768]{1,0:T(8,128)(2,1)S(1)}, bf16[128,768]{1,0:T(8,128)(2,1)S(1)}, u32[]{:S(2)}, u32[]{:S(2)}) %collective-permute-start.4) | collective-permute-done | bytes 196640 | tf_op jit(solution)/shard_map/ppermute | solution.py:54
  19.2 2.7 %collective-permute-start.8 = (bf16[128,768]{1,0:T(8,128)(2,1)S(1)}, bf16[128,768]{1,0:T(8,128)(2,1)}, u32[]{:S(2)}, u32[]{:S(2)}) collective-permute-start(bf16[128,768]{1,0:T(8,128)(2,1)S(1)} %add.46.refs_8_), channel_id=1, source_target_pairs={{0,16},{4,20},{8,24},{12,28},{16,0},{20,4},{24,8},{28,12},{1,17},{... | collective-permute-start | bytes 589832 | tf_op jit(solution)/shard_map/ppermute | solution.py:54
  21.9 4.6 %shard_map.138 = (f32[512,1152]{1,0:T(8,128)S(1)}, f32[512,1]{1,0:T(8,128)S(1)}) custom-call(s32[1]{0:T(128)} %bitcast.refs_0_.mine, bf16[3072,384]{1,0:T(8,128)(2,1)} %refs_2_.5, bf16[3072,384]{1,0:T(8,128)(2,1)} %refs_3_.5, bf16[3072,384]{1,0:T(8,128)(2,1)} %refs_4_.1, f32[4,768]{1,0:T(4,128)S(1)} %reshape.100.refs_4_.refs_5_, ...), custom_call_target="tpu_custom_call" | custom-call | tf_op jit(solution)/shard_map/pallas_call | solution.py:32
  26.6 3.0 %shard_map.141 = (f32[512,1152]{1,0:T(8,128)S(1)}, f32[512,1]{1,0:T(8,128)S(1)}) custom-call(s32[1]{0:T(128)} %bitcast.refs_0_.mine, bf16[3072,384]{1,0:T(8,128)(2,1)} %refs_2_.5, bf16[3072,384]{1,0:T(8,128)(2,1)} %refs_3_.5, bf16[3072,384]{1,0:T(8,128)(2,1)} %refs_4_.1, f32[4,768]{1,0:T(4,128)S(1)} %reshape.100.refs_4_.refs_5_, ...), custom_call_target="tpu_custom_call" | custom-call | flops 10000000000 | tf_op jit(solution)/shard_map/pallas_call | solution.py:32
  29.7 3.4 %shard_map.142 = (bf16[768,512]{1,0:T(8,128)(2,1)}, bf16[384,512]{1,0:T(8,128)(2,1)S(1)}, bf16[384,128]{1,0:T(8,128)(2,1)S(1)}) custom-call(s32[1]{0:T(128)} %bitcast.refs_0_.mine, s32[1]{0:T(128)} %bitcast.1.base.refs_1_, bf16[3072,384]{1,0:T(8,128)(2,1)} %refs_2_.5, bf16[3072,384]{1,0:T(8,128)(2,1)} %refs_3_.5, bf16[3072,384]{1,0:T(8,128)(2,1)} %refs_4_.1, ...), custom_call_target="tpu_custom_call" | custom-call | tf_op jit(solution)/shard_map/pallas_call | solution.py:32
  38.1 4.1 %shard_map.143 = (f32[384,512]{1,0:T(8,128)S(1)}, f32[8,512]{1,0:T(8,128)S(1)}, f32[8,512]{1,0:T(8,128)S(1)}) custom-call(s32[1,512]{1,0:T(1,128)S(1)} %bitcast.35, bf16[384,512]{1,0:T(8,128)(2,1)S(1)} %get-tuple-element.28.query, bf16[768,512]{1,0:T(8,128)(2,1)S(1)} %copy-done.2), custom_call_target="tpu_custom_call" | custom-call | tf_op jit(solution)/shard_map/pallas_call | solution.py:32
  43.3 1.8 %shard_map.144.own.refs_0_ = bf16[400,128]{1,0:T(8,128)(2,1)} custom-call(s32[1,128]{1,0:T(1,128)S(1)} %sub.41.low, s32[1,128]{1,0:T(1,128)S(1)} %subtract_bitcast_fusion.high, bf16[768,512]{1,0:T(8,128)(2,1)S(1)} %copy-done.2, bf16[384,128]{1,0:T(8,128)(2,1)S(1)} %get-tuple-element.29.refs_0_, bf16[384,128]{1,0:T(8,128)(2,1)S(1)} %collective-permute-done.6.refs_1_, ...), custom_call_target="tpu_custom_call" | custom-call | tf_op jit(solution)/shard_map/pallas_call | solution.py:32
  48.3 2.4 %collective-permute-start.9 = (bf16[400,128]{1,0:T(8,128)(2,1)}, bf16[400,128]{1,0:T(8,128)(2,1)}, u32[]{:S(2)}, u32[]{:S(2)}) collective-permute-start(bf16[400,128]{1,0:T(8,128)(2,1)} %shard_map.144.own.refs_0_), channel_id=1, source_target_pairs={{0,4},{4,0},{8,12},{12,8},{16,20},{20,16},{24,28},{28,24},{1,5},{5... | collective-permute-start | bytes 307208 | tf_op jit(solution)/shard_map/ppermute | solution.py:54
  50.7 3.8 %collective-permute-done.9.other = bf16[400,128]{1,0:T(8,128)(2,1)} collective-permute-done((bf16[400,128]{1,0:T(8,128)(2,1)}, bf16[400,128]{1,0:T(8,128)(2,1)}, u32[]{:S(2)}, u32[]{:S(2)}) %collective-permute-start.9) | collective-permute-done | bytes 102432 | tf_op jit(solution)/shard_map/ppermute | solution.py:54
  56.2 3.3 %collective-permute-start.10 = (bf16[400,128]{1,0:T(8,128)(2,1)}, bf16[400,128]{1,0:T(8,128)(2,1)}, u32[]{:S(2)}, u32[]{:S(2)}) collective-permute-start(bf16[400,128]{1,0:T(8,128)(2,1)} %shard_map.145.own), channel_id=1, source_target_pairs={{0,8},{4,12},{8,0},{12,4},{16,24},{20,28},{24,16},{28,20},{1,9},{5... | collective-permute-start | bytes 307208 | tf_op jit(solution)/shard_map/ppermute | solution.py:54
  59.5 3.1 %collective-permute-done.10.other = bf16[400,128]{1,0:T(8,128)(2,1)} collective-permute-done((bf16[400,128]{1,0:T(8,128)(2,1)}, bf16[400,128]{1,0:T(8,128)(2,1)}, u32[]{:S(2)}, u32[]{:S(2)}) %collective-permute-start.10) | collective-permute-done | bytes 102432 | tf_op jit(solution)/shard_map/ppermute | solution.py:54
  64.2 3.2 %collective-permute-start.11 = (bf16[400,128]{1,0:T(8,128)(2,1)}, bf16[400,128]{1,0:T(8,128)(2,1)}, u32[]{:S(2)}, u32[]{:S(2)}) collective-permute-start(bf16[400,128]{1,0:T(8,128)(2,1)} %shard_map.147.own), channel_id=1, source_target_pairs={{0,16},{4,20},{8,24},{12,28},{16,0},{20,4},{24,8},{28,12},{1,17},{... | collective-permute-start | bytes 307208 | tf_op jit(solution)/shard_map/ppermute | solution.py:54
  67.4 3.1 %collective-permute-start.5 = (bf16[768,512]{1,0:T(8,128)(2,1)S(1)}, bf16[768,512]{1,0:T(8,128)(2,1)}, u32[]{:S(2)}, u32[]{:S(2)}) collective-permute-start(bf16[768,512]{1,0:T(8,128)(2,1)S(1)} %copy-done.3), channel_id=1, source_target_pairs={{0,4},{4,8},{8,12},{12,16},{16,20},{20,24},{24,28},{1,5},{5,9},{9,... | collective-permute-start | bytes 2359304 | tf_op jit(solution)/shard_map/ppermute | solution.py:60
  73.5 3.7 %collective-permute-start.13 = (bf16[768,512]{1,0:T(8,128)(2,1)}, bf16[768,512]{1,0:T(8,128)(2,1)}, u32[]{:S(2)}, u32[]{:S(2)}) collective-permute-start(bf16[768,512]{1,0:T(8,128)(2,1)} %shard_map.149), channel_id=1, source_target_pairs={{0,8},{4,12},{8,16},{12,20},{16,24},{20,28},{1,9},{5,13},{9,17},{1... | collective-permute-start | bytes 2359304 | tf_op jit(solution)/shard_map/ppermute | solution.py:60
  78.4 4.4 %collective-permute-done.20.refs_2_ = bf16[384,128]{1,0:T(8,128)(2,1)} collective-permute-done((bf16[384,128]{1,0:T(8,128)(2,1)}, bf16[384,128]{1,0:T(8,128)(2,1)}, u32[]{:S(2)}, u32[]{:S(2)}) %collective-permute-start.20) | collective-permute-done | bytes 98336 | tf_op jit(solution)/shard_map/ppermute | solution.py:54
  84.4 6.5 %shard_map.151 = (bf16[2048,128]{1,0:T(8,128)(2,1)}, bf16[2048,128]{1,0:T(8,128)(2,1)S(1)}, f32[1,128]{1,0:T(1,128)S(1)}) custom-call(s32[1]{0:T(128)} %bitcast.12.start, bf16[384,128]{1,0:T(8,128)(2,1)} %slice.20.refs_0_, bf16[384,128]{1,0:T(8,128)(2,1)} %collective-permute-done.19.refs_1_, bf16[384,128]{1,0:T(8,128)(2,1)} %collective-permute-done.20.refs_2_, ...), custom_call_target="tpu_custom_call" | custom-call | tf_op jit(solution)/shard_map/pallas_call | solution.py:368
  92.4 2.2 %collective-permute-done.22.came = bf16[2048,128]{1,0:T(8,128)(2,1)} collective-permute-done((bf16[2048,128]{1,0:T(8,128)(2,1)}, bf16[2048,128]{1,0:T(8,128)(2,1)}, u32[]{:S(2)}, u32[]{:S(2)}) %collective-permute-start.22) | collective-permute-done | bytes 524320 | tf_op jit(solution)/shard_map/ppermute | solution.py:54
  100.9 1.9 %shard_map.150.refs_0_ = bf16[512,384]{1,0:T(8,128)(2,1)S(1)} custom-call(s32[1,512]{1,0:T(1,128)S(1)} %bitcast.36, bf16[384,512]{1,0:T(8,128)(2,1)S(1)} %copy-done.8, bf16[768,512]{1,0:T(8,128)(2,1)} %collective-permute-done.5.refs_0_, bf16[768,512]{1,0:T(8,128)(2,1)} %collective-permute-done.13.refs_1_, f32[384,512]{1,0:T(8,128)S(1)} %copy-done.16, ...), custom_call_target="tpu_custom_call" | custom-call | flops 30000001024 | tf_op jit(solution)/shard_map/pallas_call | solution.py:32
  102.7 2.4 %collective-permute-done.23.came = bf16[1024,128]{1,0:T(8,128)(2,1)S(1)} collective-permute-done((bf16[1024,128]{1,0:T(8,128)(2,1)S(1)}, bf16[1024,128]{1,0:T(8,128)(2,1)S(1)}, u32[]{:S(2)}, u32[]{:S(2)}) %collective-permute-start.23) | collective-permute-done | bytes 262176 | tf_op jit(solution)/shard_map/ppermute | solution.py:54
  105.3 7.4 %collective-permute-start.24 = (f32[1,128]{1,0:T(1,128)S(1)}, f32[1,128]{1,0:T(1,128)S(1)}, u32[]{:S(2)}, u32[]{:S(2)}) collective-permute-start(f32[1,128]{1,0:T(1,128)S(1)} %shard_map.153), channel_id=1, source_target_pairs={{0,4},{4,0},{8,12},{12,8},{16,20},{20,16},{24,28},{28,24},{1,5},{5... | collective-permute-start | bytes 1544 | tf_op jit(solution)/shard_map/ppermute | solution.py:54
  114.2 2.5 %collective-permute-start.25 = (f32[1,128]{1,0:T(1,128)S(1)}, f32[1,128]{1,0:T(1,128)S(1)}, u32[]{:S(2)}, u32[]{:S(2)}) collective-permute-start(f32[1,128]{1,0:T(1,128)S(1)} %max.20), channel_id=1, source_target_pairs={{0,8},{4,12},{8,0},{12,4},{16,24},{20,28},{24,16},{28,20},{1,9},{5... | collective-permute-start | bytes 1544 | tf_op jit(solution)/shard_map/ppermute | solution.py:54
  118.2 3.0 %collective-permute-start.26 = (f32[1,128]{1,0:T(1,128)S(1)}, f32[1,128]{1,0:T(1,128)S(1)}, u32[]{:S(2)}, u32[]{:S(2)}) collective-permute-start(f32[1,128]{1,0:T(1,128)S(1)} %max.21), channel_id=1, source_target_pairs={{0,16},{4,20},{8,24},{12,28},{16,0},{20,4},{24,8},{28,12},{1,17},{... | collective-permute-start | bytes 1544 | tf_op jit(solution)/shard_map/ppermute | solution.py:54
  128.2 3.0 %collective-permute-done.15 = bf16[512,384]{1,0:T(8,128)(2,1)S(1)} collective-permute-done((bf16[512,384]{1,0:T(8,128)(2,1)S(1)}, bf16[512,384]{1,0:T(8,128)(2,1)S(1)}, u32[]{:S(2)}, u32[]{:S(2)}) %collective-permute-start.15) | collective-permute-done | bytes 393248 | tf_op jit(solution)/shard_map/ppermute | solution.py:54
  (115 shorter events, 51.9 us)
Async XLA Ops:
  0.6 21.3 %collective-permute-start.1 = (bf16[512,768]{1,0:T(8,128)(2,1)}, bf16[512,768]{1,0:T(8,128)(2,1)S(1)}, u32[]{:S(2)}, u32[]{:S(2)}) collective-permute-start(bf16[512,768]{1,0:T(8,128)(2,1)} %tokens.1), channel_id=1, source_target_pairs={{0,1},{1,0},{2,3},{3,2},{4,5},{5,4},{6,7},{7,6},{8,9},{9,8},{10,11... | collective-permute-start | bytes 2359304 | tf_op jit(solution)/shard_map/ppermute | solution.py:54
  1.1 25.3 %collective-permute-start = (bf16[512,768]{1,0:T(8,128)(2,1)}, bf16[512,768]{1,0:T(8,128)(2,1)S(1)}, u32[]{:S(2)}, u32[]{:S(2)}) collective-permute-start(bf16[512,768]{1,0:T(8,128)(2,1)} %tokens.1), channel_id=1, source_target_pairs={{0,2},{1,3},{2,0},{3,1},{4,6},{5,7},{6,4},{7,5},{8,10},{9,11},{10,... | collective-permute-start | bytes 2359304 | tf_op jit(solution)/shard_map/ppermute | solution.py:54
  5.9 7.0 %collective-permute-start.3 = (bf16[128,768]{1,0:T(8,128)(2,1)S(1)}, bf16[128,768]{1,0:T(8,128)(2,1)S(1)}, u32[]{:S(2)}, u32[]{:S(2)}) collective-permute-start(bf16[128,768]{1,0:T(8,128)(2,1)S(1)} %shard_map.140), channel_id=1, source_target_pairs={{0,4},{4,0},{8,12},{12,8},{16,20},{20,16},{24,28},{28,24},{1,5},{5... | collective-permute-start | bytes 589832 | tf_op jit(solution)/shard_map/ppermute | solution.py:54
  13.0 6.2 %collective-permute-start.4 = (bf16[128,768]{1,0:T(8,128)(2,1)S(1)}, bf16[128,768]{1,0:T(8,128)(2,1)S(1)}, u32[]{:S(2)}, u32[]{:S(2)}) collective-permute-start(bf16[128,768]{1,0:T(8,128)(2,1)S(1)} %add.45), channel_id=1, source_target_pairs={{0,8},{4,12},{8,0},{12,4},{16,24},{20,28},{24,16},{28,20},{1,9},{5... | collective-permute-start | bytes 589832 | tf_op jit(solution)/shard_map/ppermute | solution.py:54
  19.2 16.7 %collective-permute-start.8 = (bf16[128,768]{1,0:T(8,128)(2,1)S(1)}, bf16[128,768]{1,0:T(8,128)(2,1)}, u32[]{:S(2)}, u32[]{:S(2)}) collective-permute-start(bf16[128,768]{1,0:T(8,128)(2,1)S(1)} %add.46.refs_8_), channel_id=1, source_target_pairs={{0,16},{4,20},{8,24},{12,28},{16,0},{20,4},{24,8},{28,12},{1,17},{... | collective-permute-start | bytes 589832 | tf_op jit(solution)/shard_map/ppermute | solution.py:54
  33.2 9.9 %collective-permute-start.6 = (bf16[384,128]{1,0:T(8,128)(2,1)S(1)}, bf16[384,128]{1,0:T(8,128)(2,1)S(1)}, u32[]{:S(2)}, u32[]{:S(2)}) collective-permute-start(bf16[384,128]{1,0:T(8,128)(2,1)S(1)} %get-tuple-element.29.refs_0_), channel_id=1, source_target_pairs={{4,0},{8,4},{12,8},{16,12},{20,16},{24,20},{28,24},{5,1},{9,5},{13... | collective-permute-start | bytes 294920 | tf_op jit(solution)/shard_map/ppermute | solution.py:60
  34.5 8.8 %collective-permute-start.7 = (bf16[384,128]{1,0:T(8,128)(2,1)S(1)}, bf16[384,128]{1,0:T(8,128)(2,1)S(1)}, u32[]{:S(2)}, u32[]{:S(2)}) collective-permute-start(bf16[384,128]{1,0:T(8,128)(2,1)S(1)} %get-tuple-element.29.refs_0_), channel_id=1, source_target_pairs={{8,0},{12,4},{16,8},{20,12},{24,16},{28,20},{9,1},{13,5},{17,9},{2... | collective-permute-start | bytes 294920 | tf_op jit(solution)/shard_map/ppermute | solution.py:60
  46.4 25.1 %collective-permute-start.12 = (bf16[384,768]{1,0:T(8,128)(2,1)}, bf16[384,768]{1,0:T(8,128)(2,1)S(1)}, u32[]{:S(2)}, u32[]{:S(2)}) collective-permute-start(bf16[384,768]{1,0:T(8,128)(2,1)} %get-tuple-element.32), channel_id=1, source_target_pairs={{0,1},{1,0},{2,3},{3,2},{4,5},{5,4},{6,7},{7,6},{8,9},{9,8},{10,11... | collective-permute-start | bytes 1769480 | tf_op jit(solution)/shard_map/ppermute | solution.py:54
  46.7 31.7 %collective-permute-start.16 = (bf16[384,768]{1,0:T(8,128)(2,1)}, bf16[384,768]{1,0:T(8,128)(2,1)}, u32[]{:S(2)}, u32[]{:S(2)}) collective-permute-start(bf16[384,768]{1,0:T(8,128)(2,1)} %get-tuple-element.35), channel_id=1, source_target_pairs={{0,2},{1,3},{2,0},{3,1},{4,6},{5,7},{6,4},{7,5},{8,10},{9,11},{10,... | collective-permute-start | bytes 1769480 | tf_op jit(solution)/shard_map/ppermute | solution.py:54
  47.2 36.3 %collective-permute-start.18 = (bf16[384,768]{1,0:T(8,128)(2,1)}, bf16[384,768]{1,0:T(8,128)(2,1)S(1)}, u32[]{:S(2)}, u32[]{:S(2)}) collective-permute-start(bf16[384,768]{1,0:T(8,128)(2,1)} %get-tuple-element.36), channel_id=1, source_target_pairs={{0,3},{1,2},{2,1},{3,0},{4,7},{5,6},{6,5},{7,4},{8,11},{9,10},{10,... | collective-permute-start | bytes 1769480 | tf_op jit(solution)/shard_map/ppermute | solution.py:54
  48.3 6.3 %collective-permute-start.9 = (bf16[400,128]{1,0:T(8,128)(2,1)}, bf16[400,128]{1,0:T(8,128)(2,1)}, u32[]{:S(2)}, u32[]{:S(2)}) collective-permute-start(bf16[400,128]{1,0:T(8,128)(2,1)} %shard_map.144.own.refs_0_), channel_id=1, source_target_pairs={{0,4},{4,0},{8,12},{12,8},{16,20},{20,16},{24,28},{28,24},{1,5},{5... | collective-permute-start | bytes 307208 | tf_op jit(solution)/shard_map/ppermute | solution.py:54
  56.2 6.3 %collective-permute-start.10 = (bf16[400,128]{1,0:T(8,128)(2,1)}, bf16[400,128]{1,0:T(8,128)(2,1)}, u32[]{:S(2)}, u32[]{:S(2)}) collective-permute-start(bf16[400,128]{1,0:T(8,128)(2,1)} %shard_map.145.own), channel_id=1, source_target_pairs={{0,8},{4,12},{8,0},{12,4},{16,24},{20,28},{24,16},{28,20},{1,9},{5... | collective-permute-start | bytes 307208 | tf_op jit(solution)/shard_map/ppermute | solution.py:54
  64.2 7.3 %collective-permute-start.11 = (bf16[400,128]{1,0:T(8,128)(2,1)}, bf16[400,128]{1,0:T(8,128)(2,1)}, u32[]{:S(2)}, u32[]{:S(2)}) collective-permute-start(bf16[400,128]{1,0:T(8,128)(2,1)} %shard_map.147.own), channel_id=1, source_target_pairs={{0,16},{4,20},{8,24},{12,28},{16,0},{20,4},{24,8},{28,12},{1,17},{... | collective-permute-start | bytes 307208 | tf_op jit(solution)/shard_map/ppermute | solution.py:54
  67.4 29.9 %collective-permute-start.5 = (bf16[768,512]{1,0:T(8,128)(2,1)S(1)}, bf16[768,512]{1,0:T(8,128)(2,1)}, u32[]{:S(2)}, u32[]{:S(2)}) collective-permute-start(bf16[768,512]{1,0:T(8,128)(2,1)S(1)} %copy-done.3), channel_id=1, source_target_pairs={{0,4},{4,8},{8,12},{12,16},{16,20},{20,24},{24,28},{1,5},{5,9},{9,... | collective-permute-start | bytes 2359304 | tf_op jit(solution)/shard_map/ppermute | solution.py:60
  73.5 23.8 %collective-permute-start.13 = (bf16[768,512]{1,0:T(8,128)(2,1)}, bf16[768,512]{1,0:T(8,128)(2,1)}, u32[]{:S(2)}, u32[]{:S(2)}) collective-permute-start(bf16[768,512]{1,0:T(8,128)(2,1)} %shard_map.149), channel_id=1, source_target_pairs={{0,8},{4,12},{8,16},{12,20},{16,24},{20,28},{1,9},{5,13},{9,17},{1... | collective-permute-start | bytes 2359304 | tf_op jit(solution)/shard_map/ppermute | solution.py:60
  77.8 4.9 %collective-permute-start.20 = (bf16[384,128]{1,0:T(8,128)(2,1)}, bf16[384,128]{1,0:T(8,128)(2,1)}, u32[]{:S(2)}, u32[]{:S(2)}) collective-permute-start(bf16[384,128]{1,0:T(8,128)(2,1)} %slice.20.refs_0_), channel_id=1, source_target_pairs={{0,2},{1,3},{2,0},{3,1},{4,6},{5,7},{6,4},{7,5},{8,10},{9,11},{10,... | collective-permute-start | bytes 294920 | tf_op jit(solution)/shard_map/ppermute | solution.py:54
  78.4 5.1 %collective-permute-start.19 = (bf16[384,128]{1,0:T(8,128)(2,1)}, bf16[384,128]{1,0:T(8,128)(2,1)}, u32[]{:S(2)}, u32[]{:S(2)}) collective-permute-start(bf16[384,128]{1,0:T(8,128)(2,1)} %slice.20.refs_0_), channel_id=1, source_target_pairs={{0,1},{1,0},{2,3},{3,2},{4,5},{5,4},{6,7},{7,6},{8,9},{9,8},{10,11... | collective-permute-start | bytes 294920 | tf_op jit(solution)/shard_map/ppermute | solution.py:54
  96.7 8.4 %collective-permute-start.23 = (bf16[1024,128]{1,0:T(8,128)(2,1)S(1)}, bf16[1024,128]{1,0:T(8,128)(2,1)S(1)}, u32[]{:S(2)}, u32[]{:S(2)}) collective-permute-start(bf16[1024,128]{1,0:T(8,128)(2,1)S(1)} %get-tuple-element.41), channel_id=1, source_target_pairs={{0,2},{1,3},{2,0},{3,1},{4,6},{5,7},{6,4},{7,5},{8,10},{9,11},{10,... | collective-permute-start | bytes 786440 | tf_op jit(solution)/shard_map/ppermute | solution.py:54
  105.3 8.9 %collective-permute-start.24 = (f32[1,128]{1,0:T(1,128)S(1)}, f32[1,128]{1,0:T(1,128)S(1)}, u32[]{:S(2)}, u32[]{:S(2)}) collective-permute-start(f32[1,128]{1,0:T(1,128)S(1)} %shard_map.153), channel_id=1, source_target_pairs={{0,4},{4,0},{8,12},{12,8},{16,20},{20,16},{24,28},{28,24},{1,5},{5... | collective-permute-start | bytes 1544 | tf_op jit(solution)/shard_map/ppermute | solution.py:54
  114.2 4.0 %collective-permute-start.25 = (f32[1,128]{1,0:T(1,128)S(1)}, f32[1,128]{1,0:T(1,128)S(1)}, u32[]{:S(2)}, u32[]{:S(2)}) collective-permute-start(f32[1,128]{1,0:T(1,128)S(1)} %max.20), channel_id=1, source_target_pairs={{0,8},{4,12},{8,0},{12,4},{16,24},{20,28},{24,16},{28,20},{1,9},{5... | collective-permute-start | bytes 1544 | tf_op jit(solution)/shard_map/ppermute | solution.py:54
  118.2 4.6 %collective-permute-start.26 = (f32[1,128]{1,0:T(1,128)S(1)}, f32[1,128]{1,0:T(1,128)S(1)}, u32[]{:S(2)}, u32[]{:S(2)}) collective-permute-start(f32[1,128]{1,0:T(1,128)S(1)} %max.21), channel_id=1, source_target_pairs={{0,16},{4,20},{8,24},{12,28},{16,0},{20,4},{24,8},{28,12},{1,17},{... | collective-permute-start | bytes 1544 | tf_op jit(solution)/shard_map/ppermute | solution.py:54
  122.8 3.6 %collective-permute-start.27 = (f32[2,128]{1,0:T(2,128)S(1)}, f32[2,128]{1,0:T(2,128)S(1)}, u32[]{:S(2)}, u32[]{:S(2)}) collective-permute-start(f32[2,128]{1,0:T(2,128)S(1)} %pad_maximum_fusion), channel_id=1, source_target_pairs={{0,2},{1,3},{2,0},{3,1},{4,6},{5,7},{6,4},{7,5},{8,10},{9,11},{10,... | collective-permute-start | bytes 3080 | tf_op jit(solution)/shard_map/ppermute | solution.py:54
  123.4 7.8 %collective-permute-start.15 = (bf16[512,384]{1,0:T(8,128)(2,1)S(1)}, bf16[512,384]{1,0:T(8,128)(2,1)S(1)}, u32[]{:S(2)}, u32[]{:S(2)}) collective-permute-start(bf16[512,384]{1,0:T(8,128)(2,1)S(1)} %shard_map.150.refs_0_), channel_id=1, source_target_pairs={{0,2},{1,3},{2,0},{3,1},{4,6},{5,7},{6,4},{7,5},{8,10},{9,11},{10,... | collective-permute-start | bytes 1179656 | tf_op jit(solution)/shard_map/ppermute | solution.py:54
  127.1 5.7 %collective-permute-start.14 = (bf16[512,384]{1,0:T(8,128)(2,1)S(1)}, bf16[512,384]{1,0:T(8,128)(2,1)S(1)}, u32[]{:S(2)}, u32[]{:S(2)}) collective-permute-start(bf16[512,384]{1,0:T(8,128)(2,1)S(1)} %shard_map.150.refs_0_), channel_id=1, source_target_pairs={{0,1},{1,0},{2,3},{3,2},{4,5},{5,4},{6,7},{7,6},{8,9},{9,8},{10,11... | collective-permute-start | bytes 1179656 | tf_op jit(solution)/shard_map/ppermute | solution.py:54
  (24 other events, 130.2 us)

commit v2 on v1

v2 whole, which is shorter than its diff:
```python
from functools import partial

import jax
import jax.numpy as jnp
import numpy as np
from jax import lax
from jax.experimental import pallas as pl
from jax.experimental.pallas import tpu as pltpu
from jax.sharding import PartitionSpec as P

D = 3072
HD = 96
EPS = 1e-05
NEG = -1e30
FLOOR = -5e29
NEVER = 2**30
LEVEL_ROWS = 16
SHRINK = 2.0**-16
DAMP = 2.0**-24
LOG2_E = 1.4426950408889634
F32 = jnp.float32
BF16 = jnp.bfloat16
VMEM_LIMIT = 12 * 1024 * 1024

SCALARS = pl.BlockSpec(memory_space=pltpu.SMEM)
ANYWHERE = pl.BlockSpec(memory_space=pl.ANY)
FAR_MEMORY = pl.BlockSpec(memory_space=pltpu.HBM)


WHOLE = pl.BlockSpec(memory_space=pltpu.VMEM)


def whole(array):
    return pl.BlockSpec(array.shape, lambda i: (0, 0), pipeline_mode=pl.Buffered(1))


def call(body, outs, scalars, arrays, after=(), scratch=(), length=0, far=(), blocked=False):
    return pl.pallas_call(
        body,
        grid=(1,) if blocked else (),
        out_shape=outs,
        in_specs=[SCALARS] * len(scalars)
        + [FAR_MEMORY] * len(far)
        + [whole(array) if blocked else WHOLE for array in arrays]
        + [ANYWHERE] * len(after),
        out_specs=[whole(out) if blocked else WHOLE for out in outs],
        scratch_shapes=list(scratch),
        compiler_params=pltpu.CompilerParams(vmem_limit_bytes=VMEM_LIMIT),
        cost_estimate=pl.CostEstimate(
            flops=length * 10**9, bytes_accessed=0, transcendentals=0
        ),
    )(*scalars, *far, *arrays, *after)


def pinned(arrays):
    return [pltpu.with_memory_space_constraint(a, pltpu.HBM) for a in arrays]


def struct(shape, dtype):
    return jax.ShapeDtypeStruct(shape, dtype)


def swap(array, axis, bit):
    count = lax.axis_size(axis)
    return lax.ppermute(array, axis, [(i, i ^ bit) for i in range(count)])


def shifted(array, axis, by):
    count = lax.axis_size(axis)
    pairs = [(i, i + by) for i in range(count) if 0 <= i + by < count]
    return lax.ppermute(array, axis, pairs)


def spread(array):
    far = swap(array, "tp", 2)
    near = swap(array, "tp", 1)
    return array, near, far, swap(far, "tp", 1)


def mm(a, b):
    return jnp.dot(a, b, preferred_element_type=F32)


def mm_last(a, b):
    return lax.dot_general(a, b, (((1,), (1,)), ((), ())), preferred_element_type=F32)


def mm_first(a, b):
    return lax.dot_general(a, b, (((0,), (0,)), ((), ())), preferred_element_type=F32)


AHEAD = ((2, (0, 1, 2)), (3, (0, 1)), (3, (2,)))


def project_body(blocks, first, last, kinds, *refs):
    refs = list(refs)
    take = lambda count: [refs.pop(0) for _ in range(count)]
    mine = refs.pop(0)
    base = refs.pop(0) if last else None
    weights = take(3 if first else 1)
    (gain,) = take(1)
    pieces = take(len(blocks))
    accum, squares = take(2) if not first else (None, None)
    cosine, sine, asked = take(3) if last else (None, None, None)
    if first:
        held, sems = refs[-2:]
        del refs[-2:]
    rows, part = pieces[0].shape
    width = weights[0].shape[-1]
    copies = []
    onward = []
    if first:
        split_columns(mine, refs.pop(0), refs[-7:-3])
        for (block, needed), out in zip(AHEAD, refs[-3:]):
            at = pl.ds(pl.multiple_of((mine[0] ^ block) * part, part), part)
            onward += [
                pltpu.make_async_copy(weights[i].at[at, :], out.at[j], sems.at[i, block])
                for j, i in enumerate(needed)
            ]
        del refs[-7:]
    for i in range(3 if first else 0):
        for j, block in enumerate(blocks):
            at = pl.ds(pl.multiple_of((mine[0] ^ block) * part, part), part)
            copies.append(
                pltpu.make_async_copy(weights[i].at[at, :], held.at[i, j], sems.at[i, j])
            )
    for copy in copies + onward:
        copy.start()
    wide = [piece[...].astype(F32) for piece in pieces]
    total = sum(jnp.sum(w * w, axis=1, keepdims=True) for w in wide)
    if not first:
        total = total + squares[...]
    scaled = [
        (w * (gain[pl.ds(mine[0] ^ block, 1), :] * DAMP)).astype(BF16)
        for block, w in zip(blocks, wide)
    ]
    factor = lax.rsqrt(total / D + EPS) * (1.0 / DAMP)
    middle = HD // 2
    for i in kinds:
        place = kinds.index(i)
        at = slice(place * width, (place + 1) * width)
        field = 0.0
        for j, x in enumerate(scaled):
            if first:
                copies[i * len(blocks) + j].wait()
                field = field + mm(x, held[i, j])
            else:
                field = field + mm(x, weights[0][place])
        if not first:
            field = field + accum[:, at]
        if first:
            refs[-2][:, at] = field
            continue
        if not last:
            out = refs[-4] if i < 2 else refs[-2]
            out[:, at if i < 2 else slice(0, width)] = field
            continue
        field = (field * factor).T
        if 2 in kinds:
            query, own = refs[-2:]
        else:
            kv = refs[-1]
        for h in range(width // HD):
            at = h * HD
            a = field[at : at + middle]
            b = field[at + middle : at + HD]
            if i == 1:
                kv[2 * at + HD : 2 * at + 2 * HD, :] = field[at : at + HD].astype(BF16)
            else:
                to, out = (at, query) if i == 2 else (2 * at, kv)
                out[to : to + middle, :] = (a * cosine[...] - b * sine[...]).astype(BF16)
                out[to + middle : to + HD, :] = (b * cosine[...] + a * sine[...]).astype(BF16)
    if last and 2 in kinds:
        row = base[0] + lax.broadcasted_iota(jnp.int32, (rows, asked.shape[1]), 0)
        own[...] = mm(query[...], (asked[...] == row).astype(BF16)).astype(BF16)
    if not last:
        refs[-1][...] = total
        if not first:
            refs[-3][...] = total
    for copy in onward:
        copy.wait()


def project(
    blocks,
    mine,
    gain,
    pieces,
    weights,
    before=(),
    ending=None,
    after=(),
    length=0,
    kinds=(0, 1, 2),
    w_out=None,
):
    rows = pieces[0].shape[0]
    width = weights[0].shape[-1]
    scalars, arrays = [mine], [gain, *pieces, *before]
    if ending is None:
        outs = [struct((rows, 3 * width), F32), struct((rows, 1), F32)]
        if before:
            outs = [struct((rows, 2 * width), F32), struct((rows, 1), F32)]
            outs += [struct((rows, width), F32), struct((rows, 1), F32)]
    if not before:
        arrays.append(w_out)
        outs += [struct((w_out.shape[1] // 4, w_out.shape[0]), BF16)] * 4
        outs += [struct((len(n), pieces[0].shape[1], width), BF16) for _, n in AHEAD]
    if ending is not None:
        base, cosine, sine, asked = ending
        scalars.append(base)
        arrays += [cosine, sine, asked]
        outs = [struct((2 * width, rows), BF16)]
        if 2 in kinds:
            outs = [struct((width, rows), BF16), struct((width, asked.shape[1]), BF16)]
    body = partial(project_body, blocks, not before, ending is not None, kinds)
    if before:
        arrays = list(weights) + arrays
        return call(body, outs, scalars, arrays, after, length=length)
    scratch = [
        pltpu.VMEM((3, len(blocks), pieces[0].shape[1], width), BF16),
        pltpu.SemaphoreType.DMA((3, 4)),
    ]
    return call(body, outs, scalars, arrays, after, scratch, length, weights)


def copy_body(source, *refs):
    refs[-1][...] = source[...]


def prepare_body(base, lengths, segments, inverse, cosine, sine, low, asked_low):
    prompts = lengths.shape[0]
    rows = segments.shape[1]
    segment = segments[...]
    asked = lax.broadcasted_iota(jnp.int32, asked_low.shape, 1)
    each = asked_low.shape[1] // prompts
    first = jnp.zeros((1, rows), jnp.int32)
    asked_first = jnp.zeros(asked_low.shape, jnp.int32)
    start = jnp.int32(0)
    for p in range(prompts):
        first = jnp.where(segment == p, start, first)
        asked_first = jnp.where(
            (asked >= p * each) & (asked < (p + 1) * each), start, asked_first
        )
        start = start + lengths[p]
    valid = segment >= 0
    slot = base[0] + lax.broadcasted_iota(jnp.int32, (1, rows), 1)
    position = jnp.where(valid, slot - first, 0).astype(F32)
    angles = inverse[...] * position
    cosine[...] = jnp.cos(angles)
    sine[...] = jnp.sin(angles)
    low[...] = jnp.where(valid, first - base[0], NEVER)
    asked_low[...] = asked_first - base[0]


def pick_body(base, slots, tokens, out):
    rows = tokens.shape[0]
    count = slots.shape[1]
    row = base[0] + lax.broadcasted_iota(jnp.int32, (rows, count), 0)
    out[...] = mm_first(tokens[...], (slots[...] == row).astype(BF16)).astype(BF16)


def add_body(first, second, *refs):
    refs[-1][...] = first[...] + second[...]


def request_body(count, low, high, block, *refs):
    out = refs[-1]
    query = sum(part[...] for part in refs[:count])
    width, rows = query.shape
    half = block.shape[1] // 2
    allowed = []
    for i in range(2):
        key_slot = i * half + lax.broadcasted_iota(jnp.int32, (half, rows), 0)
        allowed.append((key_slot >= low[...]) & (key_slot <= high[...]))
    results = []
    levels = []
    for h in range(width // HD):
        at = slice(h * HD, (h + 1) * HD)
        k_at = slice(2 * h * HD, (2 * h + 1) * HD)
        v_at = slice((2 * h + 1) * HD, (2 * h + 2) * HD)
        scores = [
            jnp.where(
                allowed[i], mm_first(block[k_at, i * half : (i + 1) * half], query[at, :]) * HD**-0.5, NEG
            )
            for i in range(2)
        ]
        largest = jnp.maximum(*[jnp.max(part, axis=0, keepdims=True) for part in scores])
        largest = jnp.maximum(largest, FLOOR)
        weights = [jnp.exp(part - largest) for part in scores]
        total = sum(jnp.sum(part, axis=0, keepdims=True) for part in weights)
        mixed = sum(
            mm(block[v_at, i * half : (i + 1) * half], weights[i].astype(BF16)) for i in range(2)
        )
        filled = total > 0
        safe = jnp.where(filled, total, 1.0)
        results.append((mixed * (1.0 / safe)).astype(BF16))
        levels.append(jnp.where(filled, largest + jnp.log(safe), NEG))
    for h, result in enumerate(results):
        out[h * HD : (h + 1) * HD, :] = result
    out[width:, :] = pack_levels(levels)


def pack_levels(levels):
    row = lax.broadcasted_iota(jnp.int32, (LEVEL_ROWS, levels[0].shape[1]), 0)
    packed = jnp.zeros(row.shape, F32)
    for h, level in enumerate(levels):
        for part in range(3):
            rounded = level.astype(BF16).astype(F32)
            packed = jnp.where(row == 3 * h + part, rounded, packed)
            level = level - rounded
    return packed.astype(BF16)


def combine_body(flip, own, other, *refs):
    out = refs[-1]
    width = own.shape[0] - LEVEL_ROWS
    turned = flip[0] > 0
    a = own[...].astype(F32)
    b = other[...].astype(F32)
    lower = jnp.where(turned, b, a)
    upper = jnp.where(turned, a, b)
    levels = []
    results = []
    for h in range(width // HD):
        marks = []
        for side in (lower, upper):
            at = width + 3 * h
            marks.append(side[at : at + 1] + side[at + 1 : at + 2] + side[at + 2 : at + 3])
        top = jnp.maximum(*marks)
        one, two = (jnp.exp(mark - top) for mark in marks)
        both = one + two
        levels.append(top + jnp.log(both))
        at = slice(h * HD, (h + 1) * HD)
        results.append((lower[at] * (one / both) + upper[at] * (two / both)).astype(BF16))
    for h, result in enumerate(results):
        out[h * HD : (h + 1) * HD, :] = result
    if out.shape[0] > width:
        out[width:, :] = pack_levels(levels)


def combine(flip, own, other, rows, after=()):
    return call(
        combine_body, [struct((rows, own.shape[1]), BF16)], [flip], [own, other], after,
        blocked=True,
    )[0]


def attend_body(distances, last, mine, low, query, *refs):
    width, rows = query.shape
    half = rows // 2
    heads = width // HD
    blocks = refs[: len(distances)]
    state = refs[len(distances) :]
    accum, largest, total = refs[-3:]
    if distances[0] == 0:
        accum[...] = jnp.zeros(accum.shape, F32)
        largest[...] = jnp.full(largest.shape, FLOOR, F32)
        total[...] = jnp.zeros(total.shape, F32)
    else:
        accum[...] = state[0][...]
        largest[...] = state[1][...]
        total[...] = state[2][...]

    def visit(distance, block, i, until, j):
        q_at = slice(i * half, until * half)
        k_half = slice(j * half, (j + 1) * half)
        shape = (half, (until - i) * half)
        key_slot = (
            j * half - distance * rows + lax.broadcasted_iota(jnp.int32, shape, 0)
        )
        allowed = key_slot >= low[:, q_at]
        if distance == 0:
            query_slot = i * half + lax.broadcasted_iota(jnp.int32, shape, 1)
            allowed = allowed & (key_slot <= query_slot)
        scores = [
            mm_first(
                block[2 * h * HD : (2 * h + 1) * HD, k_half],
                query[h * HD : (h + 1) * HD, q_at],
            )
            for h in range(heads)
        ]
        parts = []
        for h in range(heads):
            score = jnp.where(allowed, scores[h] * (HD**-0.5 * LOG2_E), NEG)
            m_old = largest[h : h + 1, q_at]
            m_new = jnp.maximum(m_old, jnp.max(score, axis=0, keepdims=True))
            parts.append((m_new, jnp.exp2(score - m_new), jnp.exp2(m_old - m_new)))
        done = []
        for h, (m_new, weights, factor) in enumerate(parts):
            v_at = slice((2 * h + 1) * HD, (2 * h + 2) * HD)
            t_new = total[h : h + 1, q_at] * factor + jnp.sum(weights, axis=0, keepdims=True)
            mixed = accum[h * HD : (h + 1) * HD, q_at] * factor + mm(
                block[v_at, k_half], weights.astype(BF16)
            )
            done.append((m_new, t_new, mixed))
        for h, (m_new, t_new, mixed) in enumerate(done):
            accum[h * HD : (h + 1) * HD, q_at] = mixed
            largest[h : h + 1, q_at] = m_new
            total[h : h + 1, q_at] = t_new

    limits = [jnp.min(low[:, i * half : (i + 1) * half]) for i in range(2)]
    for distance, block in zip(distances, blocks):
        for j in range(2):
            end = (j + 1) * half - distance * rows
            if distance == 0 and j == 1:
                pl.when(limits[1] < end)(partial(visit, distance, block, 1, 2, j))
            else:
                pl.when(limits[1] < end)(partial(visit, distance, block, 0, 2, j))
                pl.when((limits[1] >= end) & (limits[0] < end))(
                    partial(visit, distance, block, 0, 1, j)
                )
    if last:
        out = refs[-4]
        for h in range(heads):
            at = slice(h * HD, (h + 1) * HD)
            t_h = total[h : h + 1, :]
            accum[at, :] = accum[at, :] * (1.0 / jnp.where(t_h > 0, t_h, 1.0))
        out[...] = accum[...].T.astype(BF16)


def attend(distances, last, mine, low, query, blocks, state, length=0, after=()):
    width, rows = query.shape
    shapes = [struct((width, rows), F32), struct((8, rows), F32), struct((8, rows), F32)]
    scratch = []
    outs = shapes
    if last:
        scratch = [pltpu.VMEM(s.shape, s.dtype) for s in shapes]
        outs = [struct((rows, width), BF16)]
    return call(
        partial(attend_body, distances, last),
        outs,
        [mine],
        [low, query, *blocks, *state],
        after,
        scratch,
        length,
        blocked=distances[0] > 0,
    )


def rows_body(gain_far, weight_far, *refs):
    parts, weights = refs[:4], refs[4:7]
    tokens = refs[7]
    squares, scaled, again, gain, own_weight, sems = refs[-6:]
    copies = [
        pltpu.make_async_copy(weight_far, own_weight, sems.at[0]),
        pltpu.make_async_copy(gain_far, gain, sems.at[1]),
    ]
    for copy in copies:
        copy.start()
    summed = sum(
        mm(w[...], a[...]).astype(BF16).astype(F32) for a, w in zip(parts[1:], weights)
    )
    copies[0].wait()
    summed = summed + mm(own_weight[...], parts[0][...]).astype(BF16).astype(F32)
    rows = tokens[...].astype(F32) + summed
    squares[...] = jnp.sum(rows * rows, axis=0, keepdims=True)
    copies[1].wait()
    scaled[...] = (rows * (gain[...] * SHRINK)).astype(BF16)
    again[...] = scaled[...]


def logits_body(limit, start, vocab, scaled, *refs):
    out = refs[-1]
    first = (start[0] + pl.program_id(0)) * out.shape[0]
    row = first + lax.broadcasted_iota(jnp.int32, out.shape, 0)
    out[...] = jnp.where(row < limit, mm(vocab[...], scaled[...]), NEG).astype(BF16)


def half_logits(start, vocab, scaled, after=()):
    limit, width = vocab.shape
    count = scaled.shape[1]
    tile = pl.cdiv(limit, 4 * 32) * 32
    return pl.pallas_call(
        partial(logits_body, limit),
        grid_spec=pltpu.PrefetchScalarGridSpec(
            num_scalar_prefetch=1,
            grid=(2,),
            in_specs=[
                pl.BlockSpec((tile, width), lambda i, start: (start[0] + i, 0)),
                pl.BlockSpec((width, count), lambda i, start: (0, 0)),
            ]
            + [ANYWHERE] * len(after),
            out_specs=pl.BlockSpec((tile, count), lambda i, start: (i, 0)),
        ),
        out_shape=struct((2 * tile, count), BF16),
        compiler_params=pltpu.CompilerParams(vmem_limit_bytes=VMEM_LIMIT),
        cost_estimate=pl.CostEstimate(flops=0, bytes_accessed=0, transcendentals=0),
    )(start, vocab, scaled, *after)


def fold_body(side, kept, came, send, keep):
    quarter = send.shape[0]
    for out, turn in ((send, 1 - side[0]), (keep, side[0])):
        at = pl.ds(pl.multiple_of(turn * quarter, 16), quarter)
        out[...] = (kept[at, :].astype(F32) + came[at, :].astype(F32)).astype(out.dtype)


def top_body(kept, came, *refs):
    out = refs[-1]
    out[...] = jnp.max(kept[...] + came[...].astype(F32), axis=0, keepdims=True)


def pair_body(first, second, *refs):
    refs[-1][0:1, :] = first[...]
    refs[-1][1:2, :] = second[...]


def split_columns(mine, source, outs):
    width = outs[0].shape[0]
    for b in range(4):
        at = pl.ds(pl.multiple_of((mine[0] ^ b) * width, width), width)
        outs[b][...] = source[:, at].T


def shards(
    tokens,
    norm_gain,
    w_query,
    w_key,
    w_value,
    w_out,
    final_gain,
    w_vocab,
    segment_ids,
    prompt_lengths,
    request_slots,
):
    rows, columns = tokens.shape
    half = rows // 2
    width = w_query.shape[1]
    heads = width // HD
    n_seq = lax.axis_size("seq")
    span = n_seq // 4
    seq_index = lax.axis_index("seq")
    tp_index = lax.axis_index("tp")
    mine = tp_index.reshape(1)
    base = seq_index * rows
    requests = request_slots.shape[0]

    powers = np.arange(HD // 2, dtype=np.float32) * np.float32(2.0 / HD)
    inverse = (np.float32(10000.0) ** -powers).astype(np.float32)[:, None]
    cosine, sine, low, request_low = call(
        prepare_body,
        [
            struct((HD // 2, rows), F32),
            struct((HD // 2, rows), F32),
            struct((1, rows), jnp.int32),
            struct((1, requests), jnp.int32),
        ],
        [base.reshape(1), prompt_lengths],
        [segment_ids[None, :], jnp.asarray(inverse)],
        blocked=True,
    )
    far = swap(tokens, "tp", 2)
    pieces = [tokens, swap(tokens, "tp", 1), far]
    gain = norm_gain.reshape(4, columns)
    weights = [
        pltpu.with_memory_space_constraint(w, pltpu.HBM) for w in (w_key, w_value, w_query)
    ]
    *sums, w_split, w_1, w_2, w_3, far_weights, last_kv, last_query = project(
        (0, 1), mine, gain, pieces[:2], weights, after=(cosine,), w_out=w_out
    )
    w_parts = [w_split] + [swap(w, "tp", b) for b, w in ((1, w_1), (2, w_2), (3, w_3))]
    (relayed,) = call(copy_body, [struct(far.shape, BF16)], [], [far], sums[1:])
    pieces.append(swap(relayed, "tp", 1))

    asked = request_slots[None, :]
    inside = asked - base
    (own_tokens,) = call(
        pick_body, [struct((columns, requests), BF16)], [base.reshape(1)], [asked, tokens],
        blocked=True,
    )
    all_tokens = [own_tokens]
    last_gain = final_gain[:, None]
    *kv_sums, query_sums, query_squares = project(
        (2,), mine, gain, pieces[2:3], [far_weights], sums, None, (last_gain,), length=10
    )
    ending = (base.reshape(1), cosine, sine, asked)
    query, own_query = project(
        (3,), mine, gain, pieces[3:], [last_query], (query_sums, query_squares), ending, (), 2, (2,)
    )
    asking = [own_query] + [shifted(own_query, "seq", -by) for by in range(1, span + 1)]
    bit = n_seq // 2
    while bit:
        all_tokens += call(
            add_body,
            [struct(own_tokens.shape, BF16)],
            [],
            [all_tokens[-1], swap(all_tokens[-1], "seq", bit)],
            sums[1:2] if len(all_tokens) == 1 else (own_query,),
        )
        bit //= 2
    (kv,) = project(
        (3,),
        mine,
        gain,
        pieces[3:],
        [last_kv],
        kv_sums,
        ending,
        (own_query,),
        10,
        (0, 1),
    )

    kv_cache = jnp.transpose(kv.reshape(heads, 2 * HD, rows), (0, 2, 1))
    behind = shifted(kv, "seq", 1)

    (mixed,) = call(
        partial(request_body, len(asking)),
        [struct((width + LEVEL_ROWS, requests), BF16)],
        [],
        [request_low, inside, kv, *asking],
        all_tokens[3:4],
    )
    own_state = attend((0,), False, mine, low, query, (kv,), (), length=10, after=(mixed,))

    afters = [own_state[1:2], all_tokens[-1:] if n_seq > 8 else (), w_parts[2:3]]
    stages = [mixed]
    bit = 1
    while bit < n_seq:
        flip = ((seq_index & bit) > 0).astype(jnp.int32).reshape(1)
        after = afters.pop(0) if afters else ()
        bit *= 2
        kept_rows = width + LEVEL_ROWS if bit < n_seq else width
        other = swap(stages[-1], "seq", bit // 2)
        stages.append(combine(flip, stages[-1], other, kept_rows, after))
    request_mixed = spread(stages[-1])
    (later_kv,) = call(copy_body, [struct(kv.shape, BF16)], [], [kv], stages[-1:])

    core = tp_index & 1
    side = tp_index >> 1
    squares, scaled, again = call(
        rows_body,
        [struct((1, requests), F32)] + [struct(own_tokens.shape, BF16)] * 2,
        [],
        [*request_mixed, *w_parts[1:], all_tokens[-1]],
        scratch=[
            pltpu.VMEM((columns, 1), F32),
            pltpu.VMEM((columns, width), BF16),
            pltpu.SemaphoreType.DMA((2,)),
        ],
        far=pinned([last_gain, w_split]),
    )
    vocab = pltpu.with_memory_space_constraint(w_vocab.T, pltpu.HBM)
    sent = half_logits((2 * (1 - core)).reshape(1), vocab, scaled)
    kept = half_logits((2 * core).reshape(1), vocab, again, (sent,))
    quarter = kept.shape[0] // 2
    sent, kept = call(
        fold_body,
        [struct((quarter, requests), BF16), struct((quarter, requests), F32)],
        [side.reshape(1)],
        [kept, swap(sent, "tp", 1)],
    )
    blocks = [behind] + [shifted(later_kv, "seq", by) for by in range(2, span + 1)]
    distances = list(range(1, span + 1))
    state = own_state
    while distances:
        last = len(distances) <= 3
        state = attend(distances[:3], last, mine, low, query, blocks[:3], state, 30)
        distances, blocks = distances[3:], blocks[3:]
    (best,) = call(
        top_body, [struct((1, requests), F32)], [], [kept, swap(sent, "tp", 2)], state[:1]
    )
    bit = 1
    while bit < n_seq:
        best = jnp.maximum(best, swap(best, "seq", bit))
        bit *= 2
    attended = spread(state[0])
    (pair,) = call(
        pair_body, [struct((2, requests), F32)], [], [best, squares], attended[2:3]
    )
    for bit in (2, 1):
        other = swap(pair, "tp", bit)
        pair = jnp.stack([jnp.maximum(pair[0], other[0]), pair[1] + other[1]])
    hidden_norm = jnp.sqrt(pair[1] / D + EPS)
    top_logit = pair[0] / hidden_norm * (1.0 / SHRINK)

    summed = sum(
        mm_last(part, w).astype(BF16).astype(F32) for part, w in zip(attended, w_parts)
    )
    hidden = (tokens.astype(F32) + summed).astype(BF16)
    return (kv_cache, hidden, hidden_norm, top_logit)


def solution(mesh):
    return jax.shard_map(
        shards,
        mesh=mesh,
        in_specs=(
            P("seq", "tp"),
            P(),
            P(None, "tp"),
            P(None, "tp"),
            P(None, "tp"),
            P("tp", None),
            P("tp"),
            P("tp", "seq"),
            P("seq"),
            P(),
            P(),
        ),
        out_specs=(P("tp", "seq", None), P("seq", "tp"), P(), P()),
        check_vma=False,
    )
```

time: 136 us -> 120 us (0.88)
  waiting for transfers between devices: 33.1 us -> 26.1 us
  other arithmetic: 5.03 us -> 0.56 us
  starting transfers between devices: 46 us -> 42.6 us
    ppermute x25, waiting for transfers between devices: 32.9 us -> 26 us  [swap(): return lax.ppermute(array, axis, [(i, i ^ bit) for i in range(count)])]
    ppermute x25, starting transfers between devices: 36.7 us -> 33.3 us  [swap(): return lax.ppermute(array, axis, [(i, i ^ bit) for i in range(count)])]
    unnamed x38 -> x56, local copies, waits for them, and re-layouts: 9.73 us -> 10.6 us
    pallas_call x16 -> x23, Pallas kernels: 33.6 us -> 33.8 us  [the longest x21 27.8 us: call(): pl.pallas_call(body, grid=(1,) if blocked else (), out_shape=outs, in_spe...]
  transfers between devices with their start and end apart: 29 -> 29, of which waited for: 15 -> 11; matrix products, arithmetic and copies ran while one was open for 7% -> 3% of each run, Pallas kernels for 22% -> 28%
where the time goes in v2:
time: 120 us
  starting transfers between devices  42.6 us (36%)
  Pallas kernels  33.8 us (28%)
  waiting for transfers between devices  26.1 us (22%)
  local copies, waits for them, and re-layouts  12.2 us (10%)
  matrix products  3.38 us (3%)
    ppermute x25, starting transfers between devices, swap(): return lax.ppermute(array, axis, [(i, i ^ bit) for i in range(count)])  33.3 us
    pallas_call x21, Pallas kernels, call(): pl.pallas_call(body, grid=(1,) if blocked else (), out_shape=outs, in_spe...  27.8 us
    ppermute x25, waiting for transfers between devices, swap(): return lax.ppermute(array, axis, [(i, i ^ bit) for i in range(count)])  26 us
    unnamed x56, local copies, waits for them, and re-layouts  10.6 us
    ppermute x4, starting transfers between devices, shifted(): return lax.ppermute(array, axis, pairs)  9.36 us
    pallas_call x2, Pallas kernels, half_logits(): pl.pallas_call(partial(logits_body, limit), grid_spec=pltpu.PrefetchScala...  6.01 us
    dot_general x4, matrix products, mm_last(): lax.dot_general(a, b, (((1,), (1,)), ((), ())), preferred_element_type=F32)  3.38 us
  transfers between devices with their start and end apart: 29, of which 11 were waited for; matrix products, arithmetic and copies ran while one was open for 3% of the time, Pallas kernels for 28%

profile of v2, /device:TPU:0, one launch (start us, length us, event | category | flops | bytes accessed | tf_op | source)
XLA Modules:
  0.0 119.7 jit_solution(1514344115351292822)
XLA Ops:
  1.1 2.6 %collective-permute-start.1 = (bf16[512,768]{1,0:T(8,128)(2,1)}, bf16[512,768]{1,0:T(8,128)(2,1)S(1)}, u32[]{:S(2)}, u32[]{:S(2)}) collective-permute-start(bf16[512,768]{1,0:T(8,128)(2,1)} %tokens.1), channel_id=1, source_target_pairs={{0,2},{1,3},{2,0},{3,1},{4,6},{5,7},{6,4},{7,5},{8,10},{9,11},{10,... | collective-permute-start | bytes 2359304 | tf_op jit(solution)/shard_map/ppermute | solution.py:65
  6.0 2.7 %collective-permute-start.6 = (bf16[768,128]{1,0:T(8,128)(2,1)S(1)}, bf16[768,128]{1,0:T(8,128)(2,1)S(1)}, u32[]{:S(2)}, u32[]{:S(2)}) collective-permute-start(bf16[768,128]{1,0:T(8,128)(2,1)S(1)} %shard_map.153.first), channel_id=1, source_target_pairs={{0,16},{4,20},{8,24},{12,28},{16,0},{20,4},{24,8},{28,12},{1,17},{... | collective-permute-start | bytes 589832 | tf_op jit(solution)/shard_map/ppermute | solution.py:65
  15.0 7.4 %shard_map.148 = (f32[512,1152]{1,0:T(8,128)S(1)}, f32[512,1]{1,0:T(8,128)S(1)}, bf16[768,384]{1,0:T(8,128)(2,1)S(1)}, bf16[768,384]{1,0:T(8,128)(2,1)}, bf16[76...) custom-call(s32[1]{0:T(128)} %bitcast.refs_0_.mine, ...), custom_call_target="tpu_custom_call" | custom-call | tf_op jit(solution)/shard_map/pallas_call | solution.py:38
  31.9 2.7 %collective-permute-start.8 = (bf16[768,128]{1,0:T(8,128)(2,1)S(1)}, bf16[768,128]{1,0:T(8,128)(2,1)S(1)}, u32[]{:S(2)}, u32[]{:S(2)}) collective-permute-start(bf16[768,128]{1,0:T(8,128)(2,1)S(1)} %shard_map.155.first), channel_id=1, source_target_pairs={{0,4},{4,0},{8,12},{12,8},{16,20},{20,16},{24,28},{28,24},{1,5},{5... | collective-permute-start | bytes 589832 | tf_op jit(solution)/shard_map/ppermute | solution.py:65
  34.6 2.0 %shard_map.152.block.refs_0_.source = bf16[768,512]{1,0:T(8,128)(2,1)} custom-call(s32[1]{0:T(128)} %bitcast.refs_0_.mine, s32[1]{0:T(128)} %bitcast.1.base.refs_1_, bf16[2,768,384]{2,1,0:T(8,128)(2,1)S(1)} %get-tuple-element.32.refs_2_, f32[4,768]{1,0:T(4,128)S(1)} %reshape.57.refs_4_.refs_2_.refs_3_, bf16[512,768]{1,0:T(8,128)(2,1)S(1)} %collective-permute-done.2.refs_4_, ...), custom_call_target="tpu_custom_call" | custom-call | flops 10000000000 | tf_op jit(solution)/shard_map/pallas_call | solution.py:38
  36.6 3.9 %collective-permute-done.8.second = bf16[768,128]{1,0:T(8,128)(2,1)S(1)} collective-permute-done((bf16[768,128]{1,0:T(8,128)(2,1)S(1)}, bf16[768,128]{1,0:T(8,128)(2,1)S(1)}, u32[]{:S(2)}, u32[]{:S(2)}) %collective-permute-start.8) | collective-permute-done | bytes 196640 | tf_op jit(solution)/shard_map/ppermute | solution.py:65
  43.1 2.5 %collective-permute-start.9 = (bf16[400,128]{1,0:T(8,128)(2,1)S(1)}, bf16[400,128]{1,0:T(8,128)(2,1)S(1)}, u32[]{:S(2)}, u32[]{:S(2)}) collective-permute-start(bf16[400,128]{1,0:T(8,128)(2,1)S(1)} %shard_map.157.refs_1_.own), channel_id=1, source_target_pairs={{0,4},{4,0},{8,12},{12,8},{16,20},{20,16},{24,28},{28,24},{1,5},{5... | collective-permute-start | bytes 307208 | tf_op jit(solution)/shard_map/ppermute | solution.py:65
  46.8 1.9 %shard_map.158 = (f32[384,512]{1,0:T(8,128)S(1)}, f32[8,512]{1,0:T(8,128)S(1)}, f32[8,512]{1,0:T(8,128)S(1)}) custom-call(s32[1]{0:T(128)} %bitcast.refs_0_.mine, s32[1,512]{1,0:T(1,128)S(1)} %get-tuple-element.43.low, bf16[384,512]{1,0:T(8,128)(2,1)S(1)} %get-tuple-element.44.query, bf16[768,512]{1,0:T(8,128)(2,1)S(1)} %copy-done.3, ...), custom_call_target="tpu_custom_call" | custom-call | flops 10000000000 | tf_op jit(solution)/shard_map/pallas_call | solution.py:38
  51.9 3.7 %collective-permute-done.10.other = bf16[400,128]{1,0:T(8,128)(2,1)} collective-permute-done((bf16[400,128]{1,0:T(8,128)(2,1)}, bf16[400,128]{1,0:T(8,128)(2,1)}, u32[]{:S(2)}, u32[]{:S(2)}) %collective-permute-start.10) | collective-permute-done | bytes 102432 | tf_op jit(solution)/shard_map/ppermute | solution.py:65
  57.3 2.4 %collective-permute-start.11 = (bf16[400,128]{1,0:T(8,128)(2,1)}, bf16[400,128]{1,0:T(8,128)(2,1)}, u32[]{:S(2)}, u32[]{:S(2)}) collective-permute-start(bf16[400,128]{1,0:T(8,128)(2,1)} %shard_map.160.own), channel_id=1, source_target_pairs={{0,16},{4,20},{8,24},{12,28},{16,0},{20,4},{24,8},{28,12},{1,17},{... | collective-permute-start | bytes 307208 | tf_op jit(solution)/shard_map/ppermute | solution.py:65
  59.7 3.8 %collective-permute-start.3 = (bf16[768,512]{1,0:T(8,128)(2,1)S(1)}, bf16[768,512]{1,0:T(8,128)(2,1)}, u32[]{:S(2)}, u32[]{:S(2)}) collective-permute-start(bf16[768,512]{1,0:T(8,128)(2,1)S(1)} %copy-done.4), channel_id=1, source_target_pairs={{0,4},{4,8},{8,12},{12,16},{16,20},{20,24},{24,28},{1,5},{5,9},{9,... | collective-permute-start | bytes 2359304 | tf_op jit(solution)/shard_map/ppermute | solution.py:71
  67.4 3.0 %collective-permute-start.13 = (bf16[768,512]{1,0:T(8,128)(2,1)}, bf16[768,512]{1,0:T(8,128)(2,1)}, u32[]{:S(2)}, u32[]{:S(2)}) collective-permute-start(bf16[768,512]{1,0:T(8,128)(2,1)} %shard_map.162), channel_id=1, source_target_pairs={{0,8},{4,12},{8,16},{12,20},{16,24},{20,28},{1,9},{5,13},{9,17},{1... | collective-permute-start | bytes 2359304 | tf_op jit(solution)/shard_map/ppermute | solution.py:71
  70.4 1.9 %collective-permute-start.20 = (bf16[384,128]{1,0:T(8,128)(2,1)}, bf16[384,128]{1,0:T(8,128)(2,1)}, u32[]{:S(2)}, u32[]{:S(2)}) collective-permute-start(bf16[384,128]{1,0:T(8,128)(2,1)} %shard_map.161.refs_0_), channel_id=1, source_target_pairs={{0,2},{1,3},{2,0},{3,1},{4,6},{5,7},{6,4},{7,5},{8,10},{9,11},{10,... | collective-permute-start | bytes 294920 | tf_op jit(solution)/shard_map/ppermute | solution.py:65
  72.4 3.0 %collective-permute-done.20.refs_2_ = bf16[384,128]{1,0:T(8,128)(2,1)} collective-permute-done((bf16[384,128]{1,0:T(8,128)(2,1)}, bf16[384,128]{1,0:T(8,128)(2,1)}, u32[]{:S(2)}, u32[]{:S(2)}) %collective-permute-start.20) | collective-permute-done | bytes 98336 | tf_op jit(solution)/shard_map/ppermute | solution.py:65
  77.0 3.2 %shard_map.164 = (f32[1,128]{1,0:T(1,128)S(1)}, bf16[768,128]{1,0:T(8,128)(2,1)S(1)}, bf16[768,128]{1,0:T(8,128)(2,1)S(1)}) custom-call(f32[768,1]{1,0:T(8,128)} %copy-done.8, bf16[768,384]{1,0:T(8,128)(2,1)} %copy-done.5, bf16[384,128]{1,0:T(8,128)(2,1)} %shard_map.161.refs_0_, bf16[384,128]{1,0:T(8,128)(2,1)} %collective-permute-done.19.refs_1_, ...), custom_call_target="tpu_custom_call" | custom-call | tf_op jit(solution)/shard_map/pallas_call | solution.py:38
  80.9 3.3 %shard_map.165.refs_0_ = bf16[2048,128]{1,0:T(8,128)(2,1)} custom-call(s32[1]{0:T(128)} %bitcast.13.start, bf16[4008,768]{1,0:T(8,128)(2,1)} %bitcast.36, bf16[768,128]{1,0:T(8,128)(2,1)S(1)} %get-tuple-element.54.scaled), custom_call_target="tpu_custom_call" | custom-call | tf_op jit(solution)/shard_map/pallas_call | solution.py:475
  84.4 2.7 %shard_map.166.kept = bf16[2048,128]{1,0:T(8,128)(2,1)S(1)} custom-call(s32[1]{0:T(128)} %bitcast.11.start, bf16[4008,768]{1,0:T(8,128)(2,1)} %bitcast.37, bf16[768,128]{1,0:T(8,128)(2,1)S(1)} %copy-done.12, bf16[2048,128]{1,0:T(8,128)(2,1)} %shard_map.165.refs_0_), custom_call_target="tpu_custom_call" | custom-call | tf_op jit(solution)/shard_map/pallas_call | solution.py:475
  88.3 2.0 %collective-permute-start.23 = (bf16[1024,128]{1,0:T(8,128)(2,1)S(1)}, bf16[1024,128]{1,0:T(8,128)(2,1)S(1)}, u32[]{:S(2)}, u32[]{:S(2)}) collective-permute-start(bf16[1024,128]{1,0:T(8,128)(2,1)S(1)} %get-tuple-element.56), channel_id=1, source_target_pairs={{0,2},{1,3},{2,0},{3,1},{4,6},{5,7},{6,4},{7,5},{8,10},{9,11},{10,... | collective-permute-start | bytes 786440 | tf_op jit(solution)/shard_map/ppermute | solution.py:65
  90.4 1.9 %shard_map.163.refs_0_ = bf16[512,384]{1,0:T(8,128)(2,1)S(1)} custom-call(s32[1]{0:T(128)} %bitcast.refs_0_.mine, s32[1,512]{1,0:T(1,128)S(1)} %copy-done.21, bf16[384,512]{1,0:T(8,128)(2,1)S(1)} %copy-done.23, bf16[768,512]{1,0:T(8,128)(2,1)} %collective-permute-done.3.refs_0_, bf16[768,512]{1,0:T(8,128)(2,1)} %collective-permute-done.13.refs_1_, ...), custom_call_target="tpu_custom_call" | custom-call | flops 30000001024 | tf_op jit(solution)/shard_map/pallas_call | solution.py:38
  92.5 5.0 %collective-permute-done.23.came = bf16[1024,128]{1,0:T(8,128)(2,1)S(1)} collective-permute-done((bf16[1024,128]{1,0:T(8,128)(2,1)S(1)}, bf16[1024,128]{1,0:T(8,128)(2,1)S(1)}, u32[]{:S(2)}, u32[]{:S(2)}) %collective-permute-start.23) | collective-permute-done | bytes 262176 | tf_op jit(solution)/shard_map/ppermute | solution.py:65
  97.6 4.8 %collective-permute-start.24 = (f32[1,128]{1,0:T(1,128)S(1)}, f32[1,128]{1,0:T(1,128)S(1)}, u32[]{:S(2)}, u32[]{:S(2)}) collective-permute-start(f32[1,128]{1,0:T(1,128)S(1)} %shard_map.168), channel_id=1, source_target_pairs={{0,4},{4,0},{8,12},{12,8},{16,20},{20,16},{24,28},{28,24},{1,5},{5... | collective-permute-start | bytes 1544 | tf_op jit(solution)/shard_map/ppermute | solution.py:65
  104.0 2.7 %collective-permute-start.25 = (f32[1,128]{1,0:T(1,128)S(1)}, f32[1,128]{1,0:T(1,128)S(1)}, u32[]{:S(2)}, u32[]{:S(2)}) collective-permute-start(f32[1,128]{1,0:T(1,128)S(1)} %max.20), channel_id=1, source_target_pairs={{0,8},{4,12},{8,0},{12,4},{16,24},{20,28},{24,16},{28,20},{1,9},{5... | collective-permute-start | bytes 1544 | tf_op jit(solution)/shard_map/ppermute | solution.py:65
  108.3 2.7 %collective-permute-start.26 = (f32[1,128]{1,0:T(1,128)S(1)}, f32[1,128]{1,0:T(1,128)S(1)}, u32[]{:S(2)}, u32[]{:S(2)}) collective-permute-start(f32[1,128]{1,0:T(1,128)S(1)} %max.21), channel_id=1, source_target_pairs={{0,16},{4,20},{8,24},{12,28},{16,0},{20,4},{24,8},{28,12},{1,17},{... | collective-permute-start | bytes 1544 | tf_op jit(solution)/shard_map/ppermute | solution.py:65
  113.6 2.7 %collective-permute-done.27 = f32[2,128]{1,0:T(2,128)S(1)} collective-permute-done((f32[2,128]{1,0:T(2,128)S(1)}, f32[2,128]{1,0:T(2,128)S(1)}, u32[]{:S(2)}, u32[]{:S(2)}) %collective-permute-start.27) | collective-permute-done | bytes 1056 | tf_op jit(solution)/shard_map/ppermute | solution.py:65
  (126 shorter events, 43.8 us)
Async XLA Ops:
  0.6 12.7 %collective-permute-start = (bf16[512,768]{1,0:T(8,128)(2,1)}, bf16[512,768]{1,0:T(8,128)(2,1)}, u32[]{:S(2)}, u32[]{:S(2)}) collective-permute-start(bf16[512,768]{1,0:T(8,128)(2,1)} %tokens.1), channel_id=1, source_target_pairs={{0,1},{1,0},{2,3},{3,2},{4,5},{5,4},{6,7},{7,6},{8,9},{9,8},{10,11... | collective-permute-start | bytes 2359304 | tf_op jit(solution)/shard_map/ppermute | solution.py:65
  1.1 21.3 %collective-permute-start.1 = (bf16[512,768]{1,0:T(8,128)(2,1)}, bf16[512,768]{1,0:T(8,128)(2,1)S(1)}, u32[]{:S(2)}, u32[]{:S(2)}) collective-permute-start(bf16[512,768]{1,0:T(8,128)(2,1)} %tokens.1), channel_id=1, source_target_pairs={{0,2},{1,3},{2,0},{3,1},{4,6},{5,7},{6,4},{7,5},{8,10},{9,11},{10,... | collective-permute-start | bytes 2359304 | tf_op jit(solution)/shard_map/ppermute | solution.py:65
  6.0 16.6 %collective-permute-start.6 = (bf16[768,128]{1,0:T(8,128)(2,1)S(1)}, bf16[768,128]{1,0:T(8,128)(2,1)S(1)}, u32[]{:S(2)}, u32[]{:S(2)}) collective-permute-start(bf16[768,128]{1,0:T(8,128)(2,1)S(1)} %shard_map.153.first), channel_id=1, source_target_pairs={{0,16},{4,20},{8,24},{12,28},{16,0},{20,4},{24,8},{28,12},{1,17},{... | collective-permute-start | bytes 589832 | tf_op jit(solution)/shard_map/ppermute | solution.py:65
  22.5 5.7 %collective-permute-start.2 = (bf16[512,768]{1,0:T(8,128)(2,1)S(1)}, bf16[512,768]{1,0:T(8,128)(2,1)S(1)}, u32[]{:S(2)}, u32[]{:S(2)}) collective-permute-start(bf16[512,768]{1,0:T(8,128)(2,1)S(1)} %shard_map.149), channel_id=1, source_target_pairs={{0,1},{1,0},{2,3},{3,2},{4,5},{5,4},{6,7},{7,6},{8,9},{9,8},{10,11... | collective-permute-start | bytes 2359304 | tf_op jit(solution)/shard_map/ppermute | solution.py:65
  22.7 9.2 %collective-permute-start.7 = (bf16[768,128]{1,0:T(8,128)(2,1)S(1)}, bf16[768,128]{1,0:T(8,128)(2,1)S(1)}, u32[]{:S(2)}, u32[]{:S(2)}) collective-permute-start(bf16[768,128]{1,0:T(8,128)(2,1)S(1)} %shard_map.154.first), channel_id=1, source_target_pairs={{0,8},{4,12},{8,0},{12,4},{16,24},{20,28},{24,16},{28,20},{1,9},{5... | collective-permute-start | bytes 589832 | tf_op jit(solution)/shard_map/ppermute | solution.py:65
  24.3 39.2 %collective-permute-start.12 = (bf16[768,384]{1,0:T(8,128)(2,1)}, bf16[768,384]{1,0:T(8,128)(2,1)S(1)}, u32[]{:S(2)}, u32[]{:S(2)}) collective-permute-start(bf16[768,384]{1,0:T(8,128)(2,1)} %get-tuple-element.47), channel_id=1, source_target_pairs={{0,2},{1,3},{2,0},{3,1},{4,6},{5,7},{6,4},{7,5},{8,10},{9,11},{10,... | collective-permute-start | bytes 1769480 | tf_op jit(solution)/shard_map/ppermute | solution.py:65
  25.7 46.7 %collective-permute-start.15 = (bf16[768,384]{1,0:T(8,128)(2,1)}, bf16[768,384]{1,0:T(8,128)(2,1)S(1)}, u32[]{:S(2)}, u32[]{:S(2)}) collective-permute-start(bf16[768,384]{1,0:T(8,128)(2,1)} %get-tuple-element.51), channel_id=1, source_target_pairs={{0,1},{1,0},{2,3},{3,2},{4,5},{5,4},{6,7},{7,6},{8,9},{9,8},{10,11... | collective-permute-start | bytes 1769480 | tf_op jit(solution)/shard_map/ppermute | solution.py:65
  29.2 11.6 %collective-permute-start.4 = (bf16[384,128]{1,0:T(8,128)(2,1)S(1)}, bf16[384,128]{1,0:T(8,128)(2,1)S(1)}, u32[]{:S(2)}, u32[]{:S(2)}) collective-permute-start(bf16[384,128]{1,0:T(8,128)(2,1)S(1)} %get-tuple-element.42.refs_10_.refs_0_), channel_id=1, source_target_pairs={{4,0},{8,4},{12,8},{16,12},{20,16},{24,20},{28,24},{5,1},{9,5},{13... | collective-permute-start | bytes 294920 | tf_op jit(solution)/shard_map/ppermute | solution.py:71
  30.5 10.3 %collective-permute-start.5 = (bf16[384,128]{1,0:T(8,128)(2,1)S(1)}, bf16[384,128]{1,0:T(8,128)(2,1)S(1)}, u32[]{:S(2)}, u32[]{:S(2)}) collective-permute-start(bf16[384,128]{1,0:T(8,128)(2,1)S(1)} %get-tuple-element.42.refs_10_.refs_0_), channel_id=1, source_target_pairs={{8,0},{12,4},{16,8},{20,12},{24,16},{28,20},{9,1},{13,5},{17,9},{2... | collective-permute-start | bytes 294920 | tf_op jit(solution)/shard_map/ppermute | solution.py:71
  31.9 8.6 %collective-permute-start.8 = (bf16[768,128]{1,0:T(8,128)(2,1)S(1)}, bf16[768,128]{1,0:T(8,128)(2,1)S(1)}, u32[]{:S(2)}, u32[]{:S(2)}) collective-permute-start(bf16[768,128]{1,0:T(8,128)(2,1)S(1)} %shard_map.155.first), channel_id=1, source_target_pairs={{0,4},{4,0},{8,12},{12,8},{16,20},{20,16},{24,28},{28,24},{1,5},{5... | collective-permute-start | bytes 589832 | tf_op jit(solution)/shard_map/ppermute | solution.py:65
  40.5 34.9 %collective-permute-start.18 = (bf16[768,384]{1,0:T(8,128)(2,1)}, bf16[768,384]{1,0:T(8,128)(2,1)S(1)}, u32[]{:S(2)}, u32[]{:S(2)}) collective-permute-start(bf16[768,384]{1,0:T(8,128)(2,1)} %get-tuple-element.52), channel_id=1, source_target_pairs={{0,3},{1,2},{2,1},{3,0},{4,7},{5,6},{6,5},{7,4},{8,11},{9,10},{10,... | collective-permute-start | bytes 1769480 | tf_op jit(solution)/shard_map/ppermute | solution.py:65
  43.1 6.5 %collective-permute-start.9 = (bf16[400,128]{1,0:T(8,128)(2,1)S(1)}, bf16[400,128]{1,0:T(8,128)(2,1)S(1)}, u32[]{:S(2)}, u32[]{:S(2)}) collective-permute-start(bf16[400,128]{1,0:T(8,128)(2,1)S(1)} %shard_map.157.refs_1_.own), channel_id=1, source_target_pairs={{0,4},{4,0},{8,12},{12,8},{16,20},{20,16},{24,28},{28,24},{1,5},{5... | collective-permute-start | bytes 307208 | tf_op jit(solution)/shard_map/ppermute | solution.py:65
  50.3 5.3 %collective-permute-start.10 = (bf16[400,128]{1,0:T(8,128)(2,1)}, bf16[400,128]{1,0:T(8,128)(2,1)}, u32[]{:S(2)}, u32[]{:S(2)}) collective-permute-start(bf16[400,128]{1,0:T(8,128)(2,1)} %shard_map.159.own), channel_id=1, source_target_pairs={{0,8},{4,12},{8,0},{12,4},{16,24},{20,28},{24,16},{28,20},{1,9},{5... | collective-permute-start | bytes 307208 | tf_op jit(solution)/shard_map/ppermute | solution.py:65
  57.3 7.6 %collective-permute-start.11 = (bf16[400,128]{1,0:T(8,128)(2,1)}, bf16[400,128]{1,0:T(8,128)(2,1)}, u32[]{:S(2)}, u32[]{:S(2)}) collective-permute-start(bf16[400,128]{1,0:T(8,128)(2,1)} %shard_map.160.own), channel_id=1, source_target_pairs={{0,16},{4,20},{8,24},{12,28},{16,0},{20,4},{24,8},{28,12},{1,17},{... | collective-permute-start | bytes 307208 | tf_op jit(solution)/shard_map/ppermute | solution.py:65
  59.7 30.6 %collective-permute-start.3 = (bf16[768,512]{1,0:T(8,128)(2,1)S(1)}, bf16[768,512]{1,0:T(8,128)(2,1)}, u32[]{:S(2)}, u32[]{:S(2)}) collective-permute-start(bf16[768,512]{1,0:T(8,128)(2,1)S(1)} %copy-done.4), channel_id=1, source_target_pairs={{0,4},{4,8},{8,12},{12,16},{16,20},{20,24},{24,28},{1,5},{5,9},{9,... | collective-permute-start | bytes 2359304 | tf_op jit(solution)/shard_map/ppermute | solution.py:71
  67.4 22.9 %collective-permute-start.13 = (bf16[768,512]{1,0:T(8,128)(2,1)}, bf16[768,512]{1,0:T(8,128)(2,1)}, u32[]{:S(2)}, u32[]{:S(2)}) collective-permute-start(bf16[768,512]{1,0:T(8,128)(2,1)} %shard_map.162), channel_id=1, source_target_pairs={{0,8},{4,12},{8,16},{12,20},{16,24},{20,28},{1,9},{5,13},{9,17},{1... | collective-permute-start | bytes 2359304 | tf_op jit(solution)/shard_map/ppermute | solution.py:71
  70.4 4.9 %collective-permute-start.20 = (bf16[384,128]{1,0:T(8,128)(2,1)}, bf16[384,128]{1,0:T(8,128)(2,1)}, u32[]{:S(2)}, u32[]{:S(2)}) collective-permute-start(bf16[384,128]{1,0:T(8,128)(2,1)} %shard_map.161.refs_0_), channel_id=1, source_target_pairs={{0,2},{1,3},{2,0},{3,1},{4,6},{5,7},{6,4},{7,5},{8,10},{9,11},{10,... | collective-permute-start | bytes 294920 | tf_op jit(solution)/shard_map/ppermute | solution.py:65
  88.3 9.2 %collective-permute-start.23 = (bf16[1024,128]{1,0:T(8,128)(2,1)S(1)}, bf16[1024,128]{1,0:T(8,128)(2,1)S(1)}, u32[]{:S(2)}, u32[]{:S(2)}) collective-permute-start(bf16[1024,128]{1,0:T(8,128)(2,1)S(1)} %get-tuple-element.56), channel_id=1, source_target_pairs={{0,2},{1,3},{2,0},{3,1},{4,6},{5,7},{6,4},{7,5},{8,10},{9,11},{10,... | collective-permute-start | bytes 786440 | tf_op jit(solution)/shard_map/ppermute | solution.py:65
  92.3 20.4 %collective-permute-start.16 = (bf16[512,384]{1,0:T(8,128)(2,1)S(1)}, bf16[512,384]{1,0:T(8,128)(2,1)S(1)}, u32[]{:S(2)}, u32[]{:S(2)}) collective-permute-start(bf16[512,384]{1,0:T(8,128)(2,1)S(1)} %shard_map.163.refs_0_), channel_id=1, source_target_pairs={{0,2},{1,3},{2,0},{3,1},{4,6},{5,7},{6,4},{7,5},{8,10},{9,11},{10,... | collective-permute-start | bytes 1179656 | tf_op jit(solution)/shard_map/ppermute | solution.py:65
  97.6 6.4 %collective-permute-start.24 = (f32[1,128]{1,0:T(1,128)S(1)}, f32[1,128]{1,0:T(1,128)S(1)}, u32[]{:S(2)}, u32[]{:S(2)}) collective-permute-start(f32[1,128]{1,0:T(1,128)S(1)} %shard_map.168), channel_id=1, source_target_pairs={{0,4},{4,0},{8,12},{12,8},{16,20},{20,16},{24,28},{28,24},{1,5},{5... | collective-permute-start | bytes 1544 | tf_op jit(solution)/shard_map/ppermute | solution.py:65
  104.0 4.3 %collective-permute-start.25 = (f32[1,128]{1,0:T(1,128)S(1)}, f32[1,128]{1,0:T(1,128)S(1)}, u32[]{:S(2)}, u32[]{:S(2)}) collective-permute-start(f32[1,128]{1,0:T(1,128)S(1)} %max.20), channel_id=1, source_target_pairs={{0,8},{4,12},{8,0},{12,4},{16,24},{20,28},{24,16},{28,20},{1,9},{5... | collective-permute-start | bytes 1544 | tf_op jit(solution)/shard_map/ppermute | solution.py:65
  108.3 4.4 %collective-permute-start.26 = (f32[1,128]{1,0:T(1,128)S(1)}, f32[1,128]{1,0:T(1,128)S(1)}, u32[]{:S(2)}, u32[]{:S(2)}) collective-permute-start(f32[1,128]{1,0:T(1,128)S(1)} %max.21), channel_id=1, source_target_pairs={{0,16},{4,20},{8,24},{12,28},{16,0},{20,4},{24,8},{28,12},{1,17},{... | collective-permute-start | bytes 1544 | tf_op jit(solution)/shard_map/ppermute | solution.py:65
  111.5 4.9 %collective-permute-start.14 = (bf16[512,384]{1,0:T(8,128)(2,1)S(1)}, bf16[512,384]{1,0:T(8,128)(2,1)S(1)}, u32[]{:S(2)}, u32[]{:S(2)}) collective-permute-start(bf16[512,384]{1,0:T(8,128)(2,1)S(1)} %shard_map.163.refs_0_), channel_id=1, source_target_pairs={{0,1},{1,0},{2,3},{3,2},{4,5},{5,4},{6,7},{7,6},{8,9},{9,8},{10,11... | collective-permute-start | bytes 1179656 | tf_op jit(solution)/shard_map/ppermute | solution.py:65
  113.6 4.6 %collective-permute-start.17 = (bf16[512,384]{1,0:T(8,128)(2,1)S(1)}, bf16[512,384]{1,0:T(8,128)(2,1)S(1)}, u32[]{:S(2)}, u32[]{:S(2)}) collective-permute-start(bf16[512,384]{1,0:T(8,128)(2,1)S(1)} %collective-permute-done.16.refs_0_), channel_id=1, source_target_pairs={{0,1},{1,0},{2,3},{3,2},{4,5},{5,4},{6,7},{7,6},{8,9},{9,8},{10,11... | collective-permute-start | bytes 1179656 | tf_op jit(solution)/shard_map/ppermute | solution.py:65
  (33 other events, 188.1 us)

commit v3 on v2

--- a/solution.py
+++ b/solution.py
@@ -159,7 +159,7 @@
         if 2 in kinds:
             query, own = refs[-2:]
         else:
-            kv = refs[-1]
+            kv = refs[-4]
         for h in range(width // HD):
             at = h * HD
             a = field[at : at + middle]
@@ -170,6 +170,10 @@
                 to, out = (at, query) if i == 2 else (2 * at, kv)
                 out[to : to + middle, :] = (a * cosine[...] - b * sine[...]).astype(BF16)
                 out[to + middle : to + HD, :] = (b * cosine[...] + a * sine[...]).astype(BF16)
+    if last and 2 not in kinds:
+        refs[-3][...] = kv[...]
+        refs[-2][...] = kv[...]
+        refs[-1][...] = kv[:, rows // 2 :]
     if last and 2 in kinds:
         row = base[0] + lax.broadcasted_iota(jnp.int32, (rows, asked.shape[1]), 0)
         own[...] = mm(query[...], (asked[...] == row).astype(BF16)).astype(BF16)
@@ -210,7 +214,7 @@
         base, cosine, sine, asked = ending
         scalars.append(base)
         arrays += [cosine, sine, asked]
-        outs = [struct((2 * width, rows), BF16)]
+        outs = [struct((2 * width, rows), BF16)] * 3 + [struct((2 * width, rows // 2), BF16)]
         if 2 in kinds:
             outs = [struct((width, rows), BF16), struct((width, asked.shape[1]), BF16)]
     body = partial(project_body, blocks, not before, ending is not None, kinds)
@@ -228,7 +232,13 @@
     refs[-1][...] = source[...]
 
 
-def prepare_body(base, lengths, segments, inverse, cosine, sine, low, asked_low):
+def twice_body(source, *refs):
+    refs[-2][...] = source[...]
+    refs[-1][...] = source[...]
+
+
+def prepare_body(base, lengths, segments, inverse, *refs):
+    cosine, sine, low, asked_low = refs[-4:]
     prompts = lengths.shape[0]
     rows = segments.shape[1]
     segment = segments[...]
@@ -265,7 +275,6 @@
 
 
 def request_body(count, low, high, block, *refs):
-    out = refs[-1]
     query = sum(part[...] for part in refs[:count])
     width, rows = query.shape
     half = block.shape[1] // 2
@@ -296,6 +305,7 @@
         safe = jnp.where(filled, total, 1.0)
         results.append((mixed * (1.0 / safe)).astype(BF16))
         levels.append(jnp.where(filled, largest + jnp.log(safe), NEG))
+    out = refs[-1]
     for h, result in enumerate(results):
         out[h * HD : (h + 1) * HD, :] = result
     out[width:, :] = pack_levels(levels)
@@ -313,7 +323,6 @@
 
 
 def combine_body(flip, own, other, *refs):
-    out = refs[-1]
     width = own.shape[0] - LEVEL_ROWS
     turned = flip[0] > 0
     a = own[...].astype(F32)
@@ -333,6 +342,7 @@
         levels.append(top + jnp.log(both))
         at = slice(h * HD, (h + 1) * HD)
         results.append((lower[at] * (one / both) + upper[at] * (two / both)).astype(BF16))
+    out = refs[-1]
     for h, result in enumerate(results):
         out[h * HD : (h + 1) * HD, :] = result
     if out.shape[0] > width:
@@ -341,19 +351,23 @@
 
 def combine(flip, own, other, rows, after=()):
     return call(
-        combine_body, [struct((rows, own.shape[1]), BF16)], [flip], [own, other], after,
+        combine_body,
+        [struct((rows, own.shape[1]), BF16)],
+        [flip],
+        [own, other],
+        after,
         blocked=True,
     )[0]
 
 
-def attend_body(distances, last, mine, low, query, *refs):
+def attend_body(sources, last, place, low, query, *refs):
     width, rows = query.shape
     half = rows // 2
     heads = width // HD
-    blocks = refs[: len(distances)]
-    state = refs[len(distances) :]
+    blocks = refs[: len(sources)]
+    state = refs[len(sources) :]
     accum, largest, total = refs[-3:]
-    if distances[0] == 0:
+    if sources[0][0] == 0:
         accum[...] = jnp.zeros(accum.shape, F32)
         largest[...] = jnp.full(largest.shape, FLOOR, F32)
         total[...] = jnp.zeros(total.shape, F32)
@@ -362,9 +376,9 @@
         largest[...] = state[1][...]
         total[...] = state[2][...]
 
-    def visit(distance, block, i, until, j):
+    def visit(distance, block, part, i, until, j):
         q_at = slice(i * half, until * half)
-        k_half = slice(j * half, (j + 1) * half)
+        k_half = slice(part * half, (part + 1) * half)
         shape = (half, (until - i) * half)
         key_slot = (
             j * half - distance * rows + lax.broadcasted_iota(jnp.int32, shape, 0)
@@ -400,16 +414,16 @@
             total[h : h + 1, q_at] = t_new
 
     limits = [jnp.min(low[:, i * half : (i + 1) * half]) for i in range(2)]
-    for distance, block in zip(distances, blocks):
-        for j in range(2):
+    for (distance, least, most, skipped), block in zip(sources, blocks):
+        here = (place[0] >= least) & (place[0] <= most)
+        for j in range(skipped, 2):
             end = (j + 1) * half - distance * rows
+            look = partial(visit, distance, block, j - skipped)
             if distance == 0 and j == 1:
-                pl.when(limits[1] < end)(partial(visit, distance, block, 1, 2, j))
+                pl.when(limits[1] < end)(partial(look, 1, 2, j))
             else:
-                pl.when(limits[1] < end)(partial(visit, distance, block, 0, 2, j))
-                pl.when((limits[1] >= end) & (limits[0] < end))(
-                    partial(visit, distance, block, 0, 1, j)
-                )
+                pl.when(here & (limits[1] < end))(partial(look, 0, 2, j))
+                pl.when(here & (limits[1] >= end) & (limits[0] < end))(partial(look, 0, 1, j))
     if last:
         out = refs[-4]
         for h in range(heads):
@@ -419,7 +433,7 @@
         out[...] = accum[...].T.astype(BF16)
 
 
-def attend(distances, last, mine, low, query, blocks, state, length=0, after=()):
+def attend(sources, last, place, low, query, blocks, state, length=0, after=()):
     width, rows = query.shape
     shapes = [struct((width, rows), F32), struct((8, rows), F32), struct((8, rows), F32)]
     scratch = []
@@ -428,37 +442,88 @@
         scratch = [pltpu.VMEM(s.shape, s.dtype) for s in shapes]
         outs = [struct((rows, width), BF16)]
     return call(
-        partial(attend_body, distances, last),
+        partial(attend_body, sources, last),
         outs,
-        [mine],
+        [place],
         [low, query, *blocks, *state],
         after,
         scratch,
         length,
-        blocked=distances[0] > 0,
-    )
-
-
-def rows_body(gain_far, weight_far, *refs):
-    parts, weights = refs[:4], refs[4:7]
-    tokens = refs[7]
-    squares, scaled, again, gain, own_weight, sems = refs[-6:]
-    copies = [
-        pltpu.make_async_copy(weight_far, own_weight, sems.at[0]),
-        pltpu.make_async_copy(gain_far, gain, sems.at[1]),
-    ]
-    for copy in copies:
-        copy.start()
-    summed = sum(
-        mm(w[...], a[...]).astype(BF16).astype(F32) for a, w in zip(parts[1:], weights)
-    )
-    copies[0].wait()
-    summed = summed + mm(own_weight[...], parts[0][...]).astype(BF16).astype(F32)
-    rows = tokens[...].astype(F32) + summed
+        blocked=True,
+    )
+
+
+def begin_body(limit, start, vocab, weight_far, tail, tokens, own, near, near_weight, *refs):
+    half, base, weight, sems = refs[-4:]
+    rows = half.shape[0]
+    whole_rows = (limit - rows) // 16 * 16
+    lower = start[0] == 0
+
+    def fetch(at, count):
+        return pltpu.make_async_copy(
+            vocab.at[pl.ds(at, count), :], half.at[pl.ds(0, count), :], sems.at[0]
+        )
+
+    load = pltpu.make_async_copy(weight_far, weight, sems.at[1])
+    load.start()
+
+    @pl.when(lower)
+    def _():
+        fetch(0, rows).start()
+
+    @pl.when(jnp.logical_not(lower))
+    def _():
+        fetch(rows, whole_rows).start()
+
+    field = tokens[...].astype(F32) + mm(near_weight[...], near[...]).astype(BF16).astype(F32)
+    load.wait()
+    base[...] = field + mm(weight[...], own[...]).astype(BF16).astype(F32)
+
+    @pl.when(lower)
+    def _():
+        fetch(0, rows).wait()
+
+    @pl.when(jnp.logical_not(lower))
+    def _():
+        fetch(rows, whole_rows).wait()
+        if limit > rows + whole_rows:
+            half[whole_rows : whole_rows + 16, :] = tail[...]
+
+
+def begin_rows(start, vocab, weight_far, tokens, own, near, near_weight):
+    limit, width = vocab.shape
+    count = tokens.shape[1]
+    rows = pl.cdiv(limit, 4 * 32) * 64
+    last_tile = (limit - 1) // 16
+    return pl.pallas_call(
+        partial(begin_body, limit),
+        grid=(1,),
+        out_shape=[struct((rows, width), BF16), struct((width, count), F32)],
+        in_specs=[SCALARS, FAR_MEMORY, FAR_MEMORY]
+        + [pl.BlockSpec((16, width), lambda i: (last_tile, 0))]
+        + [whole(a) for a in (tokens, own, near, near_weight)],
+        out_specs=[WHOLE, whole(tokens)],
+        scratch_shapes=[pltpu.VMEM(weight_far.shape, BF16), pltpu.SemaphoreType.DMA((2,))],
+        compiler_params=pltpu.CompilerParams(vmem_limit_bytes=VMEM_LIMIT),
+        cost_estimate=pl.CostEstimate(flops=3 * 10**9, bytes_accessed=0, transcendentals=0),
+    )(start, vocab, weight_far, vocab, tokens, own, near, near_weight)
+
+
+def rows_body(gain_far, base, far, last, far_weight, last_weight, *refs):
+    squares, scaled, again, gain, sem = refs[-5:]
+    copy = pltpu.make_async_copy(gain_far, gain, sem.at[0])
+    copy.start()
+    rows = base[...] + mm(far_weight[...], far[...]).astype(BF16).astype(F32)
+    rows = rows + mm(last_weight[...], last[...]).astype(BF16).astype(F32)
     squares[...] = jnp.sum(rows * rows, axis=0, keepdims=True)
-    copies[1].wait()
+    copy.wait()
     scaled[...] = (rows * (gain[...] * SHRINK)).astype(BF16)
     again[...] = scaled[...]
+
+
+def held_body(limit, start, half, scaled, out):
+    row = start[0] + lax.broadcasted_iota(jnp.int32, out.shape, 0)
+    out[...] = jnp.where(row < limit, mm(half[...], scaled[...]), NEG).astype(BF16)
 
 
 def logits_body(limit, start, vocab, scaled, *refs):
@@ -538,7 +603,18 @@
     mine = tp_index.reshape(1)
     base = seq_index * rows
     requests = request_slots.shape[0]
-
+    prompts = prompt_lengths.shape[0]
+
+    far = swap(tokens, "tp", 2)
+    pieces = [tokens, swap(tokens, "tp", 1), far]
+    gain = norm_gain.reshape(4, columns)
+    weights = [
+        pltpu.with_memory_space_constraint(w, pltpu.HBM) for w in (w_key, w_value, w_query)
+    ]
+    *sums, w_split, w_1, w_2, w_3, far_weights, last_kv, last_query = project(
+        (0, 1), mine, gain, pieces[:2], weights, w_out=w_out
+    )
+    w_parts = [w_split] + [swap(w, "tp", b) for b, w in ((1, w_1), (2, w_2), (3, w_3))]
     powers = np.arange(HD // 2, dtype=np.float32) * np.float32(2.0 / HD)
     inverse = (np.float32(10000.0) ** -powers).astype(np.float32)[:, None]
     cosine, sine, low, request_low = call(
@@ -550,32 +626,25 @@
             struct((1, requests), jnp.int32),
         ],
         [base.reshape(1), prompt_lengths],
-        [segment_ids[None, :], jnp.asarray(inverse)],
+        pinned([segment_ids[None, :], jnp.asarray(inverse)]),
+        sums[1:2],
         blocked=True,
     )
-    far = swap(tokens, "tp", 2)
-    pieces = [tokens, swap(tokens, "tp", 1), far]
-    gain = norm_gain.reshape(4, columns)
-    weights = [
-        pltpu.with_memory_space_constraint(w, pltpu.HBM) for w in (w_key, w_value, w_query)
-    ]
-    *sums, w_split, w_1, w_2, w_3, far_weights, last_kv, last_query = project(
-        (0, 1), mine, gain, pieces[:2], weights, after=(cosine,), w_out=w_out
-    )
-    w_parts = [w_split] + [swap(w, "tp", b) for b, w in ((1, w_1), (2, w_2), (3, w_3))]
-    (relayed,) = call(copy_body, [struct(far.shape, BF16)], [], [far], sums[1:])
-    pieces.append(swap(relayed, "tp", 1))
+    last_gain = final_gain[:, None]
+    relayed, far = call(
+        twice_body, [struct(far.shape, BF16)] * 2, [], [far], (sums[1], cosine, last_gain)
+    )
+    pieces = pieces[:2] + [far, swap(relayed, "tp", 1)]
 
     asked = request_slots[None, :]
     inside = asked - base
     (own_tokens,) = call(
-        pick_body, [struct((columns, requests), BF16)], [base.reshape(1)], [asked, tokens],
+        pick_body, [struct((columns, requests), BF16)], [base.reshape(1)], pinned([asked, tokens]),
         blocked=True,
     )
     all_tokens = [own_tokens]
-    last_gain = final_gain[:, None]
     *kv_sums, query_sums, query_squares = project(
-        (2,), mine, gain, pieces[2:3], [far_weights], sums, None, (last_gain,), length=10
+        (2,), mine, gain, pieces[2:3], [far_weights], sums, None, (), length=10
     )
     ending = (base.reshape(1), cosine, sine, asked)
     query, own_query = project(
@@ -592,7 +661,7 @@
             sums[1:2] if len(all_tokens) == 1 else (own_query,),
         )
         bit //= 2
-    (kv,) = project(
+    asked_kv, own_kv, kv, kv_half = project(
         (3,),
         mine,
         gain,
@@ -608,44 +677,72 @@
     kv_cache = jnp.transpose(kv.reshape(heads, 2 * HD, rows), (0, 2, 1))
     behind = shifted(kv, "seq", 1)
 
+    last_start = n_seq - span - 1
+    ends = jnp.cumsum(prompt_lengths)
+    reach = (ends - 1) // rows - (ends - prompt_lengths) // rows
+    longest = jnp.max(jnp.where(jnp.arange(prompts) < prompts - 1, reach, 0))
+    sources = [(0, 0, n_seq, 0), (1, 0, n_seq, 0)]
+    blocks = [own_kv, behind]
+    for by in range(2, span + 1):
+        early = [(i, i + by) for i in range(last_start + 1 - by)]
+        late = [(i, i + by) for i in range(last_start, n_seq - by)]
+        sources.append((by, 0, last_start, 0))
+        blocks.append(
+            lax.cond(
+                longest >= by,
+                lambda array, pairs=early: lax.ppermute(array, "seq", pairs),
+                jnp.zeros_like,
+                kv,
+            )
+        )
+        from_half = 1 if by == span else 0
+        sources.append((by, last_start + by, n_seq, from_half))
+        blocks.append(lax.ppermute(kv_half if from_half else kv, "seq", late))
+    halo = tuple(blocks[2:4])
+
     (mixed,) = call(
         partial(request_body, len(asking)),
         [struct((width + LEVEL_ROWS, requests), BF16)],
         [],
-        [request_low, inside, kv, *asking],
-        all_tokens[3:4],
-    )
-    own_state = attend((0,), False, mine, low, query, (kv,), (), length=10, after=(mixed,))
-
-    afters = [own_state[1:2], all_tokens[-1:] if n_seq > 8 else (), w_parts[2:3]]
-    stages = [mixed]
+        [request_low, inside, asked_kv, *asking],
+        all_tokens[2:3],
+    )
+    afters = [all_tokens[3:4], (), w_parts[2:3] + [all_tokens[-1]]]
     bit = 1
     while bit < n_seq:
         flip = ((seq_index & bit) > 0).astype(jnp.int32).reshape(1)
         after = afters.pop(0) if afters else ()
+        other = swap(mixed, "seq", bit)
         bit *= 2
         kept_rows = width + LEVEL_ROWS if bit < n_seq else width
-        other = swap(stages[-1], "seq", bit // 2)
-        stages.append(combine(flip, stages[-1], other, kept_rows, after))
-    request_mixed = spread(stages[-1])
-    (later_kv,) = call(copy_body, [struct(kv.shape, BF16)], [], [kv], stages[-1:])
+        mixed = combine(flip, mixed, other, kept_rows, after)
+    _, near_mixed, far_mixed, last_mixed = spread(mixed)
 
     core = tp_index & 1
     side = tp_index >> 1
+    vocab = pltpu.with_memory_space_constraint(w_vocab.T, pltpu.HBM)
+    limit = vocab.shape[0]
+    vocab_rows = pl.cdiv(limit, 4 * 32) * 64
+    away = (vocab_rows * (1 - core)).reshape(1)
+    far_gain, own_weight = pinned([last_gain, w_split])
+    held, field = begin_rows(
+        away, vocab, own_weight, all_tokens[-1], mixed, near_mixed, w_parts[1]
+    )
     squares, scaled, again = call(
         rows_body,
         [struct((1, requests), F32)] + [struct(own_tokens.shape, BF16)] * 2,
         [],
-        [*request_mixed, *w_parts[1:], all_tokens[-1]],
-        scratch=[
-            pltpu.VMEM((columns, 1), F32),
-            pltpu.VMEM((columns, width), BF16),
-            pltpu.SemaphoreType.DMA((2,)),
-        ],
-        far=pinned([last_gain, w_split]),
-    )
-    vocab = pltpu.with_memory_space_constraint(w_vocab.T, pltpu.HBM)
-    sent = half_logits((2 * (1 - core)).reshape(1), vocab, scaled)
+        [field, far_mixed, last_mixed, *w_parts[2:]],
+        scratch=[pltpu.VMEM((columns, 1), F32), pltpu.SemaphoreType.DMA((1,))],
+        far=[far_gain],
+        after=halo[1:],
+    )
+    (sent,) = call(
+        partial(held_body, limit),
+        [struct((vocab_rows, requests), BF16)],
+        [away],
+        [held, scaled],
+    )
     kept = half_logits((2 * core).reshape(1), vocab, again, (sent,))
     quarter = kept.shape[0] // 2
     sent, kept = call(
@@ -654,13 +751,13 @@
         [side.reshape(1)],
         [kept, swap(sent, "tp", 1)],
     )
-    blocks = [behind] + [shifted(later_kv, "seq", by) for by in range(2, span + 1)]
-    distances = list(range(1, span + 1))
-    state = own_state
-    while distances:
-        last = len(distances) <= 3
-        state = attend(distances[:3], last, mine, low, query, blocks[:3], state, 30)
-        distances, blocks = distances[3:], blocks[3:]
+    state = ()
+    while sources:
+        last = len(sources) <= 4
+        state = attend(
+            sources[:4], last, seq_index.reshape(1), low, query, blocks[:4], state, 30
+        )
+        sources, blocks = sources[4:], blocks[4:]
     (best,) = call(
         top_body, [struct((1, requests), F32)], [], [kept, swap(sent, "tp", 2)], state[:1]
     )

time: 120 us -> 105 us (0.88)
  local copies, waits for them, and re-layouts: 12.2 us -> 4.22 us
  Pallas kernels: 33.8 us -> 29.3 us
  starting transfers between devices: 42.6 us -> 39.6 us
  waiting for transfers between devices: 26.1 us -> 24 us
  other arithmetic: 0.56 us -> 2.07 us
    unnamed x56 -> x28, local copies, waits for them, and re-layouts: 10.6 us -> 1.71 us
    ppermute x25, waiting for transfers between devices: 26 us -> 18.9 us  [swap(): return lax.ppermute(array, axis, [(i, i ^ bit) for i in range(count)])]
    ppermute x4 -> x3, waiting for transfers between devices: 0.01 us -> 5 us  [shifted(): return lax.ppermute(array, axis, pairs)]
    pallas_call x21 -> x20, Pallas kernels: 27.8 us -> 23.8 us  [call(): pl.pallas_call(body, grid=(1,) if blocked else (), out_shape=outs, in_spe...]
    pallas_call x2 -> x1, Pallas kernels: 6.01 us -> 2.72 us  [half_logits(): pl.pallas_call(partial(logits_body, limit), grid_spec=pltpu.PrefetchScala...]
    pallas_call x0 -> x1, Pallas kernels: none -> 2.77 us  [begin_rows(): pl.pallas_call(partial(begin_body, limit), grid=(1,), out_shape=[struct((...]
    ppermute x4 -> x3, starting transfers between devices: 9.36 us -> 7.2 us  [shifted(): return lax.ppermute(array, axis, pairs)]
    ppermute x25, starting transfers between devices: 33.3 us -> 31.7 us  [swap(): return lax.ppermute(array, axis, [(i, i ^ bit) for i in range(count)])]
  transfers between devices with their start and end apart: 29 -> 29, of which waited for: 11 -> 12; matrix products, arithmetic and copies ran while one was open for 3% -> 6% of each run, Pallas kernels for 28% -> 28%
where the time goes in v3:
time: 105 us; the launch traced here: 104 us
  starting transfers between devices  39.6 us (38%)
  Pallas kernels  29.3 us (28%)
  waiting for transfers between devices  24 us (23%)
  local copies, waits for them, and re-layouts  4.22 us (4%)
  matrix products  3.4 us (3%)
  other arithmetic  2.07 us (2%)
  between operations  1.65 us (2%)
    ppermute x25, starting transfers between devices, swap(): return lax.ppermute(array, axis, [(i, i ^ bit) for i in range(count)])  31.7 us
    pallas_call x20, Pallas kernels, call(): pl.pallas_call(body, grid=(1,) if blocked else (), out_shape=outs, in_spe...  23.8 us
    ppermute x25, waiting for transfers between devices, swap(): return lax.ppermute(array, axis, [(i, i ^ bit) for i in range(count)])  18.9 us
    ppermute x3, starting transfers between devices, shifted(): return lax.ppermute(array, axis, pairs)  7.2 us
    ppermute x3, waiting for transfers between devices, shifted(): return lax.ppermute(array, axis, pairs)  5 us
    dot_general x4, matrix products, mm_last(): lax.dot_general(a, b, (((1,), (1,)), ((), ())), preferred_element_type=F32)  3.4 us
    pallas_call x1, Pallas kernels, begin_rows(): pl.pallas_call(partial(begin_body, limit), grid=(1,), out_shape=[struct((...  2.77 us
    pallas_call x1, Pallas kernels, half_logits(): pl.pallas_call(partial(logits_body, limit), grid_spec=pltpu.PrefetchScala...  2.72 us
  transfers between devices with their start and end apart: 29, of which 12 were waited for; matrix products, arithmetic and copies ran while one was open for 6% of the time, Pallas kernels for 28%

profile of v3, /device:TPU:0, one launch (start us, length us, event | category | flops | bytes accessed | tf_op | source)
XLA Modules:
  0.0 104.3 jit_solution(13528693405657484030)
XLA Ops:
  1.2 2.6 %collective-permute-start.2 = (bf16[512,768]{1,0:T(8,128)(2,1)}, bf16[512,768]{1,0:T(8,128)(2,1)S(1)}, u32[]{:S(2)}, u32[]{:S(2)}) collective-permute-start(bf16[512,768]{1,0:T(8,128)(2,1)} %tokens.1), channel_id=1, source_target_pairs={{0,2},{1,3},{2,0},{3,1},{4,6},{5,7},{6,4},{7,5},{8,10},{9,11},{10,... | collective-permute-start | bytes 2359304 | tf_op jit(solution)/shard_map/ppermute | solution.py:65
  5.3 2.7 %collective-permute-start.12 = (bf16[768,128]{1,0:T(8,128)(2,1)S(1)}, bf16[768,128]{1,0:T(8,128)(2,1)}, u32[]{:S(2)}, u32[]{:S(2)}) collective-permute-start(bf16[768,128]{1,0:T(8,128)(2,1)S(1)} %shard_map.154.first), channel_id=1, source_target_pairs={{0,16},{4,20},{8,24},{12,28},{16,0},{20,4},{24,8},{28,12},{1,17},{... | collective-permute-start | bytes 589832 | tf_op jit(solution)/shard_map/ppermute | solution.py:65
  11.9 6.4 %shard_map.147 = (f32[512,1152]{1,0:T(8,128)S(1)}, f32[512,1]{1,0:T(8,128)S(1)}, bf16[768,384]{1,0:T(8,128)(2,1)S(1)}, bf16[768,384]{1,0:T(8,128)(2,1)}, bf16[76...) custom-call(s32[1]{0:T(128)} %bitcast.refs_0_, ...), custom_call_target="tpu_custom_call" | custom-call | tf_op jit(solution)/shard_map/pallas_call | solution.py:38
  19.6 2.5 %collective-permute-done.2.source = bf16[512,768]{1,0:T(8,128)(2,1)S(1)} collective-permute-done((bf16[512,768]{1,0:T(8,128)(2,1)}, bf16[512,768]{1,0:T(8,128)(2,1)S(1)}, u32[]{:S(2)}, u32[]{:S(2)}) %collective-permute-start.2) | collective-permute-done | bytes 786464 | tf_op jit(solution)/shard_map/ppermute | solution.py:65
  22.3 1.8 %collective-permute-start.9 = (bf16[768,384]{1,0:T(8,128)(2,1)}, bf16[768,384]{1,0:T(8,128)(2,1)S(1)}, u32[]{:S(2)}, u32[]{:S(2)}) collective-permute-start(bf16[768,384]{1,0:T(8,128)(2,1)} %get-tuple-element.61), channel_id=1, source_target_pairs={{0,2},{1,3},{2,0},{3,1},{4,6},{5,7},{6,4},{7,5},{8,10},{9,11},{10,... | collective-permute-start | bytes 1769480 | tf_op jit(solution)/shard_map/ppermute | solution.py:65
  32.5 2.2 %collective-permute-start.14 = (bf16[768,128]{1,0:T(8,128)(2,1)S(1)}, bf16[768,128]{1,0:T(8,128)(2,1)S(1)}, u32[]{:S(2)}, u32[]{:S(2)}) collective-permute-start(bf16[768,128]{1,0:T(8,128)(2,1)S(1)} %shard_map.156.first.refs_3_), channel_id=1, source_target_pairs={{0,4},{4,0},{8,12},{12,8},{16,20},{20,16},{24,28},{28,24},{1,5},{5... | collective-permute-start | bytes 589832 | tf_op jit(solution)/shard_map/ppermute | solution.py:65
  34.7 2.1 %shard_map.152 = (bf16[768,512]{1,0:T(8,128)(2,1)S(1)}, bf16[768,512]{1,0:T(8,128)(2,1)S(1)}, bf16[768,512]{1,0:T(8,128)(2,1)}, bf16[768,256]{1,0:T(8,128)(2,1)S(1)}) custom-call(s32[1]{0:T(128)} %bitcast.refs_0_, s32[1]{0:T(128)} %bitcast.1.base.refs_1_, bf16[2,768,384]{2,1,0:T(8,128)(2,1)S(1)} %get-tuple-element.40.refs_2_, ...), custom_call_target="tpu_custom_call" | custom-call | flops 10000000000 | tf_op jit(solution)/shard_map/pallas_call | solution.py:38
  36.8 2.2 %collective-permute-done.16.refs_2_ = bf16[384,128]{1,0:T(8,128)(2,1)S(1)} collective-permute-done((bf16[384,128]{1,0:T(8,128)(2,1)S(1)}, bf16[384,128]{1,0:T(8,128)(2,1)S(1)}, u32[]{:S(2)}, u32[]{:S(2)}) %collective-permute-start.16) | collective-permute-done | bytes 98336 | tf_op jit(solution)/shard_map/ppermute | solution.py:71
  41.1 3.8 %collective-permute-done.17.other = bf16[400,128]{1,0:T(8,128)(2,1)S(1)} collective-permute-done((bf16[400,128]{1,0:T(8,128)(2,1)S(1)}, bf16[400,128]{1,0:T(8,128)(2,1)S(1)}, u32[]{:S(2)}, u32[]{:S(2)}) %collective-permute-start.17) | collective-permute-done | bytes 102432 | tf_op jit(solution)/shard_map/ppermute | solution.py:65
  45.0 1.8 %collective-permute-start.18 = (bf16[400,128]{1,0:T(8,128)(2,1)S(1)}, bf16[400,128]{1,0:T(8,128)(2,1)S(1)}, u32[]{:S(2)}, u32[]{:S(2)}) collective-permute-start(bf16[400,128]{1,0:T(8,128)(2,1)S(1)} %shard_map.159.own), channel_id=1, source_target_pairs={{0,8},{4,12},{8,0},{12,4},{16,24},{20,28},{24,16},{28,20},{1,9},{5... | collective-permute-start | bytes 307208 | tf_op jit(solution)/shard_map/ppermute | solution.py:65
  46.8 3.0 %collective-permute-done.18.other = bf16[400,128]{1,0:T(8,128)(2,1)S(1)} collective-permute-done((bf16[400,128]{1,0:T(8,128)(2,1)S(1)}, bf16[400,128]{1,0:T(8,128)(2,1)S(1)}, u32[]{:S(2)}, u32[]{:S(2)}) %collective-permute-start.18) | collective-permute-done | bytes 102432 | tf_op jit(solution)/shard_map/ppermute | solution.py:65
  49.8 3.0 %collective-permute-start.19 = (bf16[400,128]{1,0:T(8,128)(2,1)S(1)}, bf16[400,128]{1,0:T(8,128)(2,1)S(1)}, u32[]{:S(2)}, u32[]{:S(2)}) collective-permute-start(bf16[400,128]{1,0:T(8,128)(2,1)S(1)} %shard_map.160.own), channel_id=1, source_target_pairs={{0,16},{4,20},{8,24},{12,28},{16,0},{20,4},{24,8},{28,12},{1,17},{... | collective-permute-start | bytes 307208 | tf_op jit(solution)/shard_map/ppermute | solution.py:65
  53.5 2.0 %collective-permute-done.19.other = bf16[400,128]{1,0:T(8,128)(2,1)S(1)} collective-permute-done((bf16[400,128]{1,0:T(8,128)(2,1)S(1)}, bf16[400,128]{1,0:T(8,128)(2,1)S(1)}, u32[]{:S(2)}, u32[]{:S(2)}) %collective-permute-start.19) | collective-permute-done | bytes 102432 | tf_op jit(solution)/shard_map/ppermute | solution.py:65
  56.1 4.6 %collective-permute-start.4 = (bf16[768,512]{1,0:T(8,128)(2,1)}, bf16[768,512]{1,0:T(8,128)(2,1)}, u32[]{:S(2)}, u32[]{:S(2)}) collective-permute-start(bf16[768,512]{1,0:T(8,128)(2,1)} %get-tuple-element.54), channel_id=1, source_target_pairs={{0,4},{4,8},{8,12},{12,16},{16,20},{20,24},{24,28},{1,5},{5,9},{9,... | collective-permute-start | bytes 2359304 | tf_op jit(solution)/shard_map/ppermute | solution.py:71
  61.0 2.8 %shard_map.162 = (bf16[2048,768]{1,0:T(8,128)(2,1)S(1)}, f32[768,128]{1,0:T(8,128)S(1)}) custom-call(s32[1]{0:T(128)} %bitcast.12.start, bf16[4008,768]{1,0:T(8,128)(2,1)} %bitcast.48, bf16[768,384]{1,0:T(8,128)(2,1)} %copy-done.2, bf16[4008,768]{1,0:T(8,128)(2,1)} %bitcast.49, bf16[768,128]{1,0:T(8,128)(2,1)S(1)} %shard_map.157.refs_0_.refs_1_.tokens, ...), custom_call_target="tpu_custom_call" | custom-call | flops 3000000000 | tf_op jit(solution)/shard_map/pallas_call | solution.py:498
  69.2 2.7 %shard_map.165.kept = bf16[2048,128]{1,0:T(8,128)(2,1)S(1)} custom-call(s32[1]{0:T(128)} %bitcast.10.start, bf16[4008,768]{1,0:T(8,128)(2,1)} %bitcast.50, bf16[768,128]{1,0:T(8,128)(2,1)S(1)} %get-tuple-element.66.scaled, bf16[2048,128]{1,0:T(8,128)(2,1)S(1)} %shard_map.164.refs_0_), custom_call_target="tpu_custom_call" | custom-call | tf_op jit(solution)/shard_map/pallas_call | solution.py:540
  73.1 1.7 %collective-permute-start.24 = (bf16[1024,128]{1,0:T(8,128)(2,1)S(1)}, bf16[1024,128]{1,0:T(8,128)(2,1)S(1)}, u32[]{:S(2)}, u32[]{:S(2)}) collective-permute-start(bf16[1024,128]{1,0:T(8,128)(2,1)S(1)} %get-tuple-element.70), channel_id=1, source_target_pairs={{0,2},{1,3},{2,0},{3,1},{4,6},{5,7},{6,4},{7,5},{8,10},{9,11},{10,... | collective-permute-start | bytes 786440 | tf_op jit(solution)/shard_map/ppermute | solution.py:65
  74.8 2.8 %collective-permute-done.4.refs_1_ = bf16[768,512]{1,0:T(8,128)(2,1)} collective-permute-done((bf16[768,512]{1,0:T(8,128)(2,1)}, bf16[768,512]{1,0:T(8,128)(2,1)}, u32[]{:S(2)}, u32[]{:S(2)}) %collective-permute-start.4) | collective-permute-done | bytes 786464 | tf_op jit(solution)/shard_map/ppermute | solution.py:71
  77.6 3.8 %shard_map.153.refs_0_ = bf16[512,384]{1,0:T(8,128)(2,1)S(1)} custom-call(s32[1]{0:T(128)} %bitcast.6.place, s32[1,512]{1,0:T(1,128)S(1)} %get-tuple-element.55.low, bf16[384,512]{1,0:T(8,128)(2,1)S(1)} %copy-done.11, bf16[768,512]{1,0:T(8,128)(2,1)S(1)} %copy-done.13, bf16[768,512]{1,0:T(8,128)(2,1)} %collective-permute-done.4.refs_1_, ...), custom_call_target="tpu_custom_call" | custom-call | flops 30000001024 | tf_op jit(solution)/shard_map/pallas_call | solution.py:38
  81.4 1.7 %collective-permute-start.8 = (bf16[512,384]{1,0:T(8,128)(2,1)S(1)}, bf16[512,384]{1,0:T(8,128)(2,1)S(1)}, u32[]{:S(2)}, u32[]{:S(2)}) collective-permute-start(bf16[512,384]{1,0:T(8,128)(2,1)S(1)} %shard_map.153.refs_0_), channel_id=1, source_target_pairs={{0,2},{1,3},{2,0},{3,1},{4,6},{5,7},{6,4},{7,5},{8,10},{9,11},{10,... | collective-permute-start | bytes 1179656 | tf_op jit(solution)/shard_map/ppermute | solution.py:65
  83.3 3.2 %collective-permute-start.25 = (f32[1,128]{1,0:T(1,128)S(1)}, f32[1,128]{1,0:T(1,128)S(1)}, u32[]{:S(2)}, u32[]{:S(2)}) collective-permute-start(f32[1,128]{1,0:T(1,128)S(1)} %shard_map.167), channel_id=1, source_target_pairs={{0,4},{4,0},{8,12},{12,8},{16,20},{20,16},{24,28},{28,24},{1,5},{5... | collective-permute-start | bytes 1544 | tf_op jit(solution)/shard_map/ppermute | solution.py:65
  88.1 3.3 %collective-permute-start.26 = (f32[1,128]{1,0:T(1,128)S(1)}, f32[1,128]{1,0:T(1,128)S(1)}, u32[]{:S(2)}, u32[]{:S(2)}) collective-permute-start(f32[1,128]{1,0:T(1,128)S(1)} %max.20), channel_id=1, source_target_pairs={{0,8},{4,12},{8,0},{12,4},{16,24},{20,28},{24,16},{28,20},{1,9},{5... | collective-permute-start | bytes 1544 | tf_op jit(solution)/shard_map/ppermute | solution.py:65
  92.9 2.6 %collective-permute-start.27 = (f32[1,128]{1,0:T(1,128)S(1)}, f32[1,128]{1,0:T(1,128)S(1)}, u32[]{:S(2)}, u32[]{:S(2)}) collective-permute-start(f32[1,128]{1,0:T(1,128)S(1)} %max.21), channel_id=1, source_target_pairs={{0,16},{4,20},{8,24},{12,28},{16,0},{20,4},{24,8},{28,12},{1,17},{... | collective-permute-start | bytes 1544 | tf_op jit(solution)/shard_map/ppermute | solution.py:65
  98.6 2.4 %collective-permute-done.28 = f32[2,128]{1,0:T(2,128)S(1)} collective-permute-done((f32[2,128]{1,0:T(2,128)S(1)}, f32[2,128]{1,0:T(2,128)S(1)}, u32[]{:S(2)}, u32[]{:S(2)}) %collective-permute-start.28) | collective-permute-done | bytes 1056 | tf_op jit(solution)/shard_map/ppermute | solution.py:65
  (101 shorter events, 36.1 us)
Async XLA Ops:
  0.6 9.6 %collective-permute-start.1 = (bf16[512,768]{1,0:T(8,128)(2,1)}, bf16[512,768]{1,0:T(8,128)(2,1)S(1)}, u32[]{:S(2)}, u32[]{:S(2)}) collective-permute-start(bf16[512,768]{1,0:T(8,128)(2,1)} %tokens.1), channel_id=1, source_target_pairs={{0,1},{1,0},{2,3},{3,2},{4,5},{5,4},{6,7},{7,6},{8,9},{9,8},{10,11... | collective-permute-start | bytes 2359304 | tf_op jit(solution)/shard_map/ppermute | solution.py:65
  1.2 20.9 %collective-permute-start.2 = (bf16[512,768]{1,0:T(8,128)(2,1)}, bf16[512,768]{1,0:T(8,128)(2,1)S(1)}, u32[]{:S(2)}, u32[]{:S(2)}) collective-permute-start(bf16[512,768]{1,0:T(8,128)(2,1)} %tokens.1), channel_id=1, source_target_pairs={{0,2},{1,3},{2,0},{3,1},{4,6},{5,7},{6,4},{7,5},{8,10},{9,11},{10,... | collective-permute-start | bytes 2359304 | tf_op jit(solution)/shard_map/ppermute | solution.py:65
  5.3 18.9 %collective-permute-start.12 = (bf16[768,128]{1,0:T(8,128)(2,1)S(1)}, bf16[768,128]{1,0:T(8,128)(2,1)}, u32[]{:S(2)}, u32[]{:S(2)}) collective-permute-start(bf16[768,128]{1,0:T(8,128)(2,1)S(1)} %shard_map.154.first), channel_id=1, source_target_pairs={{0,16},{4,20},{8,24},{12,28},{16,0},{20,4},{24,8},{28,12},{1,17},{... | collective-permute-start | bytes 589832 | tf_op jit(solution)/shard_map/ppermute | solution.py:65
  22.2 6.1 %collective-permute-start.3 = (bf16[512,768]{1,0:T(8,128)(2,1)S(1)}, bf16[512,768]{1,0:T(8,128)(2,1)S(1)}, u32[]{:S(2)}, u32[]{:S(2)}) collective-permute-start(bf16[512,768]{1,0:T(8,128)(2,1)S(1)} %get-tuple-element.43), channel_id=1, source_target_pairs={{0,1},{1,0},{2,3},{3,2},{4,5},{5,4},{6,7},{7,6},{8,9},{9,8},{10,11... | collective-permute-start | bytes 2359304 | tf_op jit(solution)/shard_map/ppermute | solution.py:65
  22.3 31.2 %collective-permute-start.9 = (bf16[768,384]{1,0:T(8,128)(2,1)}, bf16[768,384]{1,0:T(8,128)(2,1)S(1)}, u32[]{:S(2)}, u32[]{:S(2)}) collective-permute-start(bf16[768,384]{1,0:T(8,128)(2,1)} %get-tuple-element.61), channel_id=1, source_target_pairs={{0,2},{1,3},{2,0},{3,1},{4,6},{5,7},{6,4},{7,5},{8,10},{9,11},{10,... | collective-permute-start | bytes 1769480 | tf_op jit(solution)/shard_map/ppermute | solution.py:65
  24.1 32.0 %collective-permute-start.7 = (bf16[768,384]{1,0:T(8,128)(2,1)}, bf16[768,384]{1,0:T(8,128)(2,1)S(1)}, u32[]{:S(2)}, u32[]{:S(2)}) collective-permute-start(bf16[768,384]{1,0:T(8,128)(2,1)} %get-tuple-element.60), channel_id=1, source_target_pairs={{0,1},{1,0},{2,3},{3,2},{4,5},{5,4},{6,7},{7,6},{8,9},{9,8},{10,11... | collective-permute-start | bytes 1769480 | tf_op jit(solution)/shard_map/ppermute | solution.py:65
  25.3 7.2 %collective-permute-start.13 = (bf16[768,128]{1,0:T(8,128)(2,1)S(1)}, bf16[768,128]{1,0:T(8,128)(2,1)S(1)}, u32[]{:S(2)}, u32[]{:S(2)}) collective-permute-start(bf16[768,128]{1,0:T(8,128)(2,1)S(1)} %shard_map.155.first), channel_id=1, source_target_pairs={{0,8},{4,12},{8,0},{12,4},{16,24},{20,28},{24,16},{28,20},{1,9},{5... | collective-permute-start | bytes 589832 | tf_op jit(solution)/shard_map/ppermute | solution.py:65
  29.3 7.5 %collective-permute-start.15 = (bf16[384,128]{1,0:T(8,128)(2,1)S(1)}, bf16[384,128]{1,0:T(8,128)(2,1)S(1)}, u32[]{:S(2)}, u32[]{:S(2)}) collective-permute-start(bf16[384,128]{1,0:T(8,128)(2,1)S(1)} %get-tuple-element.53.refs_10_.refs_0_), channel_id=1, source_target_pairs={{4,0},{8,4},{12,8},{16,12},{20,16},{24,20},{28,24},{5,1},{9,5},{13... | collective-permute-start | bytes 294920 | tf_op jit(solution)/shard_map/ppermute | solution.py:71
  30.6 8.4 %collective-permute-start.16 = (bf16[384,128]{1,0:T(8,128)(2,1)S(1)}, bf16[384,128]{1,0:T(8,128)(2,1)S(1)}, u32[]{:S(2)}, u32[]{:S(2)}) collective-permute-start(bf16[384,128]{1,0:T(8,128)(2,1)S(1)} %get-tuple-element.53.refs_10_.refs_0_), channel_id=1, source_target_pairs={{8,0},{12,4},{16,8},{20,12},{24,16},{28,20},{9,1},{13,5},{17,9},{2... | collective-permute-start | bytes 294920 | tf_op jit(solution)/shard_map/ppermute | solution.py:71
  32.5 8.5 %collective-permute-start.14 = (bf16[768,128]{1,0:T(8,128)(2,1)S(1)}, bf16[768,128]{1,0:T(8,128)(2,1)S(1)}, u32[]{:S(2)}, u32[]{:S(2)}) collective-permute-start(bf16[768,128]{1,0:T(8,128)(2,1)S(1)} %shard_map.156.first.refs_3_), channel_id=1, source_target_pairs={{0,4},{4,0},{8,12},{12,8},{16,20},{20,16},{24,28},{28,24},{1,5},{5... | collective-permute-start | bytes 589832 | tf_op jit(solution)/shard_map/ppermute | solution.py:65
  40.2 4.7 %collective-permute-start.17 = (bf16[400,128]{1,0:T(8,128)(2,1)S(1)}, bf16[400,128]{1,0:T(8,128)(2,1)S(1)}, u32[]{:S(2)}, u32[]{:S(2)}) collective-permute-start(bf16[400,128]{1,0:T(8,128)(2,1)S(1)} %shard_map.158.own), channel_id=1, source_target_pairs={{0,4},{4,0},{8,12},{12,8},{16,20},{20,16},{24,28},{28,24},{1,5},{5... | collective-permute-start | bytes 307208 | tf_op jit(solution)/shard_map/ppermute | solution.py:65
  41.0 22.7 %collective-permute-start.11 = (bf16[768,384]{1,0:T(8,128)(2,1)}, bf16[768,384]{1,0:T(8,128)(2,1)S(1)}, u32[]{:S(2)}, u32[]{:S(2)}) collective-permute-start(bf16[768,384]{1,0:T(8,128)(2,1)} %get-tuple-element.62), channel_id=1, source_target_pairs={{0,3},{1,2},{2,1},{3,0},{4,7},{5,6},{6,5},{7,4},{8,11},{9,10},{10,... | collective-permute-start | bytes 1769480 | tf_op jit(solution)/shard_map/ppermute | solution.py:65
  45.0 4.7 %collective-permute-start.18 = (bf16[400,128]{1,0:T(8,128)(2,1)S(1)}, bf16[400,128]{1,0:T(8,128)(2,1)S(1)}, u32[]{:S(2)}, u32[]{:S(2)}) collective-permute-start(bf16[400,128]{1,0:T(8,128)(2,1)S(1)} %shard_map.159.own), channel_id=1, source_target_pairs={{0,8},{4,12},{8,0},{12,4},{16,24},{20,28},{24,16},{28,20},{1,9},{5... | collective-permute-start | bytes 307208 | tf_op jit(solution)/shard_map/ppermute | solution.py:65
  49.8 5.7 %collective-permute-start.19 = (bf16[400,128]{1,0:T(8,128)(2,1)S(1)}, bf16[400,128]{1,0:T(8,128)(2,1)S(1)}, u32[]{:S(2)}, u32[]{:S(2)}) collective-permute-start(bf16[400,128]{1,0:T(8,128)(2,1)S(1)} %shard_map.160.own), channel_id=1, source_target_pairs={{0,16},{4,20},{8,24},{12,28},{16,0},{20,4},{24,8},{28,12},{1,17},{... | collective-permute-start | bytes 307208 | tf_op jit(solution)/shard_map/ppermute | solution.py:65
  52.8 10.9 %collective-permute-start.5 = (bf16[768,256]{1,0:T(8,128)(2,1)}, bf16[768,256]{1,0:T(8,128)(2,1)S(1)}, u32[]{:S(2)}, u32[]{:S(2)}) collective-permute-start(bf16[768,256]{1,0:T(8,128)(2,1)} %copy-done.9), channel_id=1, source_target_pairs={{20,28},{21,29},{22,30},{23,31}} | collective-permute-start | bytes 1179656 | tf_op jit(solution)/shard_map/ppermute | solution.py:700
  55.6 5.2 %collective-permute-start.21 = (bf16[384,128]{1,0:T(8,128)(2,1)S(1)}, bf16[384,128]{1,0:T(8,128)(2,1)S(1)}, u32[]{:S(2)}, u32[]{:S(2)}) collective-permute-start(bf16[384,128]{1,0:T(8,128)(2,1)S(1)} %shard_map.161.own), channel_id=1, source_target_pairs={{0,2},{1,3},{2,0},{3,1},{4,6},{5,7},{6,4},{7,5},{8,10},{9,11},{10,... | collective-permute-start | bytes 294920 | tf_op jit(solution)/shard_map/ppermute | solution.py:65
  56.1 4.9 %collective-permute-start.20 = (bf16[384,128]{1,0:T(8,128)(2,1)S(1)}, bf16[384,128]{1,0:T(8,128)(2,1)S(1)}, u32[]{:S(2)}, u32[]{:S(2)}) collective-permute-start(bf16[384,128]{1,0:T(8,128)(2,1)S(1)} %shard_map.161.own), channel_id=1, source_target_pairs={{0,1},{1,0},{2,3},{3,2},{4,5},{5,4},{6,7},{7,6},{8,9},{9,8},{10,11... | collective-permute-start | bytes 294920 | tf_op jit(solution)/shard_map/ppermute | solution.py:65
  56.1 21.5 %collective-permute-start.4 = (bf16[768,512]{1,0:T(8,128)(2,1)}, bf16[768,512]{1,0:T(8,128)(2,1)}, u32[]{:S(2)}, u32[]{:S(2)}) collective-permute-start(bf16[768,512]{1,0:T(8,128)(2,1)} %get-tuple-element.54), channel_id=1, source_target_pairs={{0,4},{4,8},{8,12},{12,16},{16,20},{20,24},{24,28},{1,5},{5,9},{9,... | collective-permute-start | bytes 2359304 | tf_op jit(solution)/shard_map/ppermute | solution.py:71
  66.2 5.7 %collective-permute-start.23 = (bf16[2048,128]{1,0:T(8,128)(2,1)S(1)}, bf16[2048,128]{1,0:T(8,128)(2,1)}, u32[]{:S(2)}, u32[]{:S(2)}) collective-permute-start(bf16[2048,128]{1,0:T(8,128)(2,1)S(1)} %shard_map.164.refs_0_), channel_id=1, source_target_pairs={{0,1},{1,0},{2,3},{3,2},{4,5},{5,4},{6,7},{7,6},{8,9},{9,8},{10,11... | collective-permute-start | bytes 1572872 | tf_op jit(solution)/shard_map/ppermute | solution.py:65
  73.1 10.1 %collective-permute-start.24 = (bf16[1024,128]{1,0:T(8,128)(2,1)S(1)}, bf16[1024,128]{1,0:T(8,128)(2,1)S(1)}, u32[]{:S(2)}, u32[]{:S(2)}) collective-permute-start(bf16[1024,128]{1,0:T(8,128)(2,1)S(1)} %get-tuple-element.70), channel_id=1, source_target_pairs={{0,2},{1,3},{2,0},{3,1},{4,6},{5,7},{6,4},{7,5},{8,10},{9,11},{10,... | collective-permute-start | bytes 786440 | tf_op jit(solution)/shard_map/ppermute | solution.py:65
  81.4 15.9 %collective-permute-start.8 = (bf16[512,384]{1,0:T(8,128)(2,1)S(1)}, bf16[512,384]{1,0:T(8,128)(2,1)S(1)}, u32[]{:S(2)}, u32[]{:S(2)}) collective-permute-start(bf16[512,384]{1,0:T(8,128)(2,1)S(1)} %shard_map.153.refs_0_), channel_id=1, source_target_pairs={{0,2},{1,3},{2,0},{3,1},{4,6},{5,7},{6,4},{7,5},{8,10},{9,11},{10,... | collective-permute-start | bytes 1179656 | tf_op jit(solution)/shard_map/ppermute | solution.py:65
  83.3 4.7 %collective-permute-start.25 = (f32[1,128]{1,0:T(1,128)S(1)}, f32[1,128]{1,0:T(1,128)S(1)}, u32[]{:S(2)}, u32[]{:S(2)}) collective-permute-start(f32[1,128]{1,0:T(1,128)S(1)} %shard_map.167), channel_id=1, source_target_pairs={{0,4},{4,0},{8,12},{12,8},{16,20},{20,16},{24,28},{28,24},{1,5},{5... | collective-permute-start | bytes 1544 | tf_op jit(solution)/shard_map/ppermute | solution.py:65
  88.1 4.8 %collective-permute-start.26 = (f32[1,128]{1,0:T(1,128)S(1)}, f32[1,128]{1,0:T(1,128)S(1)}, u32[]{:S(2)}, u32[]{:S(2)}) collective-permute-start(f32[1,128]{1,0:T(1,128)S(1)} %max.20), channel_id=1, source_target_pairs={{0,8},{4,12},{8,0},{12,4},{16,24},{20,28},{24,16},{28,20},{1,9},{5... | collective-permute-start | bytes 1544 | tf_op jit(solution)/shard_map/ppermute | solution.py:65
  91.3 9.7 %collective-permute-start.6 = (bf16[512,384]{1,0:T(8,128)(2,1)S(1)}, bf16[512,384]{1,0:T(8,128)(2,1)S(1)}, u32[]{:S(2)}, u32[]{:S(2)}) collective-permute-start(bf16[512,384]{1,0:T(8,128)(2,1)S(1)} %shard_map.153.refs_0_), channel_id=1, source_target_pairs={{0,1},{1,0},{2,3},{3,2},{4,5},{5,4},{6,7},{7,6},{8,9},{9,8},{10,11... | collective-permute-start | bytes 1179656 | tf_op jit(solution)/shard_map/ppermute | solution.py:65
  (19 other events, 114.5 us)

commit v4 on v3

--- a/solution.py
+++ b/solution.py
@@ -356,6 +356,7 @@
         [flip],
         [own, other],
         after,
+        length=3,
         blocked=True,
     )[0]
 
@@ -505,7 +506,7 @@
         out_specs=[WHOLE, whole(tokens)],
         scratch_shapes=[pltpu.VMEM(weight_far.shape, BF16), pltpu.SemaphoreType.DMA((2,))],
         compiler_params=pltpu.CompilerParams(vmem_limit_bytes=VMEM_LIMIT),
-        cost_estimate=pl.CostEstimate(flops=3 * 10**9, bytes_accessed=0, transcendentals=0),
+        cost_estimate=pl.CostEstimate(flops=0, bytes_accessed=0, transcendentals=0),
     )(start, vocab, weight_far, vocab, tokens, own, near, near_weight)
 
 
@@ -707,7 +708,11 @@
         [request_low, inside, asked_kv, *asking],
         all_tokens[2:3],
     )
-    afters = [all_tokens[3:4], (), w_parts[2:3] + [all_tokens[-1]]]
+    afters = [
+        all_tokens[3:4] + w_parts[2:3] + [halo[1]],
+        halo[:1],
+        w_parts[3:4] + [all_tokens[-1]],
+    ]
     bit = 1
     while bit < n_seq:
         flip = ((seq_index & bit) > 0).astype(jnp.int32).reshape(1)
@@ -735,7 +740,6 @@
         [field, far_mixed, last_mixed, *w_parts[2:]],
         scratch=[pltpu.VMEM((columns, 1), F32), pltpu.SemaphoreType.DMA((1,))],
         far=[far_gain],
-        after=halo[1:],
     )
     (sent,) = call(
         partial(held_body, limit),

time: 105 us -> 102 us (0.971)
  starting transfers between devices: 39.6 us -> 31.5 us
  waiting for transfers between devices: 24 us -> 30.3 us
  Pallas kernels: 29.3 us -> 27.8 us
    ppermute x25, waiting for transfers between devices: 18.9 us -> 26.2 us  [swap(): return lax.ppermute(array, axis, [(i, i ^ bit) for i in range(count)])]
    ppermute x25, starting transfers between devices: 31.7 us -> 24.9 us  [swap(): return lax.ppermute(array, axis, [(i, i ^ bit) for i in range(count)])]
    pallas_call x20, Pallas kernels: 23.8 us -> 22.3 us  [call(): pl.pallas_call(body, grid=(1,) if blocked else (), out_shape=outs, in_spe...]
    ppermute x3, starting transfers between devices: 7.2 us -> 5.89 us  [shifted(): return lax.ppermute(array, axis, pairs)]
    unnamed x28 -> x30, local copies, waits for them, and re-layouts: 1.71 us -> 2.51 us
  transfers between devices with their start and end apart: 29 -> 29, of which waited for: 12 -> 12; matrix products, arithmetic and copies ran while one was open for 6% -> 7% of each run, Pallas kernels for 28% -> 27%
where the time goes in v4:
time: 102 us; the launch traced here: 101 us
  starting transfers between devices  31.5 us (31%)
  waiting for transfers between devices  30.3 us (30%)
  Pallas kernels  27.8 us (27%)
  local copies, waits for them, and re-layouts  5.03 us (5%)
  matrix products  3.38 us (3%)
  between operations  1.7 us (2%)
  other arithmetic  1.41 us (1%)
    ppermute x25, waiting for transfers between devices, swap(): return lax.ppermute(array, axis, [(i, i ^ bit) for i in range(count)])  26.2 us
    ppermute x25, starting transfers between devices, swap(): return lax.ppermute(array, axis, [(i, i ^ bit) for i in range(count)])  24.9 us
    pallas_call x20, Pallas kernels, call(): pl.pallas_call(body, grid=(1,) if blocked else (), out_shape=outs, in_spe...  22.3 us
    ppermute x3, starting transfers between devices, shifted(): return lax.ppermute(array, axis, pairs)  5.89 us
    ppermute x3, waiting for transfers between devices, shifted(): return lax.ppermute(array, axis, pairs)  4.17 us
    dot_general x4, matrix products, mm_last(): lax.dot_general(a, b, (((1,), (1,)), ((), ())), preferred_element_type=F32)  3.38 us
    pallas_call x1, Pallas kernels, begin_rows(): pl.pallas_call(partial(begin_body, limit), grid=(1,), out_shape=[struct((...  2.77 us
    pallas_call x1, Pallas kernels, half_logits(): pl.pallas_call(partial(logits_body, limit), grid_spec=pltpu.PrefetchScala...  2.7 us
  transfers between devices with their start and end apart: 29, of which 12 were waited for; matrix products, arithmetic and copies ran while one was open for 7% of the time, Pallas kernels for 27%

profile of v4, /device:TPU:0, one launch (start us, length us, event | category | flops | bytes accessed | tf_op | source)
XLA Modules:
  0.0 101.2 jit_solution(8435914443687189928)
XLA Ops:
  1.2 2.6 %collective-permute-start.2 = (bf16[512,768]{1,0:T(8,128)(2,1)}, bf16[512,768]{1,0:T(8,128)(2,1)S(1)}, u32[]{:S(2)}, u32[]{:S(2)}) collective-permute-start(bf16[512,768]{1,0:T(8,128)(2,1)} %tokens.1), channel_id=1, source_target_pairs={{0,2},{1,3},{2,0},{3,1},{4,6},{5,7},{6,4},{7,5},{8,10},{9,11},{10,... | collective-permute-start | bytes 2359304 | tf_op jit(solution)/shard_map/ppermute | solution.py:65
  5.3 2.7 %collective-permute-start.12 = (bf16[768,128]{1,0:T(8,128)(2,1)S(1)}, bf16[768,128]{1,0:T(8,128)(2,1)S(1)}, u32[]{:S(2)}, u32[]{:S(2)}) collective-permute-start(bf16[768,128]{1,0:T(8,128)(2,1)S(1)} %shard_map.154.first), channel_id=1, source_target_pairs={{0,16},{4,20},{8,24},{12,28},{16,0},{20,4},{24,8},{28,12},{1,17},{... | collective-permute-start | bytes 589832 | tf_op jit(solution)/shard_map/ppermute | solution.py:65
  9.6 1.8 %copy-done.4 = bf16[384,3072]{1,0:T(8,128)(2,1)S(1)} copy-done((bf16[384,3072]{1,0:T(8,128)(2,1)S(1)}, bf16[384,3072]{1,0:T(8,128)(2,1)}, u32[]{:S(2)}) %copy-start.4) | copy-done | bytes 2359320
  11.4 6.0 %shard_map.147 = (f32[512,1152]{1,0:T(8,128)S(1)}, f32[512,1]{1,0:T(8,128)S(1)}, bf16[768,384]{1,0:T(8,128)(2,1)S(1)}, bf16[768,384]{1,0:T(8,128)(2,1)S(1)}, bf1...) custom-call(s32[1]{0:T(128)} %bitcast.refs_0_, ...), custom_call_target="tpu_custom_call" | custom-call | tf_op jit(solution)/shard_map/pallas_call | solution.py:38
  18.7 3.4 %collective-permute-done.2.source = bf16[512,768]{1,0:T(8,128)(2,1)S(1)} collective-permute-done((bf16[512,768]{1,0:T(8,128)(2,1)}, bf16[512,768]{1,0:T(8,128)(2,1)S(1)}, u32[]{:S(2)}, u32[]{:S(2)}) %collective-permute-start.2) | collective-permute-done | bytes 786464 | tf_op jit(solution)/shard_map/ppermute | solution.py:65
  22.3 1.8 %collective-permute-start.9 = (bf16[768,384]{1,0:T(8,128)(2,1)}, bf16[768,384]{1,0:T(8,128)(2,1)S(1)}, u32[]{:S(2)}, u32[]{:S(2)}) collective-permute-start(bf16[768,384]{1,0:T(8,128)(2,1)} %get-tuple-element.61), channel_id=1, source_target_pairs={{0,2},{1,3},{2,0},{3,1},{4,6},{5,7},{6,4},{7,5},{8,10},{9,11},{10,... | collective-permute-start | bytes 1769480 | tf_op jit(solution)/shard_map/ppermute | solution.py:65
  24.2 1.6 %collective-permute-start.13 = (bf16[768,128]{1,0:T(8,128)(2,1)S(1)}, bf16[768,128]{1,0:T(8,128)(2,1)S(1)}, u32[]{:S(2)}, u32[]{:S(2)}) collective-permute-start(bf16[768,128]{1,0:T(8,128)(2,1)S(1)} %shard_map.155.first), channel_id=1, source_target_pairs={{0,8},{4,12},{8,0},{12,4},{16,24},{20,28},{24,16},{28,20},{1,9},{5... | collective-permute-start | bytes 589832 | tf_op jit(solution)/shard_map/ppermute | solution.py:65
  28.2 2.2 %shard_map.152 = (bf16[768,512]{1,0:T(8,128)(2,1)S(1)}, bf16[768,512]{1,0:T(8,128)(2,1)S(1)}, bf16[768,512]{1,0:T(8,128)(2,1)}, bf16[768,256]{1,0:T(8,128)(2,1)}) custom-call(s32[1]{0:T(128)} %bitcast.refs_0_, s32[1]{0:T(128)} %bitcast.1.base.refs_1_, bf16[2,768,384]{2,1,0:T(8,128)(2,1)S(1)} %get-tuple-element.40.refs_2_, ...), custom_call_target="tpu_custom_call" | custom-call | flops 10000000000 | tf_op jit(solution)/shard_map/pallas_call | solution.py:38
  33.7 2.7 %collective-permute-start.14 = (bf16[768,128]{1,0:T(8,128)(2,1)S(1)}, bf16[768,128]{1,0:T(8,128)(2,1)S(1)}, u32[]{:S(2)}, u32[]{:S(2)}) collective-permute-start(bf16[768,128]{1,0:T(8,128)(2,1)S(1)} %shard_map.156.first.refs_3_), channel_id=1, source_target_pairs={{0,4},{4,0},{8,12},{12,8},{16,20},{20,16},{24,28},{28,24},{1,5},{5... | collective-permute-start | bytes 589832 | tf_op jit(solution)/shard_map/ppermute | solution.py:65
  36.4 1.9 %collective-permute-done.15.refs_1_ = bf16[384,128]{1,0:T(8,128)(2,1)S(1)} collective-permute-done((bf16[384,128]{1,0:T(8,128)(2,1)S(1)}, bf16[384,128]{1,0:T(8,128)(2,1)S(1)}, u32[]{:S(2)}, u32[]{:S(2)}) %collective-permute-start.15) | collective-permute-done | bytes 98336 | tf_op jit(solution)/shard_map/ppermute | solution.py:71
  38.3 2.3 %collective-permute-done.16.refs_2_ = bf16[384,128]{1,0:T(8,128)(2,1)S(1)} collective-permute-done((bf16[384,128]{1,0:T(8,128)(2,1)S(1)}, bf16[384,128]{1,0:T(8,128)(2,1)S(1)}, u32[]{:S(2)}, u32[]{:S(2)}) %collective-permute-start.16) | collective-permute-done | bytes 98336 | tf_op jit(solution)/shard_map/ppermute | solution.py:71
  43.0 3.5 %collective-permute-done.17.other = bf16[400,128]{1,0:T(8,128)(2,1)S(1)} collective-permute-done((bf16[400,128]{1,0:T(8,128)(2,1)S(1)}, bf16[400,128]{1,0:T(8,128)(2,1)S(1)}, u32[]{:S(2)}, u32[]{:S(2)}) %collective-permute-start.17) | collective-permute-done | bytes 102432 | tf_op jit(solution)/shard_map/ppermute | solution.py:65
  47.3 1.8 %collective-permute-start.18 = (bf16[400,128]{1,0:T(8,128)(2,1)S(1)}, bf16[400,128]{1,0:T(8,128)(2,1)S(1)}, u32[]{:S(2)}, u32[]{:S(2)}) collective-permute-start(bf16[400,128]{1,0:T(8,128)(2,1)S(1)} %shard_map.159.own), channel_id=1, source_target_pairs={{0,8},{4,12},{8,0},{12,4},{16,24},{20,28},{24,16},{28,20},{1,9},{5... | collective-permute-start | bytes 307208 | tf_op jit(solution)/shard_map/ppermute | solution.py:65
  52.0 4.3 %collective-permute-start.19 = (bf16[400,128]{1,0:T(8,128)(2,1)S(1)}, bf16[400,128]{1,0:T(8,128)(2,1)S(1)}, u32[]{:S(2)}, u32[]{:S(2)}) collective-permute-start(bf16[400,128]{1,0:T(8,128)(2,1)S(1)} %shard_map.160.own), channel_id=1, source_target_pairs={{0,16},{4,20},{8,24},{12,28},{16,0},{20,4},{24,8},{28,12},{1,17},{... | collective-permute-start | bytes 307208 | tf_op jit(solution)/shard_map/ppermute | solution.py:65
  56.3 3.3 %collective-permute-start.4 = (bf16[768,512]{1,0:T(8,128)(2,1)}, bf16[768,512]{1,0:T(8,128)(2,1)}, u32[]{:S(2)}, u32[]{:S(2)}) collective-permute-start(bf16[768,512]{1,0:T(8,128)(2,1)} %get-tuple-element.54), channel_id=1, source_target_pairs={{0,4},{4,8},{8,12},{12,16},{16,20},{20,24},{24,28},{1,5},{5,9},{9,... | collective-permute-start | bytes 2359304 | tf_op jit(solution)/shard_map/ppermute | solution.py:71
  60.8 4.1 %collective-permute-done.21.far = bf16[384,128]{1,0:T(8,128)(2,1)S(1)} collective-permute-done((bf16[384,128]{1,0:T(8,128)(2,1)S(1)}, bf16[384,128]{1,0:T(8,128)(2,1)S(1)}, u32[]{:S(2)}, u32[]{:S(2)}) %collective-permute-start.21) | collective-permute-done | bytes 98336 | tf_op jit(solution)/shard_map/ppermute | solution.py:65
  64.9 2.8 %shard_map.162 = (bf16[2048,768]{1,0:T(8,128)(2,1)S(1)}, f32[768,128]{1,0:T(8,128)S(1)}) custom-call(s32[1]{0:T(128)} %bitcast.12.start, bf16[4008,768]{1,0:T(8,128)(2,1)} %bitcast.48, bf16[768,384]{1,0:T(8,128)(2,1)} %copy-done.2, bf16[4008,768]{1,0:T(8,128)(2,1)} %bitcast.49, bf16[768,128]{1,0:T(8,128)(2,1)S(1)} %shard_map.157.refs_0_.refs_1_.tokens, ...), custom_call_target="tpu_custom_call" | custom-call | tf_op jit(solution)/shard_map/pallas_call | solution.py:499
  70.5 2.7 %shard_map.165.kept = bf16[2048,128]{1,0:T(8,128)(2,1)S(1)} custom-call(s32[1]{0:T(128)} %bitcast.10.start, bf16[4008,768]{1,0:T(8,128)(2,1)} %bitcast.50, bf16[768,128]{1,0:T(8,128)(2,1)S(1)} %get-tuple-element.66.scaled, bf16[2048,128]{1,0:T(8,128)(2,1)S(1)} %shard_map.164.refs_0_), custom_call_target="tpu_custom_call" | custom-call | tf_op jit(solution)/shard_map/pallas_call | solution.py:541
  75.0 3.8 %shard_map.153.refs_0_ = bf16[512,384]{1,0:T(8,128)(2,1)S(1)} custom-call(s32[1]{0:T(128)} %bitcast.6.place, s32[1,512]{1,0:T(1,128)S(1)} %get-tuple-element.55.low, bf16[384,512]{1,0:T(8,128)(2,1)S(1)} %copy-done.12, bf16[768,512]{1,0:T(8,128)(2,1)S(1)} %copy-done.14, bf16[768,512]{1,0:T(8,128)(2,1)} %collective-permute-done.4.refs_1_, ...), custom_call_target="tpu_custom_call" | custom-call | flops 30000001024 | tf_op jit(solution)/shard_map/pallas_call | solution.py:38
  80.4 3.2 %collective-permute-done.24.came = bf16[1024,128]{1,0:T(8,128)(2,1)S(1)} collective-permute-done((bf16[1024,128]{1,0:T(8,128)(2,1)S(1)}, bf16[1024,128]{1,0:T(8,128)(2,1)S(1)}, u32[]{:S(2)}, u32[]{:S(2)}) %collective-permute-start.24) | collective-permute-done | bytes 262176 | tf_op jit(solution)/shard_map/ppermute | solution.py:65
  84.5 2.8 %collective-permute-done.25 = f32[1,128]{1,0:T(1,128)S(1)} collective-permute-done((f32[1,128]{1,0:T(1,128)S(1)}, f32[1,128]{1,0:T(1,128)S(1)}, u32[]{:S(2)}, u32[]{:S(2)}) %collective-permute-start.25) | collective-permute-done | bytes 544 | tf_op jit(solution)/shard_map/ppermute | solution.py:65
  88.2 2.7 %collective-permute-done.26 = f32[1,128]{1,0:T(1,128)S(1)} collective-permute-done((f32[1,128]{1,0:T(1,128)S(1)}, f32[1,128]{1,0:T(1,128)S(1)}, u32[]{:S(2)}, u32[]{:S(2)}) %collective-permute-start.26) | collective-permute-done | bytes 544 | tf_op jit(solution)/shard_map/ppermute | solution.py:65
  92.8 2.6 %collective-permute-done.27 = f32[1,128]{1,0:T(1,128)S(1)} collective-permute-done((f32[1,128]{1,0:T(1,128)S(1)}, f32[1,128]{1,0:T(1,128)S(1)}, u32[]{:S(2)}, u32[]{:S(2)}) %collective-permute-start.27) | collective-permute-done | bytes 544 | tf_op jit(solution)/shard_map/ppermute | solution.py:65
  96.0 2.9 %collective-permute-done.28 = f32[2,128]{1,0:T(2,128)S(1)} collective-permute-done((f32[2,128]{1,0:T(2,128)S(1)}, f32[2,128]{1,0:T(2,128)S(1)}, u32[]{:S(2)}, u32[]{:S(2)}) %collective-permute-start.28) | collective-permute-done | bytes 1056 | tf_op jit(solution)/shard_map/ppermute | solution.py:65
  (103 shorter events, 31.0 us)
Async XLA Ops:
  0.6 8.9 %collective-permute-start.1 = (bf16[512,768]{1,0:T(8,128)(2,1)}, bf16[512,768]{1,0:T(8,128)(2,1)S(1)}, u32[]{:S(2)}, u32[]{:S(2)}) collective-permute-start(bf16[512,768]{1,0:T(8,128)(2,1)} %tokens.1), channel_id=1, source_target_pairs={{0,1},{1,0},{2,3},{3,2},{4,5},{5,4},{6,7},{7,6},{8,9},{9,8},{10,11... | collective-permute-start | bytes 2359304 | tf_op jit(solution)/shard_map/ppermute | solution.py:65
  1.2 20.9 %collective-permute-start.2 = (bf16[512,768]{1,0:T(8,128)(2,1)}, bf16[512,768]{1,0:T(8,128)(2,1)S(1)}, u32[]{:S(2)}, u32[]{:S(2)}) collective-permute-start(bf16[512,768]{1,0:T(8,128)(2,1)} %tokens.1), channel_id=1, source_target_pairs={{0,2},{1,3},{2,0},{3,1},{4,6},{5,7},{6,4},{7,5},{8,10},{9,11},{10,... | collective-permute-start | bytes 2359304 | tf_op jit(solution)/shard_map/ppermute | solution.py:65
  5.3 18.8 %collective-permute-start.12 = (bf16[768,128]{1,0:T(8,128)(2,1)S(1)}, bf16[768,128]{1,0:T(8,128)(2,1)S(1)}, u32[]{:S(2)}, u32[]{:S(2)}) collective-permute-start(bf16[768,128]{1,0:T(8,128)(2,1)S(1)} %shard_map.154.first), channel_id=1, source_target_pairs={{0,16},{4,20},{8,24},{12,28},{16,0},{20,4},{24,8},{28,12},{1,17},{... | collective-permute-start | bytes 589832 | tf_op jit(solution)/shard_map/ppermute | solution.py:65
  22.2 5.0 %collective-permute-start.3 = (bf16[512,768]{1,0:T(8,128)(2,1)S(1)}, bf16[512,768]{1,0:T(8,128)(2,1)S(1)}, u32[]{:S(2)}, u32[]{:S(2)}) collective-permute-start(bf16[512,768]{1,0:T(8,128)(2,1)S(1)} %get-tuple-element.43), channel_id=1, source_target_pairs={{0,1},{1,0},{2,3},{3,2},{4,5},{5,4},{6,7},{7,6},{8,9},{9,8},{10,11... | collective-permute-start | bytes 2359304 | tf_op jit(solution)/shard_map/ppermute | solution.py:65
  22.3 20.7 %collective-permute-start.9 = (bf16[768,384]{1,0:T(8,128)(2,1)}, bf16[768,384]{1,0:T(8,128)(2,1)S(1)}, u32[]{:S(2)}, u32[]{:S(2)}) collective-permute-start(bf16[768,384]{1,0:T(8,128)(2,1)} %get-tuple-element.61), channel_id=1, source_target_pairs={{0,2},{1,3},{2,0},{3,1},{4,6},{5,7},{6,4},{7,5},{8,10},{9,11},{10,... | collective-permute-start | bytes 1769480 | tf_op jit(solution)/shard_map/ppermute | solution.py:65
  24.2 9.5 %collective-permute-start.13 = (bf16[768,128]{1,0:T(8,128)(2,1)S(1)}, bf16[768,128]{1,0:T(8,128)(2,1)S(1)}, u32[]{:S(2)}, u32[]{:S(2)}) collective-permute-start(bf16[768,128]{1,0:T(8,128)(2,1)S(1)} %shard_map.155.first), channel_id=1, source_target_pairs={{0,8},{4,12},{8,0},{12,4},{16,24},{20,28},{24,16},{28,20},{1,9},{5... | collective-permute-start | bytes 589832 | tf_op jit(solution)/shard_map/ppermute | solution.py:65
  30.4 16.1 %collective-permute-start.5 = (bf16[768,256]{1,0:T(8,128)(2,1)}, bf16[768,256]{1,0:T(8,128)(2,1)S(1)}, u32[]{:S(2)}, u32[]{:S(2)}) collective-permute-start(bf16[768,256]{1,0:T(8,128)(2,1)} %get-tuple-element.58), channel_id=1, source_target_pairs={{20,28},{21,29},{22,30},{23,31}} | collective-permute-start | bytes 1179656 | tf_op jit(solution)/shard_map/ppermute | solution.py:701
  31.1 7.3 %collective-permute-start.15 = (bf16[384,128]{1,0:T(8,128)(2,1)S(1)}, bf16[384,128]{1,0:T(8,128)(2,1)S(1)}, u32[]{:S(2)}, u32[]{:S(2)}) collective-permute-start(bf16[384,128]{1,0:T(8,128)(2,1)S(1)} %get-tuple-element.53.refs_10_.refs_0_), channel_id=1, source_target_pairs={{4,0},{8,4},{12,8},{16,12},{20,16},{24,20},{28,24},{5,1},{9,5},{13... | collective-permute-start | bytes 294920 | tf_op jit(solution)/shard_map/ppermute | solution.py:71
  32.4 8.2 %collective-permute-start.16 = (bf16[384,128]{1,0:T(8,128)(2,1)S(1)}, bf16[384,128]{1,0:T(8,128)(2,1)S(1)}, u32[]{:S(2)}, u32[]{:S(2)}) collective-permute-start(bf16[384,128]{1,0:T(8,128)(2,1)S(1)} %get-tuple-element.53.refs_10_.refs_0_), channel_id=1, source_target_pairs={{8,0},{12,4},{16,8},{20,12},{24,16},{28,20},{9,1},{13,5},{17,9},{2... | collective-permute-start | bytes 294920 | tf_op jit(solution)/shard_map/ppermute | solution.py:71
  33.7 9.2 %collective-permute-start.14 = (bf16[768,128]{1,0:T(8,128)(2,1)S(1)}, bf16[768,128]{1,0:T(8,128)(2,1)S(1)}, u32[]{:S(2)}, u32[]{:S(2)}) collective-permute-start(bf16[768,128]{1,0:T(8,128)(2,1)S(1)} %shard_map.156.first.refs_3_), channel_id=1, source_target_pairs={{0,4},{4,0},{8,12},{12,8},{16,20},{20,16},{24,28},{28,24},{1,5},{5... | collective-permute-start | bytes 589832 | tf_op jit(solution)/shard_map/ppermute | solution.py:65
  41.8 4.7 %collective-permute-start.17 = (bf16[400,128]{1,0:T(8,128)(2,1)S(1)}, bf16[400,128]{1,0:T(8,128)(2,1)S(1)}, u32[]{:S(2)}, u32[]{:S(2)}) collective-permute-start(bf16[400,128]{1,0:T(8,128)(2,1)S(1)} %shard_map.158.own), channel_id=1, source_target_pairs={{0,4},{4,0},{8,12},{12,8},{16,20},{20,16},{24,28},{28,24},{1,5},{5... | collective-permute-start | bytes 307208 | tf_op jit(solution)/shard_map/ppermute | solution.py:65
  42.9 16.7 %collective-permute-start.11 = (bf16[768,384]{1,0:T(8,128)(2,1)}, bf16[768,384]{1,0:T(8,128)(2,1)S(1)}, u32[]{:S(2)}, u32[]{:S(2)}) collective-permute-start(bf16[768,384]{1,0:T(8,128)(2,1)} %copy-done.8), channel_id=1, source_target_pairs={{0,3},{1,2},{2,1},{3,0},{4,7},{5,6},{6,5},{7,4},{8,11},{9,10},{10,... | collective-permute-start | bytes 1769480 | tf_op jit(solution)/shard_map/ppermute | solution.py:65
  47.3 4.7 %collective-permute-start.18 = (bf16[400,128]{1,0:T(8,128)(2,1)S(1)}, bf16[400,128]{1,0:T(8,128)(2,1)S(1)}, u32[]{:S(2)}, u32[]{:S(2)}) collective-permute-start(bf16[400,128]{1,0:T(8,128)(2,1)S(1)} %shard_map.159.own), channel_id=1, source_target_pairs={{0,8},{4,12},{8,0},{12,4},{16,24},{20,28},{24,16},{28,20},{1,9},{5... | collective-permute-start | bytes 307208 | tf_op jit(solution)/shard_map/ppermute | solution.py:65
  50.4 14.4 %collective-permute-start.7 = (bf16[768,384]{1,0:T(8,128)(2,1)}, bf16[768,384]{1,0:T(8,128)(2,1)S(1)}, u32[]{:S(2)}, u32[]{:S(2)}) collective-permute-start(bf16[768,384]{1,0:T(8,128)(2,1)} %copy-done.7), channel_id=1, source_target_pairs={{0,1},{1,0},{2,3},{3,2},{4,5},{5,4},{6,7},{7,6},{8,9},{9,8},{10,11... | collective-permute-start | bytes 1769480 | tf_op jit(solution)/shard_map/ppermute | solution.py:65
  52.0 8.1 %collective-permute-start.19 = (bf16[400,128]{1,0:T(8,128)(2,1)S(1)}, bf16[400,128]{1,0:T(8,128)(2,1)S(1)}, u32[]{:S(2)}, u32[]{:S(2)}) collective-permute-start(bf16[400,128]{1,0:T(8,128)(2,1)S(1)} %shard_map.160.own), channel_id=1, source_target_pairs={{0,16},{4,20},{8,24},{12,28},{16,0},{20,4},{24,8},{28,12},{1,17},{... | collective-permute-start | bytes 307208 | tf_op jit(solution)/shard_map/ppermute | solution.py:65
  56.3 18.7 %collective-permute-start.4 = (bf16[768,512]{1,0:T(8,128)(2,1)}, bf16[768,512]{1,0:T(8,128)(2,1)}, u32[]{:S(2)}, u32[]{:S(2)}) collective-permute-start(bf16[768,512]{1,0:T(8,128)(2,1)} %get-tuple-element.54), channel_id=1, source_target_pairs={{0,4},{4,8},{8,12},{12,16},{16,20},{20,24},{24,28},{1,5},{5,9},{9,... | collective-permute-start | bytes 2359304 | tf_op jit(solution)/shard_map/ppermute | solution.py:71
  60.2 4.7 %collective-permute-start.21 = (bf16[384,128]{1,0:T(8,128)(2,1)S(1)}, bf16[384,128]{1,0:T(8,128)(2,1)S(1)}, u32[]{:S(2)}, u32[]{:S(2)}) collective-permute-start(bf16[384,128]{1,0:T(8,128)(2,1)S(1)} %shard_map.161.own), channel_id=1, source_target_pairs={{0,2},{1,3},{2,0},{3,1},{4,6},{5,7},{6,4},{7,5},{8,10},{9,11},{10,... | collective-permute-start | bytes 294920 | tf_op jit(solution)/shard_map/ppermute | solution.py:65
  60.7 4.1 %collective-permute-start.20 = (bf16[384,128]{1,0:T(8,128)(2,1)S(1)}, bf16[384,128]{1,0:T(8,128)(2,1)S(1)}, u32[]{:S(2)}, u32[]{:S(2)}) collective-permute-start(bf16[384,128]{1,0:T(8,128)(2,1)S(1)} %shard_map.161.own), channel_id=1, source_target_pairs={{0,1},{1,0},{2,3},{3,2},{4,5},{5,4},{6,7},{7,6},{8,9},{9,8},{10,11... | collective-permute-start | bytes 294920 | tf_op jit(solution)/shard_map/ppermute | solution.py:65
  74.4 9.2 %collective-permute-start.24 = (bf16[1024,128]{1,0:T(8,128)(2,1)S(1)}, bf16[1024,128]{1,0:T(8,128)(2,1)S(1)}, u32[]{:S(2)}, u32[]{:S(2)}) collective-permute-start(bf16[1024,128]{1,0:T(8,128)(2,1)S(1)} %get-tuple-element.70), channel_id=1, source_target_pairs={{0,2},{1,3},{2,0},{3,1},{4,6},{5,7},{6,4},{7,5},{8,10},{9,11},{10,... | collective-permute-start | bytes 786440 | tf_op jit(solution)/shard_map/ppermute | solution.py:65
  78.8 13.3 %collective-permute-start.8 = (bf16[512,384]{1,0:T(8,128)(2,1)S(1)}, bf16[512,384]{1,0:T(8,128)(2,1)S(1)}, u32[]{:S(2)}, u32[]{:S(2)}) collective-permute-start(bf16[512,384]{1,0:T(8,128)(2,1)S(1)} %shard_map.153.refs_0_), channel_id=1, source_target_pairs={{0,2},{1,3},{2,0},{3,1},{4,6},{5,7},{6,4},{7,5},{8,10},{9,11},{10,... | collective-permute-start | bytes 1179656 | tf_op jit(solution)/shard_map/ppermute | solution.py:65
  83.8 3.6 %collective-permute-start.25 = (f32[1,128]{1,0:T(1,128)S(1)}, f32[1,128]{1,0:T(1,128)S(1)}, u32[]{:S(2)}, u32[]{:S(2)}) collective-permute-start(f32[1,128]{1,0:T(1,128)S(1)} %shard_map.167), channel_id=1, source_target_pairs={{0,4},{4,0},{8,12},{12,8},{16,20},{20,16},{24,28},{28,24},{1,5},{5... | collective-permute-start | bytes 1544 | tf_op jit(solution)/shard_map/ppermute | solution.py:65
  84.5 10.9 %collective-permute-start.6 = (bf16[512,384]{1,0:T(8,128)(2,1)S(1)}, bf16[512,384]{1,0:T(8,128)(2,1)S(1)}, u32[]{:S(2)}, u32[]{:S(2)}) collective-permute-start(bf16[512,384]{1,0:T(8,128)(2,1)S(1)} %shard_map.153.refs_0_), channel_id=1, source_target_pairs={{0,1},{1,0},{2,3},{3,2},{4,5},{5,4},{6,7},{7,6},{8,9},{9,8},{10,11... | collective-permute-start | bytes 1179656 | tf_op jit(solution)/shard_map/ppermute | solution.py:65
  90.9 4.4 %collective-permute-start.27 = (f32[1,128]{1,0:T(1,128)S(1)}, f32[1,128]{1,0:T(1,128)S(1)}, u32[]{:S(2)}, u32[]{:S(2)}) collective-permute-start(f32[1,128]{1,0:T(1,128)S(1)} %max.21), channel_id=1, source_target_pairs={{0,16},{4,20},{8,24},{12,28},{16,0},{20,4},{24,8},{28,12},{1,17},{... | collective-permute-start | bytes 1544 | tf_op jit(solution)/shard_map/ppermute | solution.py:65
  92.7 6.3 %collective-permute-start.10 = (bf16[512,384]{1,0:T(8,128)(2,1)S(1)}, bf16[512,384]{1,0:T(8,128)(2,1)S(1)}, u32[]{:S(2)}, u32[]{:S(2)}) collective-permute-start(bf16[512,384]{1,0:T(8,128)(2,1)S(1)} %collective-permute-done.8.refs_0_), channel_id=1, source_target_pairs={{0,1},{1,0},{2,3},{3,2},{4,5},{5,4},{6,7},{7,6},{8,9},{9,8},{10,11... | collective-permute-start | bytes 1179656 | tf_op jit(solution)/shard_map/ppermute | solution.py:65
  (20 other events, 104.1 us)

commit v5 on v4

--- a/solution.py
+++ b/solution.py
@@ -707,10 +707,11 @@
         [],
         [request_low, inside, asked_kv, *asking],
         all_tokens[2:3],
+        length=10,
     )
     afters = [
-        all_tokens[3:4] + w_parts[2:3] + [halo[1]],
-        halo[:1],
+        w_parts[2:3] + pinned(halo[1:]),
+        halo[:1] + tuple(all_tokens[3:4]),
         w_parts[3:4] + [all_tokens[-1]],
     ]
     bit = 1

time: 102 us -> 101 us (level)
  waiting for transfers between devices: 30.3 us -> 24 us
  starting transfers between devices: 31.5 us -> 36.8 us
    ppermute x25, waiting for transfers between devices: 26.2 us -> 19.3 us  [swap(): return lax.ppermute(array, axis, [(i, i ^ bit) for i in range(count)])]
    ppermute x3, starting transfers between devices: 5.89 us -> 8.76 us  [shifted(): return lax.ppermute(array, axis, pairs)]
    ppermute x25, starting transfers between devices: 24.9 us -> 26.6 us  [swap(): return lax.ppermute(array, axis, [(i, i ^ bit) for i in range(count)])]
    unnamed x30 -> x24, local copies, waits for them, and re-layouts: 2.51 us -> 1.71 us
  transfers between devices with their start and end apart: 29 -> 29, of which waited for: 12 -> 12; matrix products, arithmetic and copies ran while one was open for 7% -> 7% of each run, Pallas kernels for 27% -> 28%
where the time goes in v5:
time: 101 us; the launch traced here: 100 us
  starting transfers between devices  36.8 us (36%)
  Pallas kernels  28.1 us (28%)
  waiting for transfers between devices  24 us (24%)
  local copies, waits for them, and re-layouts  4.22 us (4%)
  matrix products  3.37 us (3%)
  other arithmetic  2.04 us (2%)
  between operations  1.52 us (2%)
    ppermute x25, starting transfers between devices, swap(): return lax.ppermute(array, axis, [(i, i ^ bit) for i in range(count)])  26.6 us
    pallas_call x20, Pallas kernels, call(): pl.pallas_call(body, grid=(1,) if blocked else (), out_shape=outs, in_spe...  22.6 us
    ppermute x25, waiting for transfers between devices, swap(): return lax.ppermute(array, axis, [(i, i ^ bit) for i in range(count)])  19.3 us
    ppermute x3, starting transfers between devices, shifted(): return lax.ppermute(array, axis, pairs)  8.76 us
    ppermute x3, waiting for transfers between devices, shifted(): return lax.ppermute(array, axis, pairs)  4.7 us
    dot_general x4, matrix products, mm_last(): lax.dot_general(a, b, (((1,), (1,)), ((), ())), preferred_element_type=F32)  3.37 us
    pallas_call x1, Pallas kernels, begin_rows(): pl.pallas_call(partial(begin_body, limit), grid=(1,), out_shape=[struct((...  2.77 us
    pallas_call x1, Pallas kernels, half_logits(): pl.pallas_call(partial(logits_body, limit), grid_spec=pltpu.PrefetchScala...  2.68 us
  transfers between devices with their start and end apart: 29, of which 12 were waited for; matrix products, arithmetic and copies ran while one was open for 7% of the time, Pallas kernels for 28%

profile of v5, /device:TPU:0, one launch (start us, length us, event | category | flops | bytes accessed | tf_op | source)
XLA Modules:
  0.0 100.0 jit_solution(16272304747162955811)
XLA Ops:
  1.2 2.6 %collective-permute-start.2 = (bf16[512,768]{1,0:T(8,128)(2,1)}, bf16[512,768]{1,0:T(8,128)(2,1)S(1)}, u32[]{:S(2)}, u32[]{:S(2)}) collective-permute-start(bf16[512,768]{1,0:T(8,128)(2,1)} %tokens.1), channel_id=1, source_target_pairs={{0,2},{1,3},{2,0},{3,1},{4,6},{5,7},{6,4},{7,5},{8,10},{9,11},{10,... | collective-permute-start | bytes 2359304 | tf_op jit(solution)/shard_map/ppermute | solution.py:65
  3.8 1.6 %shard_map.154.first = bf16[768,128]{1,0:T(8,128)(2,1)S(1)} custom-call(s32[1]{0:T(128)} %bitcast.1.base.refs_1_, s32[1,128]{1,0:T(1,128)} %bitcast.44, bf16[512,768]{1,0:T(8,128)(2,1)} %tokens.1), custom_call_target="tpu_custom_call" | custom-call | tf_op jit(solution)/shard_map/pallas_call | solution.py:38
  5.3 2.7 %collective-permute-start.12 = (bf16[768,128]{1,0:T(8,128)(2,1)S(1)}, bf16[768,128]{1,0:T(8,128)(2,1)S(1)}, u32[]{:S(2)}, u32[]{:S(2)}) collective-permute-start(bf16[768,128]{1,0:T(8,128)(2,1)S(1)} %shard_map.154.first), channel_id=1, source_target_pairs={{0,16},{4,20},{8,24},{12,28},{16,0},{20,4},{24,8},{28,12},{1,17},{... | collective-permute-start | bytes 589832 | tf_op jit(solution)/shard_map/ppermute | solution.py:65
  10.3 1.7 %copy-done.4 = bf16[384,3072]{1,0:T(8,128)(2,1)S(1)} copy-done((bf16[384,3072]{1,0:T(8,128)(2,1)S(1)}, bf16[384,3072]{1,0:T(8,128)(2,1)}, u32[]{:S(2)}) %copy-start.4) | copy-done | bytes 2359320
  11.9 6.2 %shard_map.147 = (f32[512,1152]{1,0:T(8,128)S(1)}, f32[512,1]{1,0:T(8,128)S(1)}, bf16[768,384]{1,0:T(8,128)(2,1)S(1)}, bf16[768,384]{1,0:T(8,128)(2,1)S(1)}, bf1...) custom-call(s32[1]{0:T(128)} %bitcast.refs_0_, ...), custom_call_target="tpu_custom_call" | custom-call | tf_op jit(solution)/shard_map/pallas_call | solution.py:38
  19.4 2.6 %collective-permute-done.2.source = bf16[512,768]{1,0:T(8,128)(2,1)S(1)} collective-permute-done((bf16[512,768]{1,0:T(8,128)(2,1)}, bf16[512,768]{1,0:T(8,128)(2,1)S(1)}, u32[]{:S(2)}, u32[]{:S(2)}) %collective-permute-start.2) | collective-permute-done | bytes 786464 | tf_op jit(solution)/shard_map/ppermute | solution.py:65
  22.3 1.8 %collective-permute-start.9 = (bf16[768,384]{1,0:T(8,128)(2,1)}, bf16[768,384]{1,0:T(8,128)(2,1)S(1)}, u32[]{:S(2)}, u32[]{:S(2)}) collective-permute-start(bf16[768,384]{1,0:T(8,128)(2,1)} %get-tuple-element.61), channel_id=1, source_target_pairs={{0,2},{1,3},{2,0},{3,1},{4,6},{5,7},{6,4},{7,5},{8,10},{9,11},{10,... | collective-permute-start | bytes 1769480 | tf_op jit(solution)/shard_map/ppermute | solution.py:65
  24.2 1.6 %collective-permute-start.13 = (bf16[768,128]{1,0:T(8,128)(2,1)S(1)}, bf16[768,128]{1,0:T(8,128)(2,1)S(1)}, u32[]{:S(2)}, u32[]{:S(2)}) collective-permute-start(bf16[768,128]{1,0:T(8,128)(2,1)S(1)} %shard_map.155.first), channel_id=1, source_target_pairs={{0,8},{4,12},{8,0},{12,4},{16,24},{20,28},{24,16},{28,20},{1,9},{5... | collective-permute-start | bytes 589832 | tf_op jit(solution)/shard_map/ppermute | solution.py:65
  30.8 2.2 %shard_map.152 = (bf16[768,512]{1,0:T(8,128)(2,1)S(1)}, bf16[768,512]{1,0:T(8,128)(2,1)S(1)}, bf16[768,512]{1,0:T(8,128)(2,1)}, bf16[768,256]{1,0:T(8,128)(2,1)}) custom-call(s32[1]{0:T(128)} %bitcast.refs_0_, s32[1]{0:T(128)} %bitcast.1.base.refs_1_, bf16[2,768,384]{2,1,0:T(8,128)(2,1)S(1)} %get-tuple-element.40.refs_2_, ...), custom_call_target="tpu_custom_call" | custom-call | flops 10000000000 | tf_op jit(solution)/shard_map/pallas_call | solution.py:38
  34.7 3.0 %collective-permute-done.16.refs_2_ = bf16[384,128]{1,0:T(8,128)(2,1)S(1)} collective-permute-done((bf16[384,128]{1,0:T(8,128)(2,1)S(1)}, bf16[384,128]{1,0:T(8,128)(2,1)S(1)}, u32[]{:S(2)}, u32[]{:S(2)}) %collective-permute-start.16) | collective-permute-done | bytes 98336 | tf_op jit(solution)/shard_map/ppermute | solution.py:71
  41.3 2.8 %collective-permute-done.17.other = bf16[400,128]{1,0:T(8,128)(2,1)S(1)} collective-permute-done((bf16[400,128]{1,0:T(8,128)(2,1)S(1)}, bf16[400,128]{1,0:T(8,128)(2,1)S(1)}, u32[]{:S(2)}, u32[]{:S(2)}) %collective-permute-start.17) | collective-permute-done | bytes 102432 | tf_op jit(solution)/shard_map/ppermute | solution.py:65
  44.1 2.5 %collective-permute-start.18 = (bf16[400,128]{1,0:T(8,128)(2,1)S(1)}, bf16[400,128]{1,0:T(8,128)(2,1)S(1)}, u32[]{:S(2)}, u32[]{:S(2)}) collective-permute-start(bf16[400,128]{1,0:T(8,128)(2,1)S(1)} %shard_map.159.own), channel_id=1, source_target_pairs={{0,8},{4,12},{8,0},{12,4},{16,24},{20,28},{24,16},{28,20},{1,9},{5... | collective-permute-start | bytes 307208 | tf_op jit(solution)/shard_map/ppermute | solution.py:65
  49.3 3.6 %collective-permute-start.19 = (bf16[400,128]{1,0:T(8,128)(2,1)S(1)}, bf16[400,128]{1,0:T(8,128)(2,1)S(1)}, u32[]{:S(2)}, u32[]{:S(2)}) collective-permute-start(bf16[400,128]{1,0:T(8,128)(2,1)S(1)} %shard_map.160.own), channel_id=1, source_target_pairs={{0,16},{4,20},{8,24},{12,28},{16,0},{20,4},{24,8},{28,12},{1,17},{... | collective-permute-start | bytes 307208 | tf_op jit(solution)/shard_map/ppermute | solution.py:65
  52.9 6.2 %collective-permute-start.4 = (bf16[768,512]{1,0:T(8,128)(2,1)}, bf16[768,512]{1,0:T(8,128)(2,1)}, u32[]{:S(2)}, u32[]{:S(2)}) collective-permute-start(bf16[768,512]{1,0:T(8,128)(2,1)} %get-tuple-element.54), channel_id=1, source_target_pairs={{0,4},{4,8},{8,12},{12,16},{16,20},{20,24},{24,28},{1,5},{5,9},{9,... | collective-permute-start | bytes 2359304 | tf_op jit(solution)/shard_map/ppermute | solution.py:71
  59.8 4.1 %collective-permute-done.21.far = bf16[384,128]{1,0:T(8,128)(2,1)S(1)} collective-permute-done((bf16[384,128]{1,0:T(8,128)(2,1)S(1)}, bf16[384,128]{1,0:T(8,128)(2,1)S(1)}, u32[]{:S(2)}, u32[]{:S(2)}) %collective-permute-start.21) | collective-permute-done | bytes 98336 | tf_op jit(solution)/shard_map/ppermute | solution.py:65
  63.9 2.8 %shard_map.162 = (bf16[2048,768]{1,0:T(8,128)(2,1)S(1)}, f32[768,128]{1,0:T(8,128)S(1)}) custom-call(s32[1]{0:T(128)} %bitcast.12.start, bf16[4008,768]{1,0:T(8,128)(2,1)} %bitcast.48, bf16[768,384]{1,0:T(8,128)(2,1)} %copy-done.2, bf16[4008,768]{1,0:T(8,128)(2,1)} %bitcast.49, bf16[768,128]{1,0:T(8,128)(2,1)S(1)} %shard_map.157.refs_1_.tokens, ...), custom_call_target="tpu_custom_call" | custom-call | tf_op jit(solution)/shard_map/pallas_call | solution.py:499
  69.5 2.7 %shard_map.165.kept = bf16[2048,128]{1,0:T(8,128)(2,1)S(1)} custom-call(s32[1]{0:T(128)} %bitcast.10.start, bf16[4008,768]{1,0:T(8,128)(2,1)} %bitcast.50, bf16[768,128]{1,0:T(8,128)(2,1)S(1)} %get-tuple-element.66.scaled, bf16[2048,128]{1,0:T(8,128)(2,1)S(1)} %shard_map.164.refs_0_), custom_call_target="tpu_custom_call" | custom-call | tf_op jit(solution)/shard_map/pallas_call | solution.py:541
  75.3 3.9 %shard_map.153.refs_0_ = bf16[512,384]{1,0:T(8,128)(2,1)S(1)} custom-call(s32[1]{0:T(128)} %bitcast.6.place, s32[1,512]{1,0:T(1,128)S(1)} %get-tuple-element.55.low, bf16[384,512]{1,0:T(8,128)(2,1)S(1)} %copy-done.9, bf16[768,512]{1,0:T(8,128)(2,1)S(1)} %copy-done.11, bf16[768,512]{1,0:T(8,128)(2,1)} %collective-permute-done.4.refs_1_, ...), custom_call_target="tpu_custom_call" | custom-call | flops 30000001024 | tf_op jit(solution)/shard_map/pallas_call | solution.py:38
  79.8 2.6 %collective-permute-done.24.came = bf16[1024,128]{1,0:T(8,128)(2,1)S(1)} collective-permute-done((bf16[1024,128]{1,0:T(8,128)(2,1)S(1)}, bf16[1024,128]{1,0:T(8,128)(2,1)S(1)}, u32[]{:S(2)}, u32[]{:S(2)}) %collective-permute-start.24) | collective-permute-done | bytes 262176 | tf_op jit(solution)/shard_map/ppermute | solution.py:65
  84.1 2.1 %collective-permute-done.25 = f32[1,128]{1,0:T(1,128)S(1)} collective-permute-done((f32[1,128]{1,0:T(1,128)S(1)}, f32[1,128]{1,0:T(1,128)S(1)}, u32[]{:S(2)}, u32[]{:S(2)}) %collective-permute-start.25) | collective-permute-done | bytes 544 | tf_op jit(solution)/shard_map/ppermute | solution.py:65
  87.8 1.9 %collective-permute-done.26 = f32[1,128]{1,0:T(1,128)S(1)} collective-permute-done((f32[1,128]{1,0:T(1,128)S(1)}, f32[1,128]{1,0:T(1,128)S(1)}, u32[]{:S(2)}, u32[]{:S(2)}) %collective-permute-start.26) | collective-permute-done | bytes 544 | tf_op jit(solution)/shard_map/ppermute | solution.py:65
  89.8 2.7 %collective-permute-start.27 = (f32[1,128]{1,0:T(1,128)S(1)}, f32[1,128]{1,0:T(1,128)S(1)}, u32[]{:S(2)}, u32[]{:S(2)}) collective-permute-start(f32[1,128]{1,0:T(1,128)S(1)} %max.21), channel_id=1, source_target_pairs={{0,16},{4,20},{8,24},{12,28},{16,0},{20,4},{24,8},{28,12},{1,17},{... | collective-permute-start | bytes 1544 | tf_op jit(solution)/shard_map/ppermute | solution.py:65
  96.1 1.6 %collective-permute-done.28 = f32[2,128]{1,0:T(2,128)S(1)} collective-permute-done((f32[2,128]{1,0:T(2,128)S(1)}, f32[2,128]{1,0:T(2,128)S(1)}, u32[]{:S(2)}, u32[]{:S(2)}) %collective-permute-start.28) | collective-permute-done | bytes 1056 | tf_op jit(solution)/shard_map/ppermute | solution.py:65
  97.9 1.6 %add_convert_fusion = bf16[512,768]{1,0:T(8,128)(2,1)} fusion(bf16[512,768]{1,0:T(8,128)(2,1)S(1)} %convolution_convert_fusion.1, bf16[512,768]{1,0:T(8,128)(2,1)S(1)} %convolution_convert_fusion.2, bf16[512,768]{1,0:T(8,128)(2,1)S(1)} %convolution_convert_fusion.3, bf16[512,768]{1,0:T(8,128)(2,1)S(1)} %copy-done, ...), kind=kOutput, calls=%fused_computation | convolution fusion | flops 306315264 | bytes 4915200 | tf_op jit(solution)/shard_map/dot_general | solution.py:85
  (97 shorter events, 32.3 us)
Async XLA Ops:
  0.6 9.6 %collective-permute-start.1 = (bf16[512,768]{1,0:T(8,128)(2,1)}, bf16[512,768]{1,0:T(8,128)(2,1)S(1)}, u32[]{:S(2)}, u32[]{:S(2)}) collective-permute-start(bf16[512,768]{1,0:T(8,128)(2,1)} %tokens.1), channel_id=1, source_target_pairs={{0,1},{1,0},{2,3},{3,2},{4,5},{5,4},{6,7},{7,6},{8,9},{9,8},{10,11... | collective-permute-start | bytes 2359304 | tf_op jit(solution)/shard_map/ppermute | solution.py:65
  1.2 20.9 %collective-permute-start.2 = (bf16[512,768]{1,0:T(8,128)(2,1)}, bf16[512,768]{1,0:T(8,128)(2,1)S(1)}, u32[]{:S(2)}, u32[]{:S(2)}) collective-permute-start(bf16[512,768]{1,0:T(8,128)(2,1)} %tokens.1), channel_id=1, source_target_pairs={{0,2},{1,3},{2,0},{3,1},{4,6},{5,7},{6,4},{7,5},{8,10},{9,11},{10,... | collective-permute-start | bytes 2359304 | tf_op jit(solution)/shard_map/ppermute | solution.py:65
  5.3 18.8 %collective-permute-start.12 = (bf16[768,128]{1,0:T(8,128)(2,1)S(1)}, bf16[768,128]{1,0:T(8,128)(2,1)S(1)}, u32[]{:S(2)}, u32[]{:S(2)}) collective-permute-start(bf16[768,128]{1,0:T(8,128)(2,1)S(1)} %shard_map.154.first), channel_id=1, source_target_pairs={{0,16},{4,20},{8,24},{12,28},{16,0},{20,4},{24,8},{28,12},{1,17},{... | collective-permute-start | bytes 589832 | tf_op jit(solution)/shard_map/ppermute | solution.py:65
  22.2 5.0 %collective-permute-start.3 = (bf16[512,768]{1,0:T(8,128)(2,1)S(1)}, bf16[512,768]{1,0:T(8,128)(2,1)S(1)}, u32[]{:S(2)}, u32[]{:S(2)}) collective-permute-start(bf16[512,768]{1,0:T(8,128)(2,1)S(1)} %get-tuple-element.43), channel_id=1, source_target_pairs={{0,1},{1,0},{2,3},{3,2},{4,5},{5,4},{6,7},{7,6},{8,9},{9,8},{10,11... | collective-permute-start | bytes 2359304 | tf_op jit(solution)/shard_map/ppermute | solution.py:65
  22.3 19.0 %collective-permute-start.9 = (bf16[768,384]{1,0:T(8,128)(2,1)}, bf16[768,384]{1,0:T(8,128)(2,1)S(1)}, u32[]{:S(2)}, u32[]{:S(2)}) collective-permute-start(bf16[768,384]{1,0:T(8,128)(2,1)} %get-tuple-element.61), channel_id=1, source_target_pairs={{0,2},{1,3},{2,0},{3,1},{4,6},{5,7},{6,4},{7,5},{8,10},{9,11},{10,... | collective-permute-start | bytes 1769480 | tf_op jit(solution)/shard_map/ppermute | solution.py:65
  24.2 10.2 %collective-permute-start.13 = (bf16[768,128]{1,0:T(8,128)(2,1)S(1)}, bf16[768,128]{1,0:T(8,128)(2,1)S(1)}, u32[]{:S(2)}, u32[]{:S(2)}) collective-permute-start(bf16[768,128]{1,0:T(8,128)(2,1)S(1)} %shard_map.155.first), channel_id=1, source_target_pairs={{0,8},{4,12},{8,0},{12,4},{16,24},{20,28},{24,16},{28,20},{1,9},{5... | collective-permute-start | bytes 589832 | tf_op jit(solution)/shard_map/ppermute | solution.py:65
  28.2 6.5 %collective-permute-start.15 = (bf16[384,128]{1,0:T(8,128)(2,1)S(1)}, bf16[384,128]{1,0:T(8,128)(2,1)S(1)}, u32[]{:S(2)}, u32[]{:S(2)}) collective-permute-start(bf16[384,128]{1,0:T(8,128)(2,1)S(1)} %get-tuple-element.53.refs_10_.refs_0_), channel_id=1, source_target_pairs={{4,0},{8,4},{12,8},{16,12},{20,16},{24,20},{28,24},{5,1},{9,5},{13... | collective-permute-start | bytes 294920 | tf_op jit(solution)/shard_map/ppermute | solution.py:71
  29.5 8.2 %collective-permute-start.16 = (bf16[384,128]{1,0:T(8,128)(2,1)S(1)}, bf16[384,128]{1,0:T(8,128)(2,1)S(1)}, u32[]{:S(2)}, u32[]{:S(2)}) collective-permute-start(bf16[384,128]{1,0:T(8,128)(2,1)S(1)} %get-tuple-element.53.refs_10_.refs_0_), channel_id=1, source_target_pairs={{8,0},{12,4},{16,8},{20,12},{24,16},{28,20},{9,1},{13,5},{17,9},{2... | collective-permute-start | bytes 294920 | tf_op jit(solution)/shard_map/ppermute | solution.py:71
  33.0 11.1 %collective-permute-start.5 = (bf16[768,256]{1,0:T(8,128)(2,1)}, bf16[768,256]{1,0:T(8,128)(2,1)}, u32[]{:S(2)}, u32[]{:S(2)}) collective-permute-start(bf16[768,256]{1,0:T(8,128)(2,1)} %get-tuple-element.58), channel_id=1, source_target_pairs={{20,28},{21,29},{22,30},{23,31}} | collective-permute-start | bytes 1179656 | tf_op jit(solution)/shard_map/ppermute | solution.py:701
  38.9 5.1 %collective-permute-start.17 = (bf16[400,128]{1,0:T(8,128)(2,1)S(1)}, bf16[400,128]{1,0:T(8,128)(2,1)S(1)}, u32[]{:S(2)}, u32[]{:S(2)}) collective-permute-start(bf16[400,128]{1,0:T(8,128)(2,1)S(1)} %shard_map.158.own), channel_id=1, source_target_pairs={{0,4},{4,0},{8,12},{12,8},{16,20},{20,16},{24,28},{28,24},{1,5},{5... | collective-permute-start | bytes 307208 | tf_op jit(solution)/shard_map/ppermute | solution.py:65
  40.1 19.0 %collective-permute-start.11 = (bf16[768,384]{1,0:T(8,128)(2,1)}, bf16[768,384]{1,0:T(8,128)(2,1)S(1)}, u32[]{:S(2)}, u32[]{:S(2)}) collective-permute-start(bf16[768,384]{1,0:T(8,128)(2,1)} %get-tuple-element.62), channel_id=1, source_target_pairs={{0,3},{1,2},{2,1},{3,0},{4,7},{5,6},{6,5},{7,4},{8,11},{9,10},{10,... | collective-permute-start | bytes 1769480 | tf_op jit(solution)/shard_map/ppermute | solution.py:65
  40.1 8.7 %collective-permute-start.14 = (bf16[768,128]{1,0:T(8,128)(2,1)S(1)}, bf16[768,128]{1,0:T(8,128)(2,1)S(1)}, u32[]{:S(2)}, u32[]{:S(2)}) collective-permute-start(bf16[768,128]{1,0:T(8,128)(2,1)S(1)} %shard_map.156.first.refs_3_), channel_id=1, source_target_pairs={{0,4},{4,0},{8,12},{12,8},{16,20},{20,16},{24,28},{28,24},{1,5},{5... | collective-permute-start | bytes 589832 | tf_op jit(solution)/shard_map/ppermute | solution.py:65
  44.1 5.1 %collective-permute-start.18 = (bf16[400,128]{1,0:T(8,128)(2,1)S(1)}, bf16[400,128]{1,0:T(8,128)(2,1)S(1)}, u32[]{:S(2)}, u32[]{:S(2)}) collective-permute-start(bf16[400,128]{1,0:T(8,128)(2,1)S(1)} %shard_map.159.own), channel_id=1, source_target_pairs={{0,8},{4,12},{8,0},{12,4},{16,24},{20,28},{24,16},{28,20},{1,9},{5... | collective-permute-start | bytes 307208 | tf_op jit(solution)/shard_map/ppermute | solution.py:65
  47.8 16.1 %collective-permute-start.7 = (bf16[768,384]{1,0:T(8,128)(2,1)}, bf16[768,384]{1,0:T(8,128)(2,1)S(1)}, u32[]{:S(2)}, u32[]{:S(2)}) collective-permute-start(bf16[768,384]{1,0:T(8,128)(2,1)} %copy-done.7), channel_id=1, source_target_pairs={{0,1},{1,0},{2,3},{3,2},{4,5},{5,4},{6,7},{7,6},{8,9},{9,8},{10,11... | collective-permute-start | bytes 1769480 | tf_op jit(solution)/shard_map/ppermute | solution.py:65
  49.3 9.8 %collective-permute-start.19 = (bf16[400,128]{1,0:T(8,128)(2,1)S(1)}, bf16[400,128]{1,0:T(8,128)(2,1)S(1)}, u32[]{:S(2)}, u32[]{:S(2)}) collective-permute-start(bf16[400,128]{1,0:T(8,128)(2,1)S(1)} %shard_map.160.own), channel_id=1, source_target_pairs={{0,16},{4,20},{8,24},{12,28},{16,0},{20,4},{24,8},{28,12},{1,17},{... | collective-permute-start | bytes 307208 | tf_op jit(solution)/shard_map/ppermute | solution.py:65
  52.9 22.4 %collective-permute-start.4 = (bf16[768,512]{1,0:T(8,128)(2,1)}, bf16[768,512]{1,0:T(8,128)(2,1)}, u32[]{:S(2)}, u32[]{:S(2)}) collective-permute-start(bf16[768,512]{1,0:T(8,128)(2,1)} %get-tuple-element.54), channel_id=1, source_target_pairs={{0,4},{4,8},{8,12},{12,16},{16,20},{20,24},{24,28},{1,5},{5,9},{9,... | collective-permute-start | bytes 2359304 | tf_op jit(solution)/shard_map/ppermute | solution.py:71
  59.2 4.7 %collective-permute-start.21 = (bf16[384,128]{1,0:T(8,128)(2,1)S(1)}, bf16[384,128]{1,0:T(8,128)(2,1)S(1)}, u32[]{:S(2)}, u32[]{:S(2)}) collective-permute-start(bf16[384,128]{1,0:T(8,128)(2,1)S(1)} %shard_map.161.own), channel_id=1, source_target_pairs={{0,2},{1,3},{2,0},{3,1},{4,6},{5,7},{6,4},{7,5},{8,10},{9,11},{10,... | collective-permute-start | bytes 294920 | tf_op jit(solution)/shard_map/ppermute | solution.py:65
  59.8 4.1 %collective-permute-start.20 = (bf16[384,128]{1,0:T(8,128)(2,1)S(1)}, bf16[384,128]{1,0:T(8,128)(2,1)S(1)}, u32[]{:S(2)}, u32[]{:S(2)}) collective-permute-start(bf16[384,128]{1,0:T(8,128)(2,1)S(1)} %shard_map.161.own), channel_id=1, source_target_pairs={{0,1},{1,0},{2,3},{3,2},{4,5},{5,4},{6,7},{7,6},{8,9},{9,8},{10,11... | collective-permute-start | bytes 294920 | tf_op jit(solution)/shard_map/ppermute | solution.py:65
  73.4 9.1 %collective-permute-start.24 = (bf16[1024,128]{1,0:T(8,128)(2,1)S(1)}, bf16[1024,128]{1,0:T(8,128)(2,1)S(1)}, u32[]{:S(2)}, u32[]{:S(2)}) collective-permute-start(bf16[1024,128]{1,0:T(8,128)(2,1)S(1)} %get-tuple-element.70), channel_id=1, source_target_pairs={{0,2},{1,3},{2,0},{3,1},{4,6},{5,7},{6,4},{7,5},{8,10},{9,11},{10,... | collective-permute-start | bytes 786440 | tf_op jit(solution)/shard_map/ppermute | solution.py:65
  79.2 13.2 %collective-permute-start.8 = (bf16[512,384]{1,0:T(8,128)(2,1)S(1)}, bf16[512,384]{1,0:T(8,128)(2,1)S(1)}, u32[]{:S(2)}, u32[]{:S(2)}) collective-permute-start(bf16[512,384]{1,0:T(8,128)(2,1)S(1)} %shard_map.153.refs_0_), channel_id=1, source_target_pairs={{0,2},{1,3},{2,0},{3,1},{4,6},{5,7},{6,4},{7,5},{8,10},{9,11},{10,... | collective-permute-start | bytes 1179656 | tf_op jit(solution)/shard_map/ppermute | solution.py:65
  82.6 3.6 %collective-permute-start.25 = (f32[1,128]{1,0:T(1,128)S(1)}, f32[1,128]{1,0:T(1,128)S(1)}, u32[]{:S(2)}, u32[]{:S(2)}) collective-permute-start(f32[1,128]{1,0:T(1,128)S(1)} %shard_map.167), channel_id=1, source_target_pairs={{0,4},{4,0},{8,12},{12,8},{16,20},{20,16},{24,28},{28,24},{1,5},{5... | collective-permute-start | bytes 1544 | tf_op jit(solution)/shard_map/ppermute | solution.py:65
  84.1 11.5 %collective-permute-start.6 = (bf16[512,384]{1,0:T(8,128)(2,1)S(1)}, bf16[512,384]{1,0:T(8,128)(2,1)S(1)}, u32[]{:S(2)}, u32[]{:S(2)}) collective-permute-start(bf16[512,384]{1,0:T(8,128)(2,1)S(1)} %shard_map.153.refs_0_), channel_id=1, source_target_pairs={{0,1},{1,0},{2,3},{3,2},{4,5},{5,4},{6,7},{7,6},{8,9},{9,8},{10,11... | collective-permute-start | bytes 1179656 | tf_op jit(solution)/shard_map/ppermute | solution.py:65
  89.8 4.4 %collective-permute-start.27 = (f32[1,128]{1,0:T(1,128)S(1)}, f32[1,128]{1,0:T(1,128)S(1)}, u32[]{:S(2)}, u32[]{:S(2)}) collective-permute-start(f32[1,128]{1,0:T(1,128)S(1)} %max.21), channel_id=1, source_target_pairs={{0,16},{4,20},{8,24},{12,28},{16,0},{20,4},{24,8},{28,12},{1,17},{... | collective-permute-start | bytes 1544 | tf_op jit(solution)/shard_map/ppermute | solution.py:65
  93.1 4.8 %collective-permute-start.10 = (bf16[512,384]{1,0:T(8,128)(2,1)S(1)}, bf16[512,384]{1,0:T(8,128)(2,1)S(1)}, u32[]{:S(2)}, u32[]{:S(2)}) collective-permute-start(bf16[512,384]{1,0:T(8,128)(2,1)S(1)} %collective-permute-done.8.refs_0_), channel_id=1, source_target_pairs={{0,1},{1,0},{2,3},{3,2},{4,5},{5,4},{6,7},{7,6},{8,9},{9,8},{10,11... | collective-permute-start | bytes 1179656 | tf_op jit(solution)/shard_map/ppermute | solution.py:65
  (17 other events, 92.4 us)

commit v6 on v5

--- a/solution.py
+++ b/solution.py
@@ -568,6 +568,11 @@
     out[...] = jnp.max(kept[...] + came[...].astype(F32), axis=0, keepdims=True)
 
 
+def join_body(pair, other, *refs):
+    refs[-1][0:1, :] = jnp.maximum(pair[0:1, :], other[0:1, :])
+    refs[-1][1:2, :] = pair[1:2, :] + other[1:2, :]
+
+
 def pair_body(first, second, *refs):
     refs[-1][0:1, :] = first[...]
     refs[-1][1:2, :] = second[...]
@@ -632,11 +637,6 @@
         blocked=True,
     )
     last_gain = final_gain[:, None]
-    relayed, far = call(
-        twice_body, [struct(far.shape, BF16)] * 2, [], [far], (sums[1], cosine, last_gain)
-    )
-    pieces = pieces[:2] + [far, swap(relayed, "tp", 1)]
-
     asked = request_slots[None, :]
     inside = asked - base
     (own_tokens,) = call(
@@ -644,22 +644,34 @@
         blocked=True,
     )
     all_tokens = [own_tokens]
+    all_tokens += call(
+        add_body,
+        [struct(own_tokens.shape, BF16)],
+        [],
+        [own_tokens, swap(own_tokens, "seq", n_seq // 2)],
+        sums[1:2],
+    )
+    relayed, far = call(
+        twice_body, [struct(far.shape, BF16)] * 2, [], [far], (sums[1], cosine, last_gain, all_tokens[1])
+    )
+    pieces = pieces[:2] + [far, swap(relayed, "tp", 1)]
+
     *kv_sums, query_sums, query_squares = project(
-        (2,), mine, gain, pieces[2:3], [far_weights], sums, None, (), length=10
+        (2,), mine, gain, pieces[2:3], [far_weights], sums, None, (), length=4
     )
     ending = (base.reshape(1), cosine, sine, asked)
     query, own_query = project(
         (3,), mine, gain, pieces[3:], [last_query], (query_sums, query_squares), ending, (), 2, (2,)
     )
     asking = [own_query] + [shifted(own_query, "seq", -by) for by in range(1, span + 1)]
-    bit = n_seq // 2
+    bit = n_seq // 4
     while bit:
         all_tokens += call(
             add_body,
             [struct(own_tokens.shape, BF16)],
             [],
             [all_tokens[-1], swap(all_tokens[-1], "seq", bit)],
-            sums[1:2] if len(all_tokens) == 1 else (own_query,),
+            (own_query,),
         )
         bit //= 2
     asked_kv, own_kv, kv, kv_half = project(
@@ -722,7 +734,8 @@
         bit *= 2
         kept_rows = width + LEVEL_ROWS if bit < n_seq else width
         mixed = combine(flip, mixed, other, kept_rows, after)
-    _, near_mixed, far_mixed, last_mixed = spread(mixed)
+    far_mixed = swap(mixed, "tp", 2)
+    near_mixed = swap(mixed, "tp", 1)
 
     core = tp_index & 1
     side = tp_index >> 1
@@ -734,6 +747,10 @@
     held, field = begin_rows(
         away, vocab, own_weight, all_tokens[-1], mixed, near_mixed, w_parts[1]
     )
+    relayed, far_mixed = call(
+        twice_body, [struct(far_mixed.shape, BF16)] * 2, [], [far_mixed], (field,)
+    )
+    last_mixed = swap(relayed, "tp", 1)
     squares, scaled, again = call(
         rows_body,
         [struct((1, requests), F32)] + [struct(own_tokens.shape, BF16)] * 2,
@@ -774,16 +791,17 @@
     (pair,) = call(
         pair_body, [struct((2, requests), F32)], [], [best, squares], attended[2:3]
     )
-    for bit in (2, 1):
-        other = swap(pair, "tp", bit)
-        pair = jnp.stack([jnp.maximum(pair[0], other[0]), pair[1] + other[1]])
+    other = swap(pair, "tp", 2)
+    pair = jnp.stack([jnp.maximum(pair[0], other[0]), pair[1] + other[1]])
+    summed = sum(
+        mm_last(part, w).astype(BF16).astype(F32) for part, w in zip(attended, w_parts)
+    )
+    hidden = (tokens.astype(F32) + summed).astype(BF16)
+    (pair,) = call(
+        join_body, [struct((2, requests), F32)], [], [pair, swap(pair, "tp", 1)], (hidden,)
+    )
     hidden_norm = jnp.sqrt(pair[1] / D + EPS)
     top_logit = pair[0] / hidden_norm * (1.0 / SHRINK)
-
-    summed = sum(
-        mm_last(part, w).astype(BF16).astype(F32) for part, w in zip(attended, w_parts)
-    )
-    hidden = (tokens.astype(F32) + summed).astype(BF16)
     return (kv_cache, hidden, hidden_norm, top_logit)
 
 

time: 101 us -> 101 us (level)
  starting transfers between devices: 36.8 us -> 39 us
  waiting for transfers between devices: 24 us -> 22.1 us
    ppermute x25, waiting for transfers between devices: 19.3 us -> 15.5 us  [swap(): return lax.ppermute(array, axis, [(i, i ^ bit) for i in range(count)])]
    ppermute x25, starting transfers between devices: 26.6 us -> 28.9 us  [swap(): return lax.ppermute(array, axis, [(i, i ^ bit) for i in range(count)])]
    ppermute x3, waiting for transfers between devices: 4.7 us -> 6.68 us  [shifted(): return lax.ppermute(array, axis, pairs)]
    unnamed x24 -> x30, local copies, waits for them, and re-layouts: 1.71 us -> 2.59 us
    pallas_call x20 -> x22, Pallas kernels: 22.6 us -> 22.6 us  [call(): pl.pallas_call(body, grid=(1,) if blocked else (), out_shape=outs, in_spe...]
  transfers between devices with their start and end apart: 29 -> 29, of which waited for: 12 -> 15; matrix products, arithmetic and copies ran while one was open for 7% -> 6% of each run, Pallas kernels for 28% -> 28%
where the time goes in v6:
time: 101 us; the launch traced here: 100 us
  starting transfers between devices  39 us (39%)
  Pallas kernels  28.1 us (28%)
  waiting for transfers between devices  22.1 us (22%)
  local copies, waits for them, and re-layouts  5.11 us (5%)
  matrix products  2.5 us (2%)
  between operations  1.69 us (2%)
  other arithmetic  1.44 us (1%)
    ppermute x25, starting transfers between devices, swap(): return lax.ppermute(array, axis, [(i, i ^ bit) for i in range(count)])  28.9 us
    pallas_call x22, Pallas kernels, call(): pl.pallas_call(body, grid=(1,) if blocked else (), out_shape=outs, in_spe...  22.6 us
    ppermute x25, waiting for transfers between devices, swap(): return lax.ppermute(array, axis, [(i, i ^ bit) for i in range(count)])  15.5 us
    ppermute x3, starting transfers between devices, shifted(): return lax.ppermute(array, axis, pairs)  9.34 us
    ppermute x3, waiting for transfers between devices, shifted(): return lax.ppermute(array, axis, pairs)  6.68 us
    pallas_call x1, Pallas kernels, begin_rows(): pl.pallas_call(partial(begin_body, limit), grid=(1,), out_shape=[struct((...  2.77 us
    pallas_call x1, Pallas kernels, half_logits(): pl.pallas_call(partial(logits_body, limit), grid_spec=pltpu.PrefetchScala...  2.71 us
    unnamed x30, local copies, waits for them, and re-layouts  2.59 us
  transfers between devices with their start and end apart: 29, of which 15 were waited for; matrix products, arithmetic and copies ran while one was open for 6% of the time, Pallas kernels for 28%

profile of v6, /device:TPU:0, one launch (start us, length us, event | category | flops | bytes accessed | tf_op | source)
XLA Modules:
  0.0 100.0 jit_solution(7069280513256798089)
XLA Ops:
  1.2 2.6 %collective-permute-start.2 = (bf16[512,768]{1,0:T(8,128)(2,1)}, bf16[512,768]{1,0:T(8,128)(2,1)S(1)}, u32[]{:S(2)}, u32[]{:S(2)}) collective-permute-start(bf16[512,768]{1,0:T(8,128)(2,1)} %tokens.1), channel_id=1, source_target_pairs={{0,2},{1,3},{2,0},{3,1},{4,6},{5,7},{6,4},{7,5},{8,10},{9,11},{10,... | collective-permute-start | bytes 2359304 | tf_op jit(solution)/shard_map/ppermute | solution.py:65
  3.8 1.6 %shard_map.149.first = bf16[768,128]{1,0:T(8,128)(2,1)S(1)} custom-call(s32[1]{0:T(128)} %bitcast.1.base.refs_1_, s32[1,128]{1,0:T(1,128)} %bitcast.44, bf16[512,768]{1,0:T(8,128)(2,1)} %tokens.1), custom_call_target="tpu_custom_call" | custom-call | tf_op jit(solution)/shard_map/pallas_call | solution.py:38
  5.3 2.7 %collective-permute-start.3 = (bf16[768,128]{1,0:T(8,128)(2,1)S(1)}, bf16[768,128]{1,0:T(8,128)(2,1)S(1)}, u32[]{:S(2)}, u32[]{:S(2)}) collective-permute-start(bf16[768,128]{1,0:T(8,128)(2,1)S(1)} %shard_map.149.first), channel_id=1, source_target_pairs={{0,16},{4,20},{8,24},{12,28},{16,0},{20,4},{24,8},{28,12},{1,17},{... | collective-permute-start | bytes 589832 | tf_op jit(solution)/shard_map/ppermute | solution.py:65
  9.6 1.8 %copy-done.5 = bf16[384,3072]{1,0:T(8,128)(2,1)S(1)} copy-done((bf16[384,3072]{1,0:T(8,128)(2,1)S(1)}, bf16[384,3072]{1,0:T(8,128)(2,1)}, u32[]{:S(2)}) %copy-start.5) | copy-done | bytes 2359320
  11.4 6.2 %shard_map.147 = (f32[512,1152]{1,0:T(8,128)S(1)}, f32[512,1]{1,0:T(8,128)S(1)}, bf16[768,384]{1,0:T(8,128)(2,1)S(1)}, bf16[768,384]{1,0:T(8,128)(2,1)S(1)}, bf1...) custom-call(s32[1]{0:T(128)} %bitcast.refs_0_, ...), custom_call_target="tpu_custom_call" | custom-call | tf_op jit(solution)/shard_map/pallas_call | solution.py:38
  19.0 3.1 %collective-permute-done.2.source = bf16[512,768]{1,0:T(8,128)(2,1)S(1)} collective-permute-done((bf16[512,768]{1,0:T(8,128)(2,1)}, bf16[512,768]{1,0:T(8,128)(2,1)S(1)}, u32[]{:S(2)}, u32[]{:S(2)}) %collective-permute-start.2) | collective-permute-done | bytes 786464 | tf_op jit(solution)/shard_map/ppermute | solution.py:65
  22.3 1.9 %collective-permute-start.13 = (bf16[768,128]{1,0:T(8,128)(2,1)S(1)}, bf16[768,128]{1,0:T(8,128)(2,1)S(1)}, u32[]{:S(2)}, u32[]{:S(2)}) collective-permute-start(bf16[768,128]{1,0:T(8,128)(2,1)S(1)} %shard_map.150.refs_3_.first), channel_id=1, source_target_pairs={{0,8},{4,12},{8,0},{12,4},{16,24},{20,28},{24,16},{28,20},{1,9},{5... | collective-permute-start | bytes 589832 | tf_op jit(solution)/shard_map/ppermute | solution.py:65
  24.2 1.5 %collective-permute-start.10 = (bf16[768,384]{1,0:T(8,128)(2,1)}, bf16[768,384]{1,0:T(8,128)(2,1)S(1)}, u32[]{:S(2)}, u32[]{:S(2)}) collective-permute-start(bf16[768,384]{1,0:T(8,128)(2,1)} %get-tuple-element.63), channel_id=1, source_target_pairs={{0,2},{1,3},{2,0},{3,1},{4,6},{5,7},{6,4},{7,5},{8,10},{9,11},{10,... | collective-permute-start | bytes 1769480 | tf_op jit(solution)/shard_map/ppermute | solution.py:65
  30.7 2.2 %shard_map.154 = (bf16[768,512]{1,0:T(8,128)(2,1)S(1)}, bf16[768,512]{1,0:T(8,128)(2,1)S(1)}, bf16[768,512]{1,0:T(8,128)(2,1)}, bf16[768,256]{1,0:T(8,128)(2,1)}) custom-call(s32[1]{0:T(128)} %bitcast.refs_0_, s32[1]{0:T(128)} %bitcast.1.base.refs_1_, bf16[2,768,384]{2,1,0:T(8,128)(2,1)S(1)} %get-tuple-element.42.refs_2_, ...), custom_call_target="tpu_custom_call" | custom-call | flops 10000000000 | tf_op jit(solution)/shard_map/pallas_call | solution.py:38
  34.6 3.0 %collective-permute-done.16.refs_2_ = bf16[384,128]{1,0:T(8,128)(2,1)S(1)} collective-permute-done((bf16[384,128]{1,0:T(8,128)(2,1)S(1)}, bf16[384,128]{1,0:T(8,128)(2,1)S(1)}, u32[]{:S(2)}, u32[]{:S(2)}) %collective-permute-start.16) | collective-permute-done | bytes 98336 | tf_op jit(solution)/shard_map/ppermute | solution.py:71
  41.2 2.8 %collective-permute-done.17.other = bf16[400,128]{1,0:T(8,128)(2,1)S(1)} collective-permute-done((bf16[400,128]{1,0:T(8,128)(2,1)S(1)}, bf16[400,128]{1,0:T(8,128)(2,1)S(1)}, u32[]{:S(2)}, u32[]{:S(2)}) %collective-permute-start.17) | collective-permute-done | bytes 102432 | tf_op jit(solution)/shard_map/ppermute | solution.py:65
  44.8 2.5 %collective-permute-start.18 = (bf16[400,128]{1,0:T(8,128)(2,1)S(1)}, bf16[400,128]{1,0:T(8,128)(2,1)S(1)}, u32[]{:S(2)}, u32[]{:S(2)}) collective-permute-start(bf16[400,128]{1,0:T(8,128)(2,1)S(1)} %shard_map.159.own), channel_id=1, source_target_pairs={{0,8},{4,12},{8,0},{12,4},{16,24},{20,28},{24,16},{28,20},{1,9},{5... | collective-permute-start | bytes 307208 | tf_op jit(solution)/shard_map/ppermute | solution.py:65
  50.0 2.9 %collective-permute-start.19 = (bf16[400,128]{1,0:T(8,128)(2,1)S(1)}, bf16[400,128]{1,0:T(8,128)(2,1)S(1)}, u32[]{:S(2)}, u32[]{:S(2)}) collective-permute-start(bf16[400,128]{1,0:T(8,128)(2,1)S(1)} %shard_map.160.own), channel_id=1, source_target_pairs={{0,16},{4,20},{8,24},{12,28},{16,0},{20,4},{24,8},{28,12},{1,17},{... | collective-permute-start | bytes 307208 | tf_op jit(solution)/shard_map/ppermute | solution.py:65
  52.9 6.8 %collective-permute-start.5 = (bf16[768,512]{1,0:T(8,128)(2,1)}, bf16[768,512]{1,0:T(8,128)(2,1)}, u32[]{:S(2)}, u32[]{:S(2)}) collective-permute-start(bf16[768,512]{1,0:T(8,128)(2,1)} %get-tuple-element.56), channel_id=1, source_target_pairs={{0,4},{4,8},{8,12},{12,16},{16,20},{20,24},{24,28},{1,5},{5,9},{9,... | collective-permute-start | bytes 2359304 | tf_op jit(solution)/shard_map/ppermute | solution.py:71
  61.1 2.8 %shard_map.162 = (bf16[2048,768]{1,0:T(8,128)(2,1)S(1)}, f32[768,128]{1,0:T(8,128)S(1)}) custom-call(s32[1]{0:T(128)} %bitcast.12.start, bf16[4008,768]{1,0:T(8,128)(2,1)} %bitcast.48, bf16[768,384]{1,0:T(8,128)(2,1)} %copy-done.3, bf16[4008,768]{1,0:T(8,128)(2,1)} %bitcast.49, bf16[768,128]{1,0:T(8,128)(2,1)S(1)} %shard_map.157.refs_1_.tokens, ...), custom_call_target="tpu_custom_call" | custom-call | tf_op jit(solution)/shard_map/pallas_call | solution.py:499
  68.9 2.7 %shard_map.166.kept = bf16[2048,128]{1,0:T(8,128)(2,1)S(1)} custom-call(s32[1]{0:T(128)} %bitcast.10.start, bf16[4008,768]{1,0:T(8,128)(2,1)} %bitcast.50, bf16[768,128]{1,0:T(8,128)(2,1)S(1)} %get-tuple-element.70.scaled, bf16[2048,128]{1,0:T(8,128)(2,1)S(1)} %shard_map.165.refs_0_), custom_call_target="tpu_custom_call" | custom-call | tf_op jit(solution)/shard_map/pallas_call | solution.py:541
  73.3 2.7 %collective-permute-done.5.refs_1_ = bf16[768,512]{1,0:T(8,128)(2,1)} collective-permute-done((bf16[768,512]{1,0:T(8,128)(2,1)}, bf16[768,512]{1,0:T(8,128)(2,1)}, u32[]{:S(2)}, u32[]{:S(2)}) %collective-permute-start.5) | collective-permute-done | bytes 786464 | tf_op jit(solution)/shard_map/ppermute | solution.py:71
  76.0 3.8 %shard_map.155.refs_0_ = bf16[512,384]{1,0:T(8,128)(2,1)S(1)} custom-call(s32[1]{0:T(128)} %bitcast.6.place, s32[1,512]{1,0:T(1,128)S(1)} %get-tuple-element.57.low, bf16[384,512]{1,0:T(8,128)(2,1)S(1)} %copy-done.12, bf16[768,512]{1,0:T(8,128)(2,1)S(1)} %copy-done.14, bf16[768,512]{1,0:T(8,128)(2,1)} %collective-permute-done.5.refs_1_, ...), custom_call_target="tpu_custom_call" | custom-call | flops 30000001024 | tf_op jit(solution)/shard_map/pallas_call | solution.py:38
  81.5 2.7 %collective-permute-start.25 = (f32[1,128]{1,0:T(1,128)S(1)}, f32[1,128]{1,0:T(1,128)S(1)}, u32[]{:S(2)}, u32[]{:S(2)}) collective-permute-start(f32[1,128]{1,0:T(1,128)S(1)} %shard_map.168), channel_id=1, source_target_pairs={{0,4},{4,0},{8,12},{12,8},{16,20},{20,16},{24,28},{28,24},{1,5},{5... | collective-permute-start | bytes 1544 | tf_op jit(solution)/shard_map/ppermute | solution.py:65
  84.2 1.5 %collective-permute-done.25 = f32[1,128]{1,0:T(1,128)S(1)} collective-permute-done((f32[1,128]{1,0:T(1,128)S(1)}, f32[1,128]{1,0:T(1,128)S(1)}, u32[]{:S(2)}, u32[]{:S(2)}) %collective-permute-start.25) | collective-permute-done | bytes 544 | tf_op jit(solution)/shard_map/ppermute | solution.py:65
  85.7 1.8 %collective-permute-start.26 = (f32[1,128]{1,0:T(1,128)S(1)}, f32[1,128]{1,0:T(1,128)S(1)}, u32[]{:S(2)}, u32[]{:S(2)}) collective-permute-start(f32[1,128]{1,0:T(1,128)S(1)} %max.13), channel_id=1, source_target_pairs={{0,8},{4,12},{8,0},{12,4},{16,24},{20,28},{24,16},{28,20},{1,9},{5... | collective-permute-start | bytes 1544 | tf_op jit(solution)/shard_map/ppermute | solution.py:65
  89.3 3.8 %collective-permute-start.27 = (f32[1,128]{1,0:T(1,128)S(1)}, f32[1,128]{1,0:T(1,128)S(1)}, u32[]{:S(2)}, u32[]{:S(2)}) collective-permute-start(f32[1,128]{1,0:T(1,128)S(1)} %max.14), channel_id=1, source_target_pairs={{0,16},{4,20},{8,24},{12,28},{16,0},{20,4},{24,8},{28,12},{1,17},{... | collective-permute-start | bytes 1544 | tf_op jit(solution)/shard_map/ppermute | solution.py:65
  94.6 1.5 %collective-permute-start.28 = (f32[2,128]{1,0:T(2,128)S(1)}, f32[2,128]{1,0:T(2,128)S(1)}, u32[]{:S(2)}, u32[]{:S(2)}) collective-permute-start(f32[2,128]{1,0:T(2,128)S(1)} %shard_map.169), channel_id=1, source_target_pairs={{0,2},{1,3},{2,0},{3,1},{4,6},{5,7},{6,4},{7,5},{8,10},{9,11},{10,... | collective-permute-start | bytes 3080 | tf_op jit(solution)/shard_map/ppermute | solution.py:65
  96.8 1.4 %collective-permute-done.28 = f32[2,128]{1,0:T(2,128)S(1)} collective-permute-done((f32[2,128]{1,0:T(2,128)S(1)}, f32[2,128]{1,0:T(2,128)S(1)}, u32[]{:S(2)}, u32[]{:S(2)}) %collective-permute-start.28) | collective-permute-done | bytes 1056 | tf_op jit(solution)/shard_map/ppermute | solution.py:65
  (105 shorter events, 33.0 us)
Async XLA Ops:
  0.6 8.9 %collective-permute-start.1 = (bf16[512,768]{1,0:T(8,128)(2,1)}, bf16[512,768]{1,0:T(8,128)(2,1)S(1)}, u32[]{:S(2)}, u32[]{:S(2)}) collective-permute-start(bf16[512,768]{1,0:T(8,128)(2,1)} %tokens.1), channel_id=1, source_target_pairs={{0,1},{1,0},{2,3},{3,2},{4,5},{5,4},{6,7},{7,6},{8,9},{9,8},{10,11... | collective-permute-start | bytes 2359304 | tf_op jit(solution)/shard_map/ppermute | solution.py:65
  1.2 20.9 %collective-permute-start.2 = (bf16[512,768]{1,0:T(8,128)(2,1)}, bf16[512,768]{1,0:T(8,128)(2,1)S(1)}, u32[]{:S(2)}, u32[]{:S(2)}) collective-permute-start(bf16[512,768]{1,0:T(8,128)(2,1)} %tokens.1), channel_id=1, source_target_pairs={{0,2},{1,3},{2,0},{3,1},{4,6},{5,7},{6,4},{7,5},{8,10},{9,11},{10,... | collective-permute-start | bytes 2359304 | tf_op jit(solution)/shard_map/ppermute | solution.py:65
  5.3 13.6 %collective-permute-start.3 = (bf16[768,128]{1,0:T(8,128)(2,1)S(1)}, bf16[768,128]{1,0:T(8,128)(2,1)S(1)}, u32[]{:S(2)}, u32[]{:S(2)}) collective-permute-start(bf16[768,128]{1,0:T(8,128)(2,1)S(1)} %shard_map.149.first), channel_id=1, source_target_pairs={{0,16},{4,20},{8,24},{12,28},{16,0},{20,4},{24,8},{28,12},{1,17},{... | collective-permute-start | bytes 589832 | tf_op jit(solution)/shard_map/ppermute | solution.py:65
  22.2 4.9 %collective-permute-start.4 = (bf16[512,768]{1,0:T(8,128)(2,1)S(1)}, bf16[512,768]{1,0:T(8,128)(2,1)S(1)}, u32[]{:S(2)}, u32[]{:S(2)}) collective-permute-start(bf16[512,768]{1,0:T(8,128)(2,1)S(1)} %get-tuple-element.45), channel_id=1, source_target_pairs={{0,1},{1,0},{2,3},{3,2},{4,5},{5,4},{6,7},{7,6},{8,9},{9,8},{10,11... | collective-permute-start | bytes 2359304 | tf_op jit(solution)/shard_map/ppermute | solution.py:65
  22.3 11.3 %collective-permute-start.13 = (bf16[768,128]{1,0:T(8,128)(2,1)S(1)}, bf16[768,128]{1,0:T(8,128)(2,1)S(1)}, u32[]{:S(2)}, u32[]{:S(2)}) collective-permute-start(bf16[768,128]{1,0:T(8,128)(2,1)S(1)} %shard_map.150.refs_3_.first), channel_id=1, source_target_pairs={{0,8},{4,12},{8,0},{12,4},{16,24},{20,28},{24,16},{28,20},{1,9},{5... | collective-permute-start | bytes 589832 | tf_op jit(solution)/shard_map/ppermute | solution.py:65
  24.2 17.0 %collective-permute-start.10 = (bf16[768,384]{1,0:T(8,128)(2,1)}, bf16[768,384]{1,0:T(8,128)(2,1)S(1)}, u32[]{:S(2)}, u32[]{:S(2)}) collective-permute-start(bf16[768,384]{1,0:T(8,128)(2,1)} %get-tuple-element.63), channel_id=1, source_target_pairs={{0,2},{1,3},{2,0},{3,1},{4,6},{5,7},{6,4},{7,5},{8,10},{9,11},{10,... | collective-permute-start | bytes 1769480 | tf_op jit(solution)/shard_map/ppermute | solution.py:65
  28.1 6.5 %collective-permute-start.15 = (bf16[384,128]{1,0:T(8,128)(2,1)S(1)}, bf16[384,128]{1,0:T(8,128)(2,1)S(1)}, u32[]{:S(2)}, u32[]{:S(2)}) collective-permute-start(bf16[384,128]{1,0:T(8,128)(2,1)S(1)} %get-tuple-element.55.refs_10_.refs_0_), channel_id=1, source_target_pairs={{4,0},{8,4},{12,8},{16,12},{20,16},{24,20},{28,24},{5,1},{9,5},{13... | collective-permute-start | bytes 294920 | tf_op jit(solution)/shard_map/ppermute | solution.py:71
  29.4 8.2 %collective-permute-start.16 = (bf16[384,128]{1,0:T(8,128)(2,1)S(1)}, bf16[384,128]{1,0:T(8,128)(2,1)S(1)}, u32[]{:S(2)}, u32[]{:S(2)}) collective-permute-start(bf16[384,128]{1,0:T(8,128)(2,1)S(1)} %get-tuple-element.55.refs_10_.refs_0_), channel_id=1, source_target_pairs={{8,0},{12,4},{16,8},{20,12},{24,16},{28,20},{9,1},{13,5},{17,9},{2... | collective-permute-start | bytes 294920 | tf_op jit(solution)/shard_map/ppermute | solution.py:71
  32.9 11.1 %collective-permute-start.6 = (bf16[768,256]{1,0:T(8,128)(2,1)}, bf16[768,256]{1,0:T(8,128)(2,1)S(1)}, u32[]{:S(2)}, u32[]{:S(2)}) collective-permute-start(bf16[768,256]{1,0:T(8,128)(2,1)} %get-tuple-element.60), channel_id=1, source_target_pairs={{20,28},{21,29},{22,30},{23,31}} | collective-permute-start | bytes 1179656 | tf_op jit(solution)/shard_map/ppermute | solution.py:713
  38.8 5.1 %collective-permute-start.17 = (bf16[400,128]{1,0:T(8,128)(2,1)S(1)}, bf16[400,128]{1,0:T(8,128)(2,1)S(1)}, u32[]{:S(2)}, u32[]{:S(2)}) collective-permute-start(bf16[400,128]{1,0:T(8,128)(2,1)S(1)} %shard_map.158.own), channel_id=1, source_target_pairs={{0,4},{4,0},{8,12},{12,8},{16,20},{20,16},{24,28},{28,24},{1,5},{5... | collective-permute-start | bytes 307208 | tf_op jit(solution)/shard_map/ppermute | solution.py:65
  40.0 19.7 %collective-permute-start.12 = (bf16[768,384]{1,0:T(8,128)(2,1)}, bf16[768,384]{1,0:T(8,128)(2,1)S(1)}, u32[]{:S(2)}, u32[]{:S(2)}) collective-permute-start(bf16[768,384]{1,0:T(8,128)(2,1)} %get-tuple-element.64), channel_id=1, source_target_pairs={{0,3},{1,2},{2,1},{3,0},{4,7},{5,6},{6,5},{7,4},{8,11},{9,10},{10,... | collective-permute-start | bytes 1769480 | tf_op jit(solution)/shard_map/ppermute | solution.py:65
  40.0 9.7 %collective-permute-start.14 = (bf16[768,128]{1,0:T(8,128)(2,1)S(1)}, bf16[768,128]{1,0:T(8,128)(2,1)S(1)}, u32[]{:S(2)}, u32[]{:S(2)}) collective-permute-start(bf16[768,128]{1,0:T(8,128)(2,1)S(1)} %shard_map.156.first.refs_3_), channel_id=1, source_target_pairs={{0,4},{4,0},{8,12},{12,8},{16,20},{20,16},{24,28},{28,24},{1,5},{5... | collective-permute-start | bytes 589832 | tf_op jit(solution)/shard_map/ppermute | solution.py:65
  44.8 5.1 %collective-permute-start.18 = (bf16[400,128]{1,0:T(8,128)(2,1)S(1)}, bf16[400,128]{1,0:T(8,128)(2,1)S(1)}, u32[]{:S(2)}, u32[]{:S(2)}) collective-permute-start(bf16[400,128]{1,0:T(8,128)(2,1)S(1)} %shard_map.159.own), channel_id=1, source_target_pairs={{0,8},{4,12},{8,0},{12,4},{16,24},{20,28},{24,16},{28,20},{1,9},{5... | collective-permute-start | bytes 307208 | tf_op jit(solution)/shard_map/ppermute | solution.py:65
  48.6 11.8 %collective-permute-start.8 = (bf16[768,384]{1,0:T(8,128)(2,1)}, bf16[768,384]{1,0:T(8,128)(2,1)S(1)}, u32[]{:S(2)}, u32[]{:S(2)}) collective-permute-start(bf16[768,384]{1,0:T(8,128)(2,1)} %copy-done.8), channel_id=1, source_target_pairs={{0,1},{1,0},{2,3},{3,2},{4,5},{5,4},{6,7},{7,6},{8,9},{9,8},{10,11... | collective-permute-start | bytes 1769480 | tf_op jit(solution)/shard_map/ppermute | solution.py:65
  50.0 9.7 %collective-permute-start.19 = (bf16[400,128]{1,0:T(8,128)(2,1)S(1)}, bf16[400,128]{1,0:T(8,128)(2,1)S(1)}, u32[]{:S(2)}, u32[]{:S(2)}) collective-permute-start(bf16[400,128]{1,0:T(8,128)(2,1)S(1)} %shard_map.160.own), channel_id=1, source_target_pairs={{0,16},{4,20},{8,24},{12,28},{16,0},{20,4},{24,8},{28,12},{1,17},{... | collective-permute-start | bytes 307208 | tf_op jit(solution)/shard_map/ppermute | solution.py:65
  52.9 23.1 %collective-permute-start.5 = (bf16[768,512]{1,0:T(8,128)(2,1)}, bf16[768,512]{1,0:T(8,128)(2,1)}, u32[]{:S(2)}, u32[]{:S(2)}) collective-permute-start(bf16[768,512]{1,0:T(8,128)(2,1)} %get-tuple-element.56), channel_id=1, source_target_pairs={{0,4},{4,8},{8,12},{12,16},{16,20},{20,24},{24,28},{1,5},{5,9},{9,... | collective-permute-start | bytes 2359304 | tf_op jit(solution)/shard_map/ppermute | solution.py:71
  59.8 5.2 %collective-permute-start.21 = (bf16[384,128]{1,0:T(8,128)(2,1)S(1)}, bf16[384,128]{1,0:T(8,128)(2,1)S(1)}, u32[]{:S(2)}, u32[]{:S(2)}) collective-permute-start(bf16[384,128]{1,0:T(8,128)(2,1)S(1)} %shard_map.161.own), channel_id=1, source_target_pairs={{0,2},{1,3},{2,0},{3,1},{4,6},{5,7},{6,4},{7,5},{8,10},{9,11},{10,... | collective-permute-start | bytes 294920 | tf_op jit(solution)/shard_map/ppermute | solution.py:65
  72.8 8.6 %collective-permute-start.24 = (bf16[1024,128]{1,0:T(8,128)(2,1)S(1)}, bf16[1024,128]{1,0:T(8,128)(2,1)S(1)}, u32[]{:S(2)}, u32[]{:S(2)}) collective-permute-start(bf16[1024,128]{1,0:T(8,128)(2,1)S(1)} %get-tuple-element.74), channel_id=1, source_target_pairs={{0,2},{1,3},{2,0},{3,1},{4,6},{5,7},{6,4},{7,5},{8,10},{9,11},{10,... | collective-permute-start | bytes 786440 | tf_op jit(solution)/shard_map/ppermute | solution.py:65
  79.9 13.2 %collective-permute-start.9 = (bf16[512,384]{1,0:T(8,128)(2,1)S(1)}, bf16[512,384]{1,0:T(8,128)(2,1)S(1)}, u32[]{:S(2)}, u32[]{:S(2)}) collective-permute-start(bf16[512,384]{1,0:T(8,128)(2,1)S(1)} %shard_map.155.refs_0_), channel_id=1, source_target_pairs={{0,2},{1,3},{2,0},{3,1},{4,6},{5,7},{6,4},{7,5},{8,10},{9,11},{10,... | collective-permute-start | bytes 1179656 | tf_op jit(solution)/shard_map/ppermute | solution.py:65
  81.5 4.2 %collective-permute-start.25 = (f32[1,128]{1,0:T(1,128)S(1)}, f32[1,128]{1,0:T(1,128)S(1)}, u32[]{:S(2)}, u32[]{:S(2)}) collective-permute-start(f32[1,128]{1,0:T(1,128)S(1)} %shard_map.168), channel_id=1, source_target_pairs={{0,4},{4,0},{8,12},{12,8},{16,20},{20,16},{24,28},{28,24},{1,5},{5... | collective-permute-start | bytes 1544 | tf_op jit(solution)/shard_map/ppermute | solution.py:65
  84.2 12.0 %collective-permute-start.7 = (bf16[512,384]{1,0:T(8,128)(2,1)S(1)}, bf16[512,384]{1,0:T(8,128)(2,1)S(1)}, u32[]{:S(2)}, u32[]{:S(2)}) collective-permute-start(bf16[512,384]{1,0:T(8,128)(2,1)S(1)} %shard_map.155.refs_0_), channel_id=1, source_target_pairs={{0,1},{1,0},{2,3},{3,2},{4,5},{5,4},{6,7},{7,6},{8,9},{9,8},{10,11... | collective-permute-start | bytes 1179656 | tf_op jit(solution)/shard_map/ppermute | solution.py:65
  89.3 5.3 %collective-permute-start.27 = (f32[1,128]{1,0:T(1,128)S(1)}, f32[1,128]{1,0:T(1,128)S(1)}, u32[]{:S(2)}, u32[]{:S(2)}) collective-permute-start(f32[1,128]{1,0:T(1,128)S(1)} %max.14), channel_id=1, source_target_pairs={{0,16},{4,20},{8,24},{12,28},{16,0},{20,4},{24,8},{28,12},{1,17},{... | collective-permute-start | bytes 1544 | tf_op jit(solution)/shard_map/ppermute | solution.py:65
  93.7 4.6 %collective-permute-start.11 = (bf16[512,384]{1,0:T(8,128)(2,1)S(1)}, bf16[512,384]{1,0:T(8,128)(2,1)S(1)}, u32[]{:S(2)}, u32[]{:S(2)}) collective-permute-start(bf16[512,384]{1,0:T(8,128)(2,1)S(1)} %collective-permute-done.9.refs_0_), channel_id=1, source_target_pairs={{0,1},{1,0},{2,3},{3,2},{4,5},{5,4},{6,7},{7,6},{8,9},{9,8},{10,11... | collective-permute-start | bytes 1179656 | tf_op jit(solution)/shard_map/ppermute | solution.py:65
  94.6 3.6 %collective-permute-start.28 = (f32[2,128]{1,0:T(2,128)S(1)}, f32[2,128]{1,0:T(2,128)S(1)}, u32[]{:S(2)}, u32[]{:S(2)}) collective-permute-start(f32[2,128]{1,0:T(2,128)S(1)} %shard_map.169), channel_id=1, source_target_pairs={{0,2},{1,3},{2,0},{3,1},{4,6},{5,7},{6,4},{7,5},{8,10},{9,11},{10,... | collective-permute-start | bytes 3080 | tf_op jit(solution)/shard_map/ppermute | solution.py:65
  (20 other events, 104.1 us)
